TPU v7x, 32 devices: a whole 2x2x4 slice. The times are simulated.
32 devices in a mesh: dp: 4 (over z), expert: 8 (over y, x, core).
Axes of the slice: x: 2, y: 2, z: 4, core: 2. Of those that a mesh axis runs over, the one named last changes fastest.
Arguments:
- tokens: bfloat16 [6144, 2048], P(('dp', 'expert')), may hold values from -6 to 6
- cotangent: bfloat16 [6144, 2048], P(('dp', 'expert')), may hold values from -6 to 6
- lengths: int32 [32, 4], P(('dp', 'expert')), may hold values from 1 to 144, 192 in all within a row
- routes: int32 [6144, 8], P(('dp', 'expert')), may hold values from 0 to 15, all different within a row; in each aligned block of 192 rows (0 to 191, 192 to 383, ...) at most 120 rows name the same one
- w_query: bfloat16 [2048, 2048], P(('dp', 'expert')), may hold values from -0.125 to 0.125
- w_key: bfloat16 [2048, 2048], P(('dp', 'expert')), may hold values from -0.125 to 0.125
- w_value: bfloat16 [2048, 2048], P(('dp', 'expert')), may hold values from -0.125 to 0.125
- w_out: bfloat16 [2048, 2048], P(('dp', 'expert')), may hold values from -0.75 to 0.75
- w_router: bfloat16 [2048, 16], P(('dp', 'expert')), may hold values from -0.06591797 to 0.06591797
- w_gate: bfloat16 [16, 2048, 1024], P('expert', 'dp'), may hold values from -0.125 to 0.125
- w_up: bfloat16 [16, 2048, 1024], P('expert', 'dp'), may hold values from -0.125 to 0.125
- w_down: bfloat16 [16, 1024, 2048], P('expert', 'dp'), may hold values from -0.75 to 0.75
- g_attn: bfloat16 [2048], P(('dp', 'expert')), may hold values from 0.099609375 to 1.8984375
- g_query: bfloat16 [2048], P(('dp', 'expert')), may hold values from 0.099609375 to 1.8984375
- g_key: bfloat16 [2048], P(('dp', 'expert')), may hold values from 0.099609375 to 1.8984375
- g_ffn: bfloat16 [2048], P(('dp', 'expert')), may hold values from 0.099609375 to 1.8984375
Outputs:
- block_out: bfloat16 [6144, 2048], P(('dp', 'expert'))
- grad_tokens: bfloat16 [6144, 2048], P(('dp', 'expert'))
- grad_query: float32 [2048, 2048], P(('dp', 'expert'))
- grad_key: float32 [2048, 2048], P(('dp', 'expert'))
- grad_value: float32 [2048, 2048], P(('dp', 'expert'))
- grad_outproj: float32 [2048, 2048], P(('dp', 'expert'))
- grad_router: float32 [2048, 16], P(('dp', 'expert'))
- grad_gate: float32 [16, 2048, 1024], P('expert', 'dp')
- grad_up: float32 [16, 2048, 1024], P('expert', 'dp')
- grad_down: float32 [16, 1024, 2048], P('expert', 'dp')
- grad_gattn: float32 [2048], P(('dp', 'expert'))
- grad_gquery: float32 [2048], P(('dp', 'expert'))
- grad_gkey: float32 [2048], P(('dp', 'expert'))
- grad_gffn: float32 [2048], P(('dp', 'expert'))
Inputs may be any that keep to these rules, and one draw needn't show every extreme that they name: Each device's row of lengths sums to 192, and its largest entry is 144. `routes`: A token's 8 experts differ. Among the rows of one device, no expert is named more than 120 times, a bound that some block reaches.
All inputs are finite; a program needn't handle non-finite values.
Results may differ from a plain program's by a relative error of at most 0.018.
Values may be sent and summed in bfloat16 or wider, within the bound.
No kernel may reach another device: no remote copies, remote signals or barrier semaphores. Data moves between devices by JAX's collectives and lax.ppermute only.
A program may use at most 448 MiB of HBM per device.

v0:
```python
import jax
import jax.numpy as jnp
from jax import lax
from jax.sharding import PartitionSpec as P

D = 2048
HEADS = 16
HD = 128


EPS = 1e-05
THETA = 50000.0


def normalize(v, gain):
    return v * lax.rsqrt(jnp.mean(v * v, axis=-1, keepdims=True) + EPS) * gain


def layout(lengths_row, row_count):
    seq_ends = jnp.cumsum(lengths_row)
    position = jnp.arange(row_count, dtype=jnp.int32)
    segment = jnp.sum((position[:, None] >= seq_ends[None, :]).astype(jnp.int32), axis=1)
    seq_starts = seq_ends - lengths_row
    labels = jnp.arange(lengths_row.shape[0], dtype=jnp.int32)
    seq_start = jnp.sum(
        jnp.where(segment[:, None] == labels[None, :], seq_starts[None, :], 0), axis=1
    )
    return (segment, position - seq_start)


def rotate(v, offset):
    half_dim = v.shape[-1] // 2
    frequency = THETA ** (-jnp.arange(half_dim).astype(v.dtype) / half_dim)
    angles = offset.astype(v.dtype)[:, None] * frequency[None, :]
    cosine = jnp.cos(angles)[:, None, :]
    sine_part = jnp.sin(angles)[:, None, :]
    first_half = v[..., :half_dim]
    second_half = v[..., half_dim:]
    return jnp.concatenate(
        [
            first_half * cosine - second_half * sine_part,
            second_half * cosine + first_half * sine_part,
        ],
        axis=-1,
    )


def head_prep(raw_q, raw_k, gain_q, gain_k, offset):
    row_count = raw_q.shape[0]
    queries = rotate(
        normalize(raw_q.reshape(row_count, HEADS, HD), gain_q.reshape(HEADS, HD)), offset
    )
    keys_rot = rotate(
        normalize(raw_k.reshape(row_count, HEADS, HD), gain_k.reshape(HEADS, HD)), offset
    )
    return (queries, keys_rot)


def route_softmax(chosen):
    peak = jnp.max(chosen, axis=-1, keepdims=True)
    exp_scores = jnp.exp(chosen - peak)
    return exp_scores / jnp.sum(exp_scores, axis=-1, keepdims=True)


def swiglu(gate_act, up_act):
    return jax.nn.silu(gate_act) * up_act


def slots(flat_routes, expert_count, capacity):
    one_hot = (flat_routes[:, None] == jnp.arange(expert_count, dtype=jnp.int32)[None, :]).astype(
        jnp.int32
    )
    slot_rank = jnp.sum((jnp.cumsum(one_hot, axis=0) - one_hot) * one_hot, axis=1)
    return flat_routes * capacity + slot_rank


def contract_rows(left, right):
    return lax.dot_general(
        left, right, (((0,), (0,)), ((), ())), preferred_element_type=jnp.float32
    )


def times_transposed(left, right):
    return lax.dot_general(
        left, right, (((1,), (1,)), ((), ())), preferred_element_type=jnp.float32
    )


def local(
    tokens,
    cotangent,
    lengths,
    routes,
    w_query,
    w_key,
    w_value,
    w_out,
    w_router,
    w_gate,
    w_up,
    w_down,
    g_attn,
    g_query,
    g_key,
    g_ffn,
):
    row_count = tokens.shape[0]
    top_count = routes.shape[1]
    local_experts = w_gate.shape[0]
    owners = lax.axis_size("expert")
    experts = local_experts * owners
    capacity = row_count * top_count * 5 // (4 * experts)
    score_scale = HD ** (-0.5)
    segment, offset = layout(lengths[0], row_count)
    seq_mask = (segment[:, None] == segment[None, :])[None]
    dense = (
        lax.all_gather(w_query, ("dp", "expert"), axis=0, tiled=True),
        lax.all_gather(w_key, ("dp", "expert"), axis=0, tiled=True),
        lax.all_gather(w_value, ("dp", "expert"), axis=0, tiled=True),
        lax.all_gather(w_out, ("dp", "expert"), axis=0, tiled=True),
        lax.all_gather(w_router, ("dp", "expert"), axis=0, tiled=True),
        lax.all_gather(g_attn, ("dp", "expert"), axis=0, tiled=True),
        lax.all_gather(g_query, ("dp", "expert"), axis=0, tiled=True),
        lax.all_gather(g_key, ("dp", "expert"), axis=0, tiled=True),
        lax.all_gather(g_ffn, ("dp", "expert"), axis=0, tiled=True),
    )
    query_w, key_w, value_w, out_w, router_w, attn_gain, query_gain, key_gain, ffn_gain = dense
    expert_full = (
        lax.all_gather(w_gate, "dp", axis=1, tiled=True),
        lax.all_gather(w_up, "dp", axis=1, tiled=True),
        lax.all_gather(w_down, "dp", axis=1, tiled=True),
    )
    gate_full, up_full, down_full = expert_full
    inputs = tokens.astype(jnp.float32)
    normed_f, norm_attn_pull = jax.vjp(normalize, inputs, attn_gain.astype(jnp.float32))
    normed_attn = normed_f.astype(jnp.bfloat16)
    raw_q = jnp.dot(normed_attn, query_w, preferred_element_type=jnp.float32)
    raw_k = jnp.dot(normed_attn, key_w, preferred_element_type=jnp.float32)
    values = jnp.dot(normed_attn, value_w, preferred_element_type=jnp.float32).astype(jnp.bfloat16)
    value_heads = values.reshape(row_count, HEADS, HD)

    def prep_local(first, second, first_gain, second_gain):
        return head_prep(first, second, first_gain, second_gain, offset)

    rotated, heads_pull = jax.vjp(
        prep_local, raw_q, raw_k, query_gain.astype(jnp.float32), key_gain.astype(jnp.float32)
    )
    queries = rotated[0].astype(jnp.bfloat16)
    keys_rot = rotated[1].astype(jnp.bfloat16)
    scores = (
        jnp.einsum("qhd,khd->hqk", queries, keys_rot, preferred_element_type=jnp.float32)
        * score_scale
    )
    scores = jnp.where(seq_mask, scores, -1e30)
    peak = jnp.max(scores, axis=-1, keepdims=True)
    exp_scores = jnp.exp(scores - peak)
    exp_total = jnp.sum(exp_scores, axis=-1, keepdims=True)
    log_total = peak + jnp.log(exp_total)
    probs_low = (exp_scores / exp_total).astype(jnp.bfloat16)
    context = (
        jnp.einsum("hqk,khd->qhd", probs_low, value_heads, preferred_element_type=jnp.float32)
        .astype(jnp.bfloat16)
        .reshape(row_count, D)
    )
    midway = inputs + jnp.dot(context, out_w, preferred_element_type=jnp.float32)
    normed2_f, norm_ffn_pull = jax.vjp(normalize, midway, ffn_gain.astype(jnp.float32))
    normed_ffn = normed2_f.astype(jnp.bfloat16)
    logits = jnp.dot(normed_ffn, router_w, preferred_element_type=jnp.float32)
    chosen = jnp.take_along_axis(logits, routes, axis=1)
    gates, gates_pull = jax.vjp(route_softmax, chosen)
    slot_index = slots(routes.reshape(-1), experts, capacity)
    sent_rows = (
        jnp.zeros((experts * capacity, D), jnp.bfloat16)
        .at[slot_index]
        .set(jnp.repeat(normed_ffn, top_count, axis=0))
    )
    sent_rows = sent_rows.reshape(owners, local_experts, capacity, D)
    arrived = lax.all_to_all(sent_rows, "expert", split_axis=0, concat_axis=2, tiled=True).reshape(
        local_experts, owners * capacity, D
    )
    gate_act = jnp.einsum("erd,edf->erf", arrived, gate_full, preferred_element_type=jnp.float32)
    up_act = jnp.einsum("erd,edf->erf", arrived, up_full, preferred_element_type=jnp.float32)
    hidden = swiglu(gate_act, up_act).astype(jnp.bfloat16)
    produced = jnp.einsum(
        "erf,efd->erd", hidden, down_full, preferred_element_type=jnp.float32
    ).astype(jnp.bfloat16)
    returned = lax.all_to_all(
        produced.reshape(1, local_experts, owners * capacity, D),
        "expert",
        split_axis=2,
        concat_axis=0,
        tiled=True,
    ).reshape(experts * capacity, D)
    picked = returned[slot_index].reshape(row_count, top_count, D).astype(jnp.float32)
    block_out = (midway + jnp.sum(gates[:, :, None] * picked, axis=1)).astype(jnp.bfloat16)
    grad_out = cotangent.astype(jnp.float32)
    grad_gates = jnp.sum(grad_out[:, None, :] * picked, axis=2)
    grad_picked = (
        (gates[:, :, None] * grad_out[:, None, :])
        .astype(jnp.bfloat16)
        .reshape(row_count * top_count, D)
    )
    grad_sent = jnp.zeros((experts * capacity, D), jnp.bfloat16).at[slot_index].set(grad_picked)
    grad_sent = grad_sent.reshape(owners, local_experts, capacity, D)
    grad_arrived = lax.all_to_all(
        grad_sent, "expert", split_axis=0, concat_axis=2, tiled=True
    ).reshape(local_experts, owners * capacity, D)
    gate_back, up_back, down_back = (
        lax.all_gather(w_gate, "dp", axis=1, tiled=True),
        lax.all_gather(w_up, "dp", axis=1, tiled=True),
        lax.all_gather(w_down, "dp", axis=1, tiled=True),
    )
    grad_hidden = jnp.einsum(
        "erd,efd->erf", grad_arrived, down_back, preferred_element_type=jnp.float32
    )
    grad_down_local = jnp.einsum(
        "erf,erd->efd", hidden, grad_arrived, preferred_element_type=jnp.float32
    )
    act_unused, act_pull = jax.vjp(swiglu, gate_act, up_act)
    grad_gate_act, grad_up_act = act_pull(grad_hidden)
    grad_gate_low = grad_gate_act.astype(jnp.bfloat16)
    grad_up_low = grad_up_act.astype(jnp.bfloat16)
    grad_gate_local = jnp.einsum(
        "erd,erf->edf", arrived, grad_gate_low, preferred_element_type=jnp.float32
    )
    grad_up_local = jnp.einsum(
        "erd,erf->edf", arrived, grad_up_low, preferred_element_type=jnp.float32
    )
    grad_arrival = jnp.einsum(
        "erf,edf->erd", grad_gate_low, gate_back, preferred_element_type=jnp.float32
    )
    grad_arrival = grad_arrival + jnp.einsum(
        "erf,edf->erd", grad_up_low, up_back, preferred_element_type=jnp.float32
    )
    grad_arrival = grad_arrival.astype(jnp.bfloat16).reshape(1, local_experts, owners * capacity, D)
    grad_back = lax.all_to_all(
        grad_arrival, "expert", split_axis=2, concat_axis=0, tiled=True
    ).reshape(experts * capacity, D)
    grad_normed_ffn = jnp.sum(
        grad_back[slot_index].reshape(row_count, top_count, D).astype(jnp.float32), axis=1
    )
    expert_grads = (
        lax.psum_scatter(grad_gate_local, "dp", scatter_dimension=1, tiled=True),
        lax.psum_scatter(grad_up_local, "dp", scatter_dimension=1, tiled=True),
        lax.psum_scatter(grad_down_local, "dp", scatter_dimension=1, tiled=True),
    )
    grad_chosen = gates_pull(grad_gates)[0]
    expert_ids = jnp.arange(experts, dtype=jnp.int32)
    grad_logits = jnp.sum(
        jnp.where(routes[:, :, None] == expert_ids[None, None, :], grad_chosen[:, :, None], 0.0),
        axis=1,
    ).astype(jnp.bfloat16)
    grad_router_local = contract_rows(normed_ffn, grad_logits)
    dense_back = (
        lax.all_gather(w_query, ("dp", "expert"), axis=0, tiled=True),
        lax.all_gather(w_key, ("dp", "expert"), axis=0, tiled=True),
        lax.all_gather(w_value, ("dp", "expert"), axis=0, tiled=True),
        lax.all_gather(w_out, ("dp", "expert"), axis=0, tiled=True),
        lax.all_gather(w_router, ("dp", "expert"), axis=0, tiled=True),
    )
    query_back, key_back, value_back, out_back, router_back = dense_back
    grad_normed_ffn = grad_normed_ffn + times_transposed(grad_logits, router_back)
    grad_midway_norm, grad_ffn_gain = norm_ffn_pull(grad_normed_ffn)
    grad_midway = grad_out + grad_midway_norm
    grad_attn = grad_midway.astype(jnp.bfloat16)
    grad_out_local = contract_rows(context, grad_attn)
    grad_context = (
        times_transposed(grad_attn, out_back).astype(jnp.bfloat16).reshape(row_count, HEADS, HD)
    )
    probs = jnp.where(seq_mask, jnp.exp(scores - log_total), 0.0)
    grad_probs = jnp.einsum(
        "qhd,khd->hqk", grad_context, value_heads, preferred_element_type=jnp.float32
    )
    grad_scores = (
        probs * (grad_probs - jnp.sum(grad_probs * probs, axis=-1, keepdims=True))
    ).astype(jnp.bfloat16)
    grad_values = (
        jnp.einsum("hqk,qhd->khd", probs_low, grad_context, preferred_element_type=jnp.float32)
        .astype(jnp.bfloat16)
        .reshape(row_count, D)
    )
    grad_queries = (
        jnp.einsum("hqk,khd->qhd", grad_scores, keys_rot, preferred_element_type=jnp.float32)
        * score_scale
    )
    grad_keys = (
        jnp.einsum("hqk,qhd->khd", grad_scores, queries, preferred_element_type=jnp.float32)
        * score_scale
    )
    grad_raw_q, grad_raw_k, grad_query_gain, grad_key_gain = heads_pull((grad_queries, grad_keys))
    grad_raw_q = grad_raw_q.astype(jnp.bfloat16)
    grad_raw_k = grad_raw_k.astype(jnp.bfloat16)
    grad_query_local = contract_rows(normed_attn, grad_raw_q)
    grad_key_local = contract_rows(normed_attn, grad_raw_k)
    grad_value_local = contract_rows(normed_attn, grad_values)
    grad_normed_attn = (
        times_transposed(grad_raw_q, query_back)
        + times_transposed(grad_raw_k, key_back)
        + times_transposed(grad_values, value_back)
    )
    grad_inputs_norm, grad_attn_gain = norm_attn_pull(grad_normed_attn)
    grad_tokens = (grad_midway + grad_inputs_norm).astype(jnp.bfloat16)
    dense_grads = (
        lax.psum_scatter(grad_query_local, ("dp", "expert"), scatter_dimension=0, tiled=True),
        lax.psum_scatter(grad_key_local, ("dp", "expert"), scatter_dimension=0, tiled=True),
        lax.psum_scatter(grad_value_local, ("dp", "expert"), scatter_dimension=0, tiled=True),
        lax.psum_scatter(grad_out_local, ("dp", "expert"), scatter_dimension=0, tiled=True),
        lax.psum_scatter(grad_router_local, ("dp", "expert"), scatter_dimension=0, tiled=True),
        lax.psum_scatter(grad_attn_gain, ("dp", "expert"), scatter_dimension=0, tiled=True),
        lax.psum_scatter(grad_query_gain, ("dp", "expert"), scatter_dimension=0, tiled=True),
        lax.psum_scatter(grad_key_gain, ("dp", "expert"), scatter_dimension=0, tiled=True),
        lax.psum_scatter(grad_ffn_gain, ("dp", "expert"), scatter_dimension=0, tiled=True),
    )
    return (
        block_out,
        grad_tokens,
        dense_grads[0],
        dense_grads[1],
        dense_grads[2],
        dense_grads[3],
        dense_grads[4],
        expert_grads[0],
        expert_grads[1],
        expert_grads[2],
        dense_grads[5],
        dense_grads[6],
        dense_grads[7],
        dense_grads[8],
    )


def solution(mesh):
    in_specs = (
        P(("dp", "expert"), None),
        P(("dp", "expert"), None),
        P(("dp", "expert"), None),
        P(("dp", "expert"), None),
        P(("dp", "expert"), None),
        P(("dp", "expert"), None),
        P(("dp", "expert"), None),
        P(("dp", "expert"), None),
        P(("dp", "expert"), None),
        P("expert", "dp", None),
        P("expert", "dp", None),
        P("expert", "dp", None),
        P(("dp", "expert")),
        P(("dp", "expert")),
        P(("dp", "expert")),
        P(("dp", "expert")),
    )
    out_specs = (
        P(("dp", "expert"), None),
        P(("dp", "expert"), None),
        P(("dp", "expert"), None),
        P(("dp", "expert"), None),
        P(("dp", "expert"), None),
        P(("dp", "expert"), None),
        P(("dp", "expert"), None),
        P("expert", "dp", None),
        P("expert", "dp", None),
        P("expert", "dp", None),
        P(("dp", "expert")),
        P(("dp", "expert")),
        P(("dp", "expert")),
        P(("dp", "expert")),
    )
    return jax.shard_map(local, mesh=mesh, in_specs=in_specs, out_specs=out_specs, check_vma=False)
```

profile of v0, /device:TPU:0, one launch (start us, length us, event | category | flops | bytes accessed | tf_op | source)
XLA Modules:
  0.0 2698.5 jit_solution(8863504874703259478)
XLA Ops:
  13.3 42.5 %all-reduce.13 = (bf16[2048]{0:T(1024)(128)(2,1)S(1)}, bf16[2048]{0:T(1024)(128)(2,1)S(1)}, bf16[2048]{0:T(1024)(128)(2,1)S(1)}, bf16[2048]{0:T(1024)(128)(2,1)S(1)}) all-reduce(bf16[2048]{0:T(1024)(128)(2,1)S(1)} %dynamic-update-slice, bf16[2048]{0:T(1024)(128)(2,1)S(1)} %dynamic-update-slice.2, ...), channel_id=1, replica_groups=mesh['dp'=4,'expert'=8] {'dp','expert'}, use_global_device_ids=true, to_apply=%add.4 | all-reduce | flops 8192 | bytes 32768
  61.6 41.7 %all-gather = bf16[32,64,16]{1,2,0:T(8,128)(2,1)S(1)} all-gather(bf16[1,64,16]{1,2,0:T(8,128)(2,1)S(1)} %bitcast.238), channel_id=1, replica_groups=mesh['dp'=4,'expert'=8] {'dp','expert'}, dimensions={0}, use_global_device_ids=true | all-gather | bytes 67584 | tf_op jit(solution)/shard_map/all_gather | solution.py:121
  113.2 57.7 %all-gather.11.cloned.1.call-done = bf16[2048,2048]{1,0:T(8,128)(2,1)} async-done(((bf16[64,2048]{1,0:T(8,128)(2,1)}), bf16[2048,2048]{1,0:T(8,128)(2,1)}) %all-gather.11.cloned.1.call-update) | async-done | bytes 8388624 | tf_op jit(solution)/shard_map/all_gather | solution.py:117
  185.0 64.9 %all-gather.9.cloned.1.call-done = bf16[2048,2048]{1,0:T(8,128)(2,1)} async-done(((bf16[64,2048]{1,0:T(8,128)(2,1)}), bf16[2048,2048]{1,0:T(8,128)(2,1)}) %all-gather.9.cloned.1.call-update) | async-done | bytes 8388624 | tf_op jit(solution)/shard_map/all_gather | solution.py:119
  257.2 71.5 %all-gather.15.cloned.1.call-done = bf16[2048,2048]{1,0:T(8,128)(2,1)} async-done(((bf16[64,2048]{1,0:T(8,128)(2,1)}), bf16[2048,2048]{1,0:T(8,128)(2,1)}) %all-gather.15.cloned.1.call-update) | async-done | bytes 8388624 | tf_op jit(solution)/shard_map/all_gather | solution.py:120
  349.7 14.5 scatter_custom_fusion.1
  369.8 13.9 scatter_custom_fusion
  383.7 73.8 %all-to-all-done.2 = bf16[8,2,120,2048]{3,2,1,0:T(8,128)(2,1)} async-done(((bf16[8,2,120,2048]{3,2,1,0:T(8,128)(2,1)}), bf16[8,2,120,2048]{3,2,1,0:T(8,128)(2,1)}, u32[]{:S(2)}, u32[]{:S(2)}) %all-to-all-start.2) | async-done | bytes 7864352 | tf_op jit(solution)/shard_map/all_to_all | solution.py:205
  470.5 80.5 %all-to-all-done = bf16[8,2,120,2048]{3,2,1,0:T(8,128)(2,1)} async-done(((bf16[8,2,120,2048]{3,2,1,0:T(8,128)(2,1)}), bf16[8,2,120,2048]{3,2,1,0:T(8,128)(2,1)}, u32[]{:S(2)}, u32[]{:S(2)}) %all-to-all-start) | async-done | bytes 7864352 | tf_op jit(solution)/shard_map/all_to_all | solution.py:178
  559.1 14.9 fusion.102
  574.0 53.7 %all-gather.17.cloned.1.call-done = bf16[2,2048,1024]{2,1,0:T(8,128)(2,1)} async-done(((bf16[2,512,1024]{2,1,0:T(8,128)(2,1)}), bf16[2,2048,1024]{2,1,0:T(8,128)(2,1)}) %all-gather.17.cloned.1.call-update) | async-done | bytes 8388624 | tf_op jit(solution)/shard_map/all_gather | solution.py:129
  627.7 15.0 fusion.101
  642.7 134.4 %all-gather.21.cloned.1.call-done = bf16[2,1024,2048]{2,1,0:T(8,128)(2,1)} async-done(((bf16[2,256,2048]{2,1,0:T(8,128)(2,1)}), bf16[2,1024,2048]{2,1,0:T(8,128)(2,1)}) %all-gather.21.cloned.1.call-update) | async-done | bytes 8388624 | tf_op jit(solution)/shard_map/all_gather | solution.py:131
  777.1 19.6 multiply_convert_fusion
  809.4 23.4 copy.236
  837.8 88.4 %all-to-all-done.1 = bf16[1,2,960,2048]{3,1,0,2:T(2,128)(2,1)} async-done(((bf16[1,2,960,2048]{3,1,0,2:T(2,128)(2,1)}), bf16[1,2,960,2048]{3,1,0,2:T(2,128)(2,1)}, u32[]{:S(2)}, u32[]{:S(2)}) %all-to-all-start.1) | async-done | bytes 7864352 | tf_op jit(solution)/shard_map/all_to_all | solution.py:187
  936.1 17.4 gather_fusion
  963.2 15.7 fusion.106
  978.9 16.0 fusion.105
  995.0 15.7 fusion.104
  1010.8 15.2 fusion.103
  1026.0 16.2 fusion.6
  1055.9 93.1 %all_to_all.60 = bf16[1,2,960,2048]{3,1,0,2:T(2,128)(2,1)S(1)} all-to-all(bf16[1,2,960,2048]{3,1,0,2:T(2,128)(2,1)S(1)} %copy.240), channel_id=1, replica_groups=mesh['dp'=4,'expert'=8] {'expert'}, dimensions={2} | all-to-all | bytes 15728640 | tf_op jit(solution)/shard_map/all_to_all | solution.py:236
  1155.9 17.4 gather_fusion.1
  1265.3 41.5 %all-reduce.12 = (f32[2048]{0:T(1024)S(1)}, f32[2048]{0:T(1024)S(1)}, f32[2048]{0:T(1024)S(1)}, f32[2048]{0:T(1024)S(1)}) all-reduce(f32[2048]{0:T(1024)S(1)} %get-tuple-element.22, f32[2048]{0:T(1024)S(1)} %bitcast.236, f32[2048]{0:T(1024)S(1)} %bitcast.235, ...), channel_id=10, replica_groups=mesh['dp'=4,'expert'=8] {'dp','expert'}, use_global_device_ids=true, to_apply=%region_37.38.clone | all-reduce | flops 8192 | bytes 65536
  1313.3 62.4 %reduce-scatter.23.cloned.1.call-done = f32[2,256,2048]{2,1,0:T(8,128)} async-done(((f32[2,1024,2048]{2,1,0:T(8,128)}), f32[2,256,2048]{2,1,0:T(8,128)}) %reduce-scatter.23.cloned.1.call-update) | async-done | bytes 4194320 | tf_op jit(solution)/shard_map/reduce_scatter | solution.py:245
  1375.8 283.8 %reduce-scatter.21.cloned.1.call-done = f32[2,512,1024]{2,1,0:T(8,128)} async-done(((f32[2,2048,1024]{2,1,0:T(8,128)}), f32[2,512,1024]{2,1,0:T(8,128)}) %reduce-scatter.21.cloned.1.call-update) | async-done | bytes 4194320 | tf_op jit(solution)/shard_map/reduce_scatter | solution.py:244
  1659.6 284.1 %reduce-scatter.19.cloned.1.call-done = f32[2,512,1024]{2,1,0:T(8,128)} async-done(((f32[2,2048,1024]{2,1,0:T(8,128)}), f32[2,512,1024]{2,1,0:T(8,128)}) %reduce-scatter.19.cloned.1.call-update) | async-done | bytes 4194320 | tf_op jit(solution)/shard_map/reduce_scatter | solution.py:243
  1943.7 186.2 %reduce-scatter.17.cloned.1.call-done = f32[64,2048]{1,0:T(8,128)} async-done(((f32[2048,2048]{1,0:T(8,128)}), f32[64,2048]{1,0:T(8,128)}) %reduce-scatter.17.cloned.1.call-update) | async-done | bytes 524304 | tf_op jit(solution)/shard_map/reduce_scatter | solution.py:307
  2129.9 187.4 %reduce-scatter.15.cloned.1.call-done = f32[64,2048]{1,0:T(8,128)} async-done(((f32[2048,2048]{1,0:T(8,128)}), f32[64,2048]{1,0:T(8,128)}) %reduce-scatter.15.cloned.1.call-update) | async-done | bytes 524304 | tf_op jit(solution)/shard_map/reduce_scatter | solution.py:306
  2317.3 187.2 %reduce-scatter.13.cloned.1.call-done = f32[64,2048]{1,0:T(8,128)} async-done(((f32[2048,2048]{1,0:T(8,128)}), f32[64,2048]{1,0:T(8,128)}) %reduce-scatter.13.cloned.1.call-update) | async-done | bytes 524304 | tf_op jit(solution)/shard_map/reduce_scatter | solution.py:305
  2504.5 187.2 %reduce-scatter.11.cloned.1.call-done = f32[64,2048]{1,0:T(8,128)} async-done(((f32[2048,2048]{1,0:T(8,128)}), f32[64,2048]{1,0:T(8,128)}) %reduce-scatter.11.cloned.1.call-update) | async-done | bytes 524304 | tf_op jit(solution)/shard_map/reduce_scatter | solution.py:304
  (336 shorter events, 246.0 us)
Async XLA Ops:
  7.2 98.4 %all-gather.13.cloned.1.call-start = ((), (), s32[]{:S(2)}) async-start(), calls=%async_computation.14 | async-start | bytes 8650752 | tf_op jit(solution)/shard_map/all_gather | solution.py:118
  7.9 163.0 %all-gather.11.cloned.1.call-start = ((), (), s32[]{:S(2)}) async-start(), calls=%async_computation.13 | async-start | bytes 8650752 | tf_op jit(solution)/shard_map/all_gather | solution.py:117
  8.7 241.2 %all-gather.9.cloned.1.call-start = ((), (), s32[]{:S(2)}) async-start(), calls=%async_computation.12 | async-start | bytes 8650752 | tf_op jit(solution)/shard_map/all_gather | solution.py:119
  9.4 319.3 %all-gather.15.cloned.1.call-start = ((), (), s32[]{:S(2)}) async-start(), calls=%async_computation.15 | async-start | bytes 8650752 | tf_op jit(solution)/shard_map/all_gather | solution.py:120
  10.0 549.1 %all-gather.19.cloned.1.call-start = ((), (), s32[]{:S(2)}) async-start(), calls=%async_computation.17 | async-start | bytes 10485760 | tf_op jit(solution)/shard_map/all_gather | solution.py:130
  10.6 617.0 %all-gather.17.cloned.1.call-start = ((), (), s32[]{:S(2)}) async-start(), calls=%async_computation.16 | async-start | bytes 10485760 | tf_op jit(solution)/shard_map/all_gather | solution.py:129
  11.2 92.3 %copy-start.34 = (bf16[192,2048]{1,0:T(8,128)(2,1)S(1)}, bf16[192,2048]{1,0:T(8,128)(2,1)}, u32[]{:S(2)}) copy-start(bf16[192,2048]{1,0:T(8,128)(2,1)} %param.17) | copy-start | bytes 2359300
  12.3 237.6 %copy-start.72 = (f32[192]{0:T(256)}, f32[192]{0:T(256)S(1)}, u32[]{:S(2)}) copy-start(f32[192]{0:T(256)S(1)} %fusion.83) | copy-start | bytes 2308
  55.8 194.0 %copy-start.48 = (f32[2048]{0:T(1024)}, f32[2048]{0:T(1024)S(1)}, u32[]{:S(2)}) copy-start(f32[2048]{0:T(1024)S(1)} %convert_element_type.135) | copy-start | bytes 24580
  55.8 278.4 %copy-start.70 = (f32[2048]{0:T(1024)}, f32[2048]{0:T(1024)S(1)}, u32[]{:S(2)}) copy-start(f32[2048]{0:T(1024)S(1)} %convert_element_type.144) | copy-start | bytes 24580
  103.5 232.0 %copy-start.46 = (bf16[2048,16]{0,1:T(8,128)(2,1)}, bf16[2048,16]{0,1:T(8,128)(2,1)S(1)}, u32[]{:S(2)}) copy-start(bf16[2048,16]{0,1:T(8,128)(2,1)S(1)} %reshape.506) | copy-start | bytes 196612
  105.0 73.9 %copy-start.68 = (f32[16,128]{1,0:T(8,128)}, f32[16,128]{1,0:T(8,128)S(1)}, u32[]{:S(2)}) copy-start(f32[16,128]{1,0:T(8,128)S(1)} %get-tuple-element.64) | copy-start | bytes 24580
  105.0 74.5 %copy-start.66 = (f32[16,128]{1,0:T(8,128)}, f32[16,128]{1,0:T(8,128)S(1)}, u32[]{:S(2)}) copy-start(f32[16,128]{1,0:T(8,128)S(1)} %get-tuple-element.65) | copy-start | bytes 24580
  105.1 76.1 %copy-start.44 = (pred[192,192]{0,1:T(8,128)(4,1)}, pred[192,192]{0,1:T(8,128)(4,1)S(1)}, u32[]{:S(2)}) copy-start(pred[192,192]{0,1:T(8,128)(4,1)S(1)} %broadcast_compare_fusion) | copy-start | bytes 110596
  105.5 74.4 %copy-start.38 = (f32[192,64]{1,0:T(8,128)}, f32[192,64]{1,0:T(8,128)S(1)}, u32[]{:S(2)}) copy-start(f32[192,64]{1,0:T(8,128)S(1)} %get-tuple-element.54) | copy-start | bytes 147460
  105.5 74.4 %copy-start.40 = (f32[192,64]{1,0:T(8,128)}, f32[192,64]{1,0:T(8,128)S(1)}, u32[]{:S(2)}) copy-start(f32[192,64]{1,0:T(8,128)S(1)} %get-tuple-element.55) | copy-start | bytes 147460
  110.9 68.0 %copy-start.4 = (f32[192,2048]{1,0:T(8,128)}, f32[192,2048]{1,0:T(8,128)S(1)}, u32[]{:S(2)}) copy-start(f32[192,2048]{1,0:T(8,128)S(1)} %fusion.93) | copy-start | bytes 4718596
  113.2 65.6 %copy-start.64 = (f32[192,16]{0,1:T(8,128)}, f32[192,16]{0,1:T(8,128)S(1)}, u32[]{:S(2)}) copy-start(f32[192,16]{0,1:T(8,128)S(1)} %copy.223) | copy-start | bytes 36868
  185.0 70.1 %copy-start.10 = (bf16[16,192,192]{1,2,0:T(8,128)(2,1)}, bf16[16,192,192]{1,2,0:T(8,128)(2,1)S(1)}, u32[]{:S(2)}) copy-start(bf16[16,192,192]{1,2,0:T(8,128)(2,1)S(1)} %divide_convert_fusion) | copy-start | bytes 3538948
  257.2 76.9 %copy-start.28 = (bf16[16,24,8,128]{3,2,1,0:T(8,128)(2,1)}, bf16[16,24,8,128]{3,2,1,0:T(8,128)(2,1)S(1)}, u32[]{:S(2)}) copy-start(bf16[16,24,8,128]{3,2,1,0:T(8,128)(2,1)S(1)} %fusion.35) | copy-start | bytes 2359300
  364.2 93.4 %all-to-all-start.2 = ((bf16[8,2,120,2048]{3,2,1,0:T(8,128)(2,1)}), bf16[8,2,120,2048]{3,2,1,0:T(8,128)(2,1)}, u32[]{:S(2)}, u32[]{:S(2)}) async-start(bf16[8,2,120,2048]{3,2,1,0:T(8,128)(2,1)} %bitcast.221), calls=%async_computation.2 | async-start | bytes 15728640 | tf_op jit(solution)/shard_map/all_to_all | solution.py:205
  369.1 408.0 %all-gather.21.cloned.1.call-start = ((), (), s32[]{:S(2)}) async-start(), calls=%async_computation.18 | async-start | bytes 10485760 | tf_op jit(solution)/shard_map/all_gather | solution.py:131
  457.5 93.5 %all-to-all-start = ((bf16[8,2,120,2048]{3,2,1,0:T(8,128)(2,1)}), bf16[8,2,120,2048]{3,2,1,0:T(8,128)(2,1)}, u32[]{:S(2)}, u32[]{:S(2)}) async-start(bf16[8,2,120,2048]{3,2,1,0:T(8,128)(2,1)} %bitcast.222), calls=%async_computation | async-start | bytes 15728640 | tf_op jit(solution)/shard_map/all_to_all | solution.py:178
  832.8 93.3 %all-to-all-start.1 = ((bf16[1,2,960,2048]{3,1,0,2:T(2,128)(2,1)}), bf16[1,2,960,2048]{3,1,0,2:T(2,128)(2,1)}, u32[]{:S(2)}, u32[]{:S(2)}) async-start(bf16[1,2,960,2048]{3,1,0,2:T(2,128)(2,1)} %copy.236), calls=%async_computation.1 | async-start | bytes 15728640 | tf_op jit(solution)/shard_map/all_to_all | solution.py:187
  837.7 474.2 %reduce-scatter.25.cloned.1.call-start = ((), (), s32[]{:S(2)}) async-start(), calls=%async_computation.26 | async-start | bytes 1081344
  963.1 412.6 %reduce-scatter.23.cloned.1.call-start = ((), (), s32[]{:S(2)}) async-start(), calls=%async_computation.25 | async-start | bytes 20971520 | tf_op jit(solution)/shard_map/reduce_scatter | solution.py:245
  978.9 680.7 %reduce-scatter.21.cloned.1.call-start = ((), (), s32[]{:S(2)}) async-start(), calls=%async_computation.24 | async-start | bytes 20971520 | tf_op jit(solution)/shard_map/reduce_scatter | solution.py:244
  994.9 948.8 %reduce-scatter.19.cloned.1.call-start = ((), (), s32[]{:S(2)}) async-start(), calls=%async_computation.23 | async-start | bytes 20971520 | tf_op jit(solution)/shard_map/reduce_scatter | solution.py:243
  1010.7 1119.2 %reduce-scatter.17.cloned.1.call-start = ((), (), s32[]{:S(2)}) async-start(), calls=%async_computation.22 | async-start | bytes 17301504 | tf_op jit(solution)/shard_map/reduce_scatter | solution.py:307
  1192.5 1124.8 %reduce-scatter.15.cloned.1.call-start = ((), (), s32[]{:S(2)}) async-start(), calls=%async_computation.21 | async-start | bytes 17301504 | tf_op jit(solution)/shard_map/reduce_scatter | solution.py:306
  1209.3 1295.2 %reduce-scatter.13.cloned.1.call-start = ((), (), s32[]{:S(2)}) async-start(), calls=%async_computation.20 | async-start | bytes 17301504 | tf_op jit(solution)/shard_map/reduce_scatter | solution.py:305
  1231.5 1460.2 %reduce-scatter.11.cloned.1.call-start = ((), (), s32[]{:S(2)}) async-start(), calls=%async_computation.19 | async-start | bytes 17301504 | tf_op jit(solution)/shard_map/reduce_scatter | solution.py:304
  (76 other events, 439.8 us)
Sparse Core Ops, SparseCore 0:
  10.9 81.2 all-gather.12
  95.1 75.8 all-gather.10
  173.8 76.0 all-gather.8
  252.6 76.0 all-gather.14
  330.1 148.2 all-gather.18
  479.9 147.7 all-gather.16
  629.2 147.8 all-gather.20
  963.3 131.9 reduce-scatter.24
  1098.4 277.3 reduce-scatter.22
  1378.5 280.9 reduce-scatter.20
  1662.6 281.0 reduce-scatter.18
  1946.4 183.4 reduce-scatter.16
  2132.8 184.4 reduce-scatter.14
  2320.0 184.4 reduce-scatter.12
  2507.2 184.4 reduce-scatter.10
where the time goes:
time: 2700 us
  waiting for transfers between devices  2010 us (74%)
  matrix products  229 us (8%)
  blocking collectives  219 us (8%)
  local copies, waits for them, and re-layouts  153 us (6%)
  other arithmetic  58.5 us (2%)
    reduce_scatter x1, waiting for transfers between devices, local(): lax.psum_scatter(grad_gate_local, 'dp', scatter_dimension=1, tiled=True)  284 us
    reduce_scatter x1, waiting for transfers between devices, local(): lax.psum_scatter(grad_up_local, 'dp', scatter_dimension=1, tiled=True)  284 us
    reduce_scatter x1, waiting for transfers between devices, local(): lax.psum_scatter(grad_value_local, ('dp', 'expert'), scatter_dimension=0,...  187 us
    reduce_scatter x1, waiting for transfers between devices, local(): lax.psum_scatter(grad_key_local, ('dp', 'expert'), scatter_dimension=0, t...  187 us
    reduce_scatter x1, waiting for transfers between devices, local(): lax.psum_scatter(grad_query_local, ('dp', 'expert'), scatter_dimension=0,...  187 us
    reduce_scatter x1, waiting for transfers between devices, local(): lax.psum_scatter(grad_out_local, ('dp', 'expert'), scatter_dimension=0, t...  186 us
    all_gather x1, waiting for transfers between devices, local(): lax.all_gather(w_down, 'dp', axis=1, tiled=True)  134 us
    all_to_all x1, blocking collectives, local(): lax.all_to_all(grad_arrival, 'expert', split_axis=2, concat_axis=0, tiled...  93.1 us
  transfers between devices with their start and end apart: 18, of which 15 were waited for; matrix products, arithmetic and copies ran while one was open for 12% of the time, Pallas kernels for 0%

commit v1 on v0

--- a/solution.py
+++ b/solution.py
@@ -1,6 +1,10 @@
+import functools
+
 import jax
 import jax.numpy as jnp
 from jax import lax
+from jax.experimental import pallas as pl
+from jax.experimental.pallas import tpu as pltpu
 from jax.sharding import PartitionSpec as P
 
 D = 2048
@@ -86,7 +90,7 @@
     )
 
 
-def local(
+def by_axes(
     tokens,
     cotangent,
     lengths,
@@ -329,6 +333,464 @@
     )
 
 
+SLOTS = 128
+
+
+def flip(value, bit):
+    count = lax.axis_size("expert")
+    return lax.ppermute(value, "expert", [(i, i ^ bit) for i in range(count)])
+
+
+def turn(value, step):
+    count = lax.axis_size("dp")
+    return lax.ppermute(value, "dp", [(i, (i + step) % count) for i in range(count)])
+
+
+def order_kernel(to_own, order_ref, v_ref, o_ref):
+    half = 64
+    lanes = v_ref.shape[1] // 2
+    groups = v_ref.shape[1] // 128
+    odd = order_ref[groups] == 1
+    for pair in range(groups // 2):
+        first = pl.ds(pl.multiple_of(order_ref[2 * pair] * 128, 128), 128)
+        second = pl.ds(pl.multiple_of(order_ref[2 * pair + 1] * 128, 128), 128)
+        if to_own:
+            a = v_ref[:, first].astype(jnp.float32)
+            b = v_ref[:, second].astype(jnp.float32)
+            low = jnp.concatenate([a[:, :half], b[:, :half]], axis=1)
+            high = jnp.concatenate([a[:, half:], b[:, half:]], axis=1)
+            o_ref[:, pair * 128 : pair * 128 + 128] = jnp.where(odd, high, low).astype(o_ref.dtype)
+            o_ref[:, lanes + pair * 128 : lanes + pair * 128 + 128] = jnp.where(
+                odd, low, high
+            ).astype(o_ref.dtype)
+        else:
+            low = v_ref[:, pair * 128 : pair * 128 + 128].astype(jnp.float32)
+            high = v_ref[:, lanes + pair * 128 : lanes + pair * 128 + 128].astype(jnp.float32)
+            low, high = jnp.where(odd, high, low), jnp.where(odd, low, high)
+            o_ref[:, first] = jnp.concatenate([low[:, :half], high[:, :half]], axis=1).astype(
+                o_ref.dtype
+            )
+            o_ref[:, second] = jnp.concatenate([low[:, half:], high[:, half:]], axis=1).astype(
+                o_ref.dtype
+            )
+
+
+def reorder(value, order, to_own):
+    return pl.pallas_call(
+        functools.partial(order_kernel, to_own),
+        out_shape=jax.ShapeDtypeStruct(value.shape, value.dtype),
+        in_specs=[
+            pl.BlockSpec(memory_space=pltpu.SMEM),
+            pl.BlockSpec(memory_space=pltpu.VMEM),
+        ],
+        out_specs=pl.BlockSpec(memory_space=pltpu.VMEM),
+        compiler_params=pltpu.CompilerParams(vmem_limit_bytes=16 * 1024 * 1024),
+        cost_estimate=pl.CostEstimate(flops=0, bytes_accessed=4 * value.size, transcendentals=0),
+    )(order, value)
+
+
+def ring_gather(value):
+    pieces = [value]
+    for _ in range(lax.axis_size("dp") - 1):
+        pieces.append(turn(pieces[-1], 1))
+    return pieces
+
+
+def ring_scatter(pieces):
+    total = pieces[-1]
+    for piece in pieces[-2::-1]:
+        total = turn(total, -1).astype(jnp.float32) + piece.astype(jnp.float32)
+        if piece is not pieces[0]:
+            total = total.astype(piece.dtype)
+    return total
+
+
+def gather_weight(shard):
+    half = shard.shape[1] // 2
+    pieces = ring_gather(shard)
+    left = jnp.concatenate([p[:, :half] for p in pieces], axis=0)
+    right = jnp.concatenate([p[:, half:] for p in pieces], axis=0)
+    left_x, right_y = flip(left, 2), flip(right, 4)
+    left = jnp.concatenate([left, left_x], axis=0)
+    right = jnp.concatenate([right, right_y], axis=0)
+    left_y, right_x = flip(left, 4), flip(right, 2)
+    n = left.shape[0] // 2
+    own = jnp.concatenate(
+        [
+            jnp.concatenate([left, left_y], axis=0),
+            jnp.concatenate([right[:n], right_x[:n], right[n:], right_x[n:]], axis=0),
+        ],
+        axis=1,
+    )
+    return own, flip(own, 1)
+
+
+def scatter_weight(own, other, rows):
+    width = own.shape[1]
+    half = width // 2
+    n = own.shape[0] // 4
+    low = jnp.bfloat16
+    total = (own + flip(other.astype(low), 1).astype(jnp.float32)).astype(low)
+    left, right = total[:, :half], total[:, half:]
+    left_y = flip(left[2 * n :], 4).astype(jnp.float32)
+    right_x = flip(jnp.concatenate([right[n : 2 * n], right[3 * n :]], axis=0), 2).astype(
+        jnp.float32
+    )
+    left = (left[: 2 * n].astype(jnp.float32) + left_y).astype(low)
+    right = (
+        jnp.concatenate([right[:n], right[2 * n : 3 * n]], axis=0).astype(jnp.float32) + right_x
+    ).astype(low)
+    left_x, right_y = flip(left[n:], 2).astype(jnp.float32), flip(right[n:], 4).astype(jnp.float32)
+    total = jnp.concatenate(
+        [
+            left[:n].astype(jnp.float32) + left_x,
+            right[:n].astype(jnp.float32) + right_y,
+        ],
+        axis=1,
+    ).astype(low)
+    return ring_scatter([total[i * rows : (i + 1) * rows] for i in range(n // rows)])
+
+
+def gather_small(shard, shard_order):
+    pieces = jnp.stack(ring_gather(shard))
+    for bit in (2, 4, 1):
+        pieces = jnp.concatenate([pieces, flip(pieces, bit)], axis=0)
+    return jnp.take(pieces, shard_order, axis=0).reshape(-1, shard.shape[1])
+
+
+def scatter_small(value, shard_order, rows):
+    pieces = jnp.take(value.reshape(-1, rows, value.shape[1]), shard_order, axis=0)
+    for bit in (1, 4, 2):
+        n = pieces.shape[0] // 2
+        pieces = pieces[:n] + flip(pieces[n:], bit)
+    return ring_scatter([pieces[i] for i in range(pieces.shape[0])])
+
+
+def gather_tokens(value):
+    pieces = ring_gather(value)
+    mine = pieces + [flip(p, 2) for p in pieces]
+    mine = jnp.stack(mine)
+    return jnp.concatenate([mine, flip(mine, 1)], axis=0)
+
+
+def scatter_tokens(blocks):
+    n = blocks.shape[0] // 4
+    low = blocks.dtype
+    wide = jnp.float32
+    across = blocks[2 * n :]
+    total = (blocks[: 2 * n].astype(wide) + flip(across, 1).astype(wide)).astype(low)
+    total = (total[:n].astype(wide) + flip(total[n:], 2).astype(wide)).astype(low)
+    return ring_scatter([total[i] for i in range(n)])
+
+
+def expert_rounds(count_dp, count_expert):
+    rounds = []
+    for k in range(count_dp):
+        pairs = []
+        for d in range(count_dp):
+            part = (d + k) % count_dp
+            for e in range(count_expert):
+                goal = 2 * (e & 1) + part // 2
+                pairs.append((d * count_expert + e, goal * count_expert + (e & ~1) + part % 2))
+        rounds.append(pairs)
+    return rounds
+
+
+def gather_expert(weight, place):
+    d, c, x, y = place
+    count_dp, count_expert = lax.axis_size("dp"), lax.axis_size("expert")
+    _, depth, width = weight.shape
+    half = width // 2
+    held = jnp.zeros((count_dp, depth, half), weight.dtype)
+    for k, pairs in enumerate(expert_rounds(count_dp, count_expert)):
+        part = (d + k) % count_dp
+        piece = lax.dynamic_slice(weight, (part // 2, 0, half * (part % 2)), (1, depth, half))
+        piece = lax.ppermute(piece, ("dp", "expert"), pairs)
+        source = (2 * (d % 2) + c - k) % count_dp
+        held = lax.dynamic_update_slice(held, piece, (source, 0, 0))
+    held = held.reshape(count_dp * depth, half)
+    far = flip(held, 4)
+    keep = jnp.where(y == c, held, far)
+    give = jnp.where(y == c, far, held)
+    got = flip(give, 1)
+    return jnp.concatenate(
+        [jnp.where(c == 0, keep, got), jnp.where(c == 0, got, keep)], axis=1
+    )
+
+
+def scatter_expert(grad, place):
+    d, c, x, y = place
+    count_dp, count_expert = lax.axis_size("dp"), lax.axis_size("expert")
+    half = grad.shape[1] // 2
+    depth = grad.shape[0] // count_dp
+    left, right = grad[:, :half], grad[:, half:]
+    keep = jnp.where(c == 0, left, right)
+    give = jnp.where(c == 0, right, left)
+    got = flip(give, 1)
+    far = flip(jnp.where(y == c, got, keep), 4)
+    total = jnp.where(y == c, keep, got).astype(jnp.float32) + far.astype(jnp.float32)
+    total = total.astype(grad.dtype).reshape(count_dp, depth, half)
+    out = jnp.zeros((2, depth, 2 * half), jnp.float32)
+    for k, pairs in enumerate(expert_rounds(count_dp, count_expert)):
+        source = (2 * (d % 2) + c - k) % count_dp
+        piece = lax.dynamic_slice(total, (source, 0, 0), (1, depth, half))
+        piece = lax.ppermute(piece, ("dp", "expert"), [(b, a) for a, b in pairs])
+        part = (d + k) % count_dp
+        out = lax.dynamic_update_slice(
+            out, piece.astype(jnp.float32), (part // 2, 0, half * (part % 2))
+        )
+    return out
+
+
+def by_links(
+    tokens,
+    cotangent,
+    lengths,
+    routes,
+    w_query,
+    w_key,
+    w_value,
+    w_out,
+    w_router,
+    w_gate,
+    w_up,
+    w_down,
+    g_attn,
+    g_query,
+    g_key,
+    g_ffn,
+):
+    low, wide = jnp.bfloat16, jnp.float32
+    row_count = tokens.shape[0]
+    rows = w_query.shape[0]
+    experts = w_router.shape[1]
+    count_dp = lax.axis_size("dp")
+    score_scale = HD ** (-0.5)
+    d = lax.axis_index("dp")
+    e = lax.axis_index("expert")
+    c, x, y = e & 1, (e >> 1) & 1, e >> 2
+    place = (d, c, x, y)
+    own_expert = 8 * c + 4 * x + d
+    group = jnp.arange(16, dtype=jnp.int32)
+    group_order = (
+        ((d - (group & 3)) % count_dp) * 4 + ((((group >> 3) & 1) ^ y) * 2 + (((group >> 2) & 1) ^ x))
+    )
+    order = jnp.concatenate([group_order, c[None]]).astype(jnp.int32)
+    shard = jnp.arange(32, dtype=jnp.int32)
+    to_own = group_order[shard & 15] * 2 + ((shard >> 4) ^ c)
+    to_whole = (
+        (((shard & 1) ^ c) * 16)
+        + (((shard >> 2) & 1) ^ y) * 8
+        + (((shard >> 1) & 1) ^ x) * 4
+        + (d - (shard >> 3)) % count_dp
+    )
+
+    slab = jnp.concatenate(
+        [w_router]
+        + [g[:, None] for g in (g_attn, g_query, g_key, g_ffn)]
+        + [jnp.zeros((rows, 128 - experts - 4), low)],
+        axis=1,
+    )
+    slab = gather_small(slab, to_whole)
+    router_w = slab[:, :experts]
+    attn_gain, query_gain, key_gain, ffn_gain = (
+        slab[:, experts + i].astype(wide) for i in range(4)
+    )
+    query_w = gather_weight(w_query)
+    key_w = gather_weight(w_key)
+    value_w = gather_weight(w_value)
+    out_w = gather_weight(w_out)
+    routes_all = gather_tokens(routes)
+    gate_w = gather_expert(w_gate, place)
+    up_w = gather_expert(w_up, place)
+    down_w = gather_expert(w_down, place)
+    grad_out_all = gather_tokens(cotangent)
+
+    segment, offset = layout(lengths[0], row_count)
+    seq_mask = (segment[:, None] == segment[None, :])[None]
+    inputs = tokens.astype(wide)
+    normed_f, norm_attn_pull = jax.vjp(normalize, inputs, attn_gain)
+    normed_attn = reorder(normed_f.astype(low), order, True)
+    half = D // 2
+
+    def times(left, pair):
+        return jnp.dot(left[:, :half], pair[0], preferred_element_type=wide) + jnp.dot(
+            left[:, half:], pair[1], preferred_element_type=wide
+        )
+
+    raw_q = times(normed_attn, query_w)
+    raw_k = times(normed_attn, key_w)
+    values = times(normed_attn, value_w).astype(low)
+    value_heads = values.reshape(row_count, HEADS, HD)
+
+    def prep_local(first, second, first_gain, second_gain):
+        return head_prep(first, second, first_gain, second_gain, offset)
+
+    rotated, heads_pull = jax.vjp(prep_local, raw_q, raw_k, query_gain, key_gain)
+    queries = rotated[0].astype(low)
+    keys_rot = rotated[1].astype(low)
+    scores = (
+        jnp.einsum("qhd,khd->hqk", queries, keys_rot, preferred_element_type=wide) * score_scale
+    )
+    scores = jnp.where(seq_mask, scores, -1e30)
+    peak = jnp.max(scores, axis=-1, keepdims=True)
+    exp_scores = jnp.exp(scores - peak)
+    exp_total = jnp.sum(exp_scores, axis=-1, keepdims=True)
+    log_total = peak + jnp.log(exp_total)
+    probs_low = (exp_scores / exp_total).astype(low)
+    context = (
+        jnp.einsum("hqk,khd->qhd", probs_low, value_heads, preferred_element_type=wide)
+        .astype(low)
+        .reshape(row_count, D)
+    )
+    context = reorder(context, order, True)
+    midway = inputs + times(context, out_w)
+    normed2_f, norm_ffn_pull = jax.vjp(normalize, midway, ffn_gain)
+    normed_ffn = normed2_f.astype(low)
+
+    normed_all = gather_tokens(normed_ffn)
+    blocks = normed_all.shape[0]
+
+    def dense_gates(logits, named):
+        logits = jnp.where(named, logits, -jnp.inf)
+        exp_logits = jnp.exp(logits - jnp.max(logits, axis=-1, keepdims=True))
+        return exp_logits / jnp.sum(exp_logits, axis=-1, keepdims=True)
+
+    expert_ids = jnp.arange(experts, dtype=jnp.int32)
+
+    def named_of(table):
+        return jnp.any(table[..., :, None] == expert_ids, axis=-2)
+
+    logits_all = jnp.einsum("btd,de->bte", normed_all, router_w, preferred_element_type=wide)
+    named_all = named_of(routes_all)
+    gates_all = dense_gates(logits_all, named_all)
+    mine = (expert_ids == own_expert)[None, None, :]
+    own_gate = jnp.sum(jnp.where(mine, gates_all, 0.0), axis=2)
+    own_named = jnp.any(named_all & mine, axis=2)
+    rank = jnp.cumsum(own_named.astype(jnp.int32), axis=1) - 1
+    slot_ids = jnp.arange(SLOTS, dtype=jnp.int32)
+    chosen = (rank[:, None, :] == slot_ids[None, :, None]) & own_named[:, None, :]
+    picks = chosen.astype(low)
+    slot_gate = jnp.sum(jnp.where(chosen, own_gate[:, None, :], 0.0), axis=2)
+
+    def to_slots(value):
+        return jnp.einsum("bst,btd->bsd", picks, value, preferred_element_type=wide).astype(low)
+
+    def to_tokens(value):
+        return jnp.einsum("bst,bsd->btd", picks, value, preferred_element_type=wide).astype(low)
+
+    arrived = to_slots(normed_all).reshape(blocks * SLOTS, D)
+    grad_rows = to_slots(grad_out_all)
+    gate_act = jnp.dot(arrived, gate_w, preferred_element_type=wide)
+    up_act = jnp.dot(arrived, up_w, preferred_element_type=wide)
+    hidden = swiglu(gate_act, up_act).astype(low)
+    produced = (
+        jnp.dot(hidden, down_w, preferred_element_type=wide).astype(low).reshape(blocks, SLOTS, D)
+    )
+    slot_grad_gate = jnp.sum(grad_rows.astype(wide) * produced.astype(wide), axis=2)
+    grad_gates_own = jnp.sum(jnp.where(chosen, slot_grad_gate[:, :, None], 0.0), axis=1)
+    grad_gates_all = jnp.where(
+        (expert_ids == own_expert)[None, :, None], grad_gates_own[:, None, :], 0.0
+    )
+    grad_gates = scatter_tokens(grad_gates_all).T
+    moe_part = to_tokens((slot_gate[:, :, None] * produced.astype(wide)).astype(low))
+    grad_produced = (
+        (slot_gate[:, :, None] * grad_rows.astype(wide)).astype(low).reshape(blocks * SLOTS, D)
+    )
+    grad_hidden = times_transposed(grad_produced, down_w)
+    act_unused, act_pull = jax.vjp(swiglu, gate_act, up_act)
+    grad_gate_act, grad_up_act = act_pull(grad_hidden)
+    grad_gate_low = grad_gate_act.astype(low)
+    grad_up_low = grad_up_act.astype(low)
+    grad_arrival = (
+        times_transposed(grad_gate_low, gate_w) + times_transposed(grad_up_low, up_w)
+    ).astype(low)
+    grad_normed_ffn = scatter_tokens(to_tokens(grad_arrival.reshape(blocks, SLOTS, D)))
+    block_out = (midway + scatter_tokens(moe_part)).astype(low)
+    grad_down = scatter_expert(contract_rows(hidden, grad_produced).astype(low), place)
+    grad_gate = scatter_expert(contract_rows(arrived, grad_gate_low).astype(low), place)
+    grad_up = scatter_expert(contract_rows(arrived, grad_up_low).astype(low), place)
+
+    grad_out = cotangent.astype(wide)
+    gates = gates_all[0]
+    grad_chosen = gates * (grad_gates - jnp.sum(gates * grad_gates, axis=1, keepdims=True))
+    grad_logits = grad_chosen.astype(low)
+    grad_router_local = contract_rows(normed_ffn, grad_logits)
+    grad_normed_ffn = grad_normed_ffn + times_transposed(grad_logits, router_w)
+    grad_midway_norm, grad_ffn_gain = norm_ffn_pull(grad_normed_ffn)
+    grad_midway = grad_out + grad_midway_norm
+    grad_attn = grad_midway.astype(low)
+
+    def weight_grad(left, right):
+        own = contract_rows(left[:, :half], right)
+        other = contract_rows(left[:, half:], right)
+        return scatter_weight(own, other, rows)
+
+    def times_back(left, pair):
+        return jnp.concatenate(
+            [times_transposed(left, pair[0]), times_transposed(left, pair[1])], axis=1
+        )
+
+    grad_outproj = weight_grad(context, grad_attn)
+    grad_context = reorder(times_back(grad_attn, out_w).astype(low), order, False).reshape(
+        row_count, HEADS, HD
+    )
+    probs = jnp.where(seq_mask, jnp.exp(scores - log_total), 0.0)
+    grad_probs = jnp.einsum("qhd,khd->hqk", grad_context, value_heads, preferred_element_type=wide)
+    grad_scores = (
+        probs * (grad_probs - jnp.sum(grad_probs * probs, axis=-1, keepdims=True))
+    ).astype(low)
+    grad_values = (
+        jnp.einsum("hqk,qhd->khd", probs_low, grad_context, preferred_element_type=wide)
+        .astype(low)
+        .reshape(row_count, D)
+    )
+    grad_queries = (
+        jnp.einsum("hqk,khd->qhd", grad_scores, keys_rot, preferred_element_type=wide)
+        * score_scale
+    )
+    grad_keys = (
+        jnp.einsum("hqk,qhd->khd", grad_scores, queries, preferred_element_type=wide) * score_scale
+    )
+    grad_raw_q, grad_raw_k, grad_query_gain, grad_key_gain = heads_pull((grad_queries, grad_keys))
+    grad_raw_q = grad_raw_q.astype(low)
+    grad_raw_k = grad_raw_k.astype(low)
+    grad_value = weight_grad(normed_attn, grad_values)
+    grad_query = weight_grad(normed_attn, grad_raw_q)
+    grad_key = weight_grad(normed_attn, grad_raw_k)
+    grad_normed_attn = (
+        times_back(grad_raw_q, query_w)
+        + times_back(grad_raw_k, key_w)
+        + times_back(grad_values, value_w)
+    )
+    grad_normed_attn = reorder(grad_normed_attn, order, False)
+    grad_inputs_norm, grad_attn_gain = norm_attn_pull(grad_normed_attn)
+    grad_tokens = (grad_midway + grad_inputs_norm).astype(low)
+    small = jnp.concatenate(
+        [grad_router_local]
+        + [g[:, None] for g in (grad_attn_gain, grad_query_gain, grad_key_gain, grad_ffn_gain)]
+        + [jnp.zeros((D, 128 - experts - 4), wide)],
+        axis=1,
+    )
+    small = scatter_small(small, to_own, rows)
+    return (
+        block_out,
+        grad_tokens,
+        grad_query,
+        grad_key,
+        grad_value,
+        grad_outproj,
+        small[:, :experts],
+        grad_gate,
+        grad_up,
+        grad_down,
+        small[:, experts],
+        small[:, experts + 1],
+        small[:, experts + 2],
+        small[:, experts + 3],
+    )
+
+
 def solution(mesh):
     in_specs = (
         P(("dp", "expert"), None),
@@ -364,4 +826,5 @@
         P(("dp", "expert")),
         P(("dp", "expert")),
     )
+    local = by_links if (mesh.shape["dp"], mesh.shape["expert"]) == (4, 8) else by_axes
     return jax.shard_map(local, mesh=mesh, in_specs=in_specs, out_specs=out_specs, check_vma=False)

time: 2700 us -> 1620 us (0.60)
  waiting for transfers between devices: 2010 us -> 716 us
  starting transfers between devices: 16.1 us -> 348 us
  blocking collectives: 219 us -> 0 us
  other arithmetic: 58.5 us -> 133 us
    reduce_scatter x7 -> x0, waiting for transfers between devices: 1380 us -> none  [the longest x1 284 us: local(): lax.psum_scatter(grad_gate_local, 'dp', scatter_dimension=1, tiled=True)]
    ppermute x0 -> x151, waiting for transfers between devices: none -> 716 us  [the longest x79 452 us: flip(): return lax.ppermute(value, 'expert', [(i, i ^ bit) for i in range(count)])]
    all_gather x7 -> x0, waiting for transfers between devices: 382 us -> none  [the longest x1 134 us: local(): lax.all_gather(w_down, 'dp', axis=1, tiled=True)]
    ppermute x0 -> x151, starting transfers between devices: none -> 348 us  [the longest x48 141 us: turn(): lax.ppermute(value, 'dp', [(i, (i + step) % count) for i in range(count)])]
    all_to_all x3 -> x0, waiting for transfers between devices: 243 us -> none  [the longest x1 88.4 us: local(): lax.all_to_all(produced.reshape(1, local_experts, owners * capacity, D),...]
    all_to_all x1 -> x0, blocking collectives: 93.1 us -> none  [local(): lax.all_to_all(grad_arrival, 'expert', split_axis=2, concat_axis=0, tiled...]
    unnamed x2 -> x0, blocking collectives: 84 us -> none
    dot_general x20 -> x21, matrix products: 170 us -> 94 us  [the longest x1 15.3 us: by_links(): up_act = jnp.dot(arrived, up_w, preferred_element_type=wide)]
  transfers between devices with their start and end apart: 18 -> 151, of which waited for: 15 -> 69; matrix products, arithmetic and copies ran while one was open for 12% -> 23% of each run, Pallas kernels for 0% -> 0%
where the time goes in v1:
time: 1620 us; the launch traced here: 1610 us
  waiting for transfers between devices  716 us (44%)
  starting transfers between devices  348 us (21%)
  matrix products  252 us (16%)
  local copies, waits for them, and re-layouts  150 us (9%)
  other arithmetic  133 us (8%)
    ppermute x79, waiting for transfers between devices, flip(): return lax.ppermute(value, 'expert', [(i, i ^ bit) for i in range(count)])  452 us
    ppermute x48, waiting for transfers between devices, turn(): lax.ppermute(value, 'dp', [(i, (i + step) % count) for i in range(count)])  231 us
    ppermute x48, starting transfers between devices, turn(): lax.ppermute(value, 'dp', [(i, (i + step) % count) for i in range(count)])  141 us
    dot_general x12, matrix products, times_transposed(): lax.dot_general(left, right, (((1,), (1,)), ((), ())), preferred_element_...  80.6 us
    ppermute x79, starting transfers between devices, flip(): return lax.ppermute(value, 'expert', [(i, i ^ bit) for i in range(count)])  76.4 us
    unnamed x404, local copies, waits for them, and re-layouts  69.6 us
    ppermute x12, starting transfers between devices, gather_expert(): piece = lax.ppermute(piece, ('dp', 'expert'), pairs)  67.8 us
    dot_general x11, matrix products, contract_rows(): lax.dot_general(left, right, (((0,), (0,)), ((), ())), preferred_element_...  67.7 us
  transfers between devices with their start and end apart: 151, of which 69 were waited for; matrix products, arithmetic and copies ran while one was open for 23% of the time, Pallas kernels for 0%

profile of v1, /device:TPU:0, one launch (start us, length us, event | category | flops | bytes accessed | tf_op | source)
XLA Modules:
  0.0 1607.9 jit_solution(17541757977111453528)
XLA Ops:
  92.5 42.0 %collective-permute-start.68 = (bf16[1,256,1024]{2,1,0:T(8,128)(2,1)S(1)}, bf16[1,256,1024]{2,1,0:T(8,128)(2,1)S(1)}, u32[]{:S(2)}, u32[]{:S(2)}) collective-permute-start(bf16[1,256,1024]{2,1,0:T(8,128)(2,1)S(1)} %copy-done.103), channel_id=1, source_target_pairs={{0,8},{1,24},{2,10},{3,26},{4,12},{5,28},{6,14},{7,30},{8,9},{9,25... | collective-permute-start | bytes 1572872 | tf_op jit(solution)/shard_map/ppermute | solution.py:508
  142.4 19.5 %collective-permute-done.68 = bf16[1,256,1024]{2,1,0:T(8,128)(2,1)S(1)} collective-permute-done((bf16[1,256,1024]{2,1,0:T(8,128)(2,1)S(1)}, bf16[1,256,1024]{2,1,0:T(8,128)(2,1)S(1)}, u32[]{:S(2)}, u32[]{:S(2)}) %collective-permute-start.68) | collective-permute-done | bytes 524320 | tf_op jit(solution)/shard_map/ppermute | solution.py:508
  181.1 29.2 %collective-permute-start.8 = (bf16[64,2048]{1,0:T(8,128)(2,1)S(1)}, bf16[64,2048]{1,0:T(8,128)(2,1)S(1)}, u32[]{:S(2)}, u32[]{:S(2)}) collective-permute-start(bf16[64,2048]{1,0:T(8,128)(2,1)S(1)} %collective-permute-done.7), channel_id=1, source_target_pairs={{0,8},{8,16},{16,24},{24,0},{1,9},{9,17},{17,25},{25,1},{2,10},{10... | collective-permute-start | bytes 786440 | tf_op jit(solution)/shard_map/ppermute | solution.py:346
  269.5 20.3 %collective-permute-start.78 = (bf16[192,2048]{1,0:T(8,128)(2,1)}, bf16[192,2048]{1,0:T(8,128)(2,1)S(1)}, u32[]{:S(2)}, u32[]{:S(2)}) collective-permute-start(bf16[192,2048]{1,0:T(8,128)(2,1)} %collective-permute-done.77), channel_id=1, source_target_pairs={{0,8},{8,16},{16,24},{24,0},{1,9},{9,17},{17,25},{25,1},{2,10},{10... | collective-permute-start | bytes 2359304 | tf_op jit(solution)/shard_map/ppermute | solution.py:346
  302.4 33.9 %collective-permute-done.20 = bf16[512,1024]{1,0:T(8,128)(2,1)S(1)} collective-permute-done((bf16[512,1024]{1,0:T(8,128)(2,1)S(1)}, bf16[512,1024]{1,0:T(8,128)(2,1)S(1)}, u32[]{:S(2)}, u32[]{:S(2)}) %collective-permute-start.20) | collective-permute-done | bytes 1048608 | tf_op jit(solution)/shard_map/ppermute | solution.py:341
  353.6 14.8 collective-permute-done.36
  377.0 15.4 collective-permute-start.79
  459.9 15.9 collective-permute-done.46
  479.1 17.3 %collective-permute-done.47 = bf16[192,2048]{1,0:T(8,128)(2,1)S(1)} collective-permute-done((bf16[192,2048]{1,0:T(8,128)(2,1)S(1)}, bf16[192,2048]{1,0:T(8,128)(2,1)S(1)}, u32[]{:S(2)}, u32[]{:S(2)}) %collective-permute-start.47) | collective-permute-done | bytes 786464 | tf_op jit(solution)/shard_map/ppermute | solution.py:346
  499.1 17.0 %collective-permute-done.48 = bf16[192,2048]{1,0:T(8,128)(2,1)S(1)} collective-permute-done((bf16[192,2048]{1,0:T(8,128)(2,1)S(1)}, bf16[192,2048]{1,0:T(8,128)(2,1)S(1)}, u32[]{:S(2)}, u32[]{:S(2)}) %collective-permute-start.48) | collective-permute-done | bytes 786464 | tf_op jit(solution)/shard_map/ppermute | solution.py:346
  520.9 15.7 collective-permute-done.50
  540.1 13.3 collective-permute-done.51
  576.3 25.6 %collective-permute-done.70 = bf16[1024,1024]{1,0:T(8,128)(2,1)S(1)} collective-permute-done((bf16[1024,1024]{1,0:T(8,128)(2,1)S(1)}, bf16[1024,1024]{1,0:T(8,128)(2,1)S(1)}, u32[]{:S(2)}, u32[]{:S(2)}) %collective-permute-start.70) | collective-permute-done | bytes 2097184 | tf_op jit(solution)/shard_map/ppermute | solution.py:341
  604.0 42.9 %collective-permute-done.64 = bf16[2048,512]{1,0:T(8,128)(2,1)S(1)} collective-permute-done((bf16[2048,512]{1,0:T(8,128)(2,1)S(1)}, bf16[2048,512]{1,0:T(8,128)(2,1)S(1)}, u32[]{:S(2)}, u32[]{:S(2)}) %collective-permute-start.64) | collective-permute-done | bytes 2097184 | tf_op jit(solution)/shard_map/ppermute | solution.py:341
  649.3 34.7 %collective-permute-done.58 = bf16[2048,512]{1,0:T(8,128)(2,1)S(1)} collective-permute-done((bf16[2048,512]{1,0:T(8,128)(2,1)S(1)}, bf16[2048,512]{1,0:T(8,128)(2,1)S(1)}, u32[]{:S(2)}, u32[]{:S(2)}) %collective-permute-start.58) | collective-permute-done | bytes 2097184 | tf_op jit(solution)/shard_map/ppermute | solution.py:341
  741.9 15.3 multiply_convert_fusion.1
  794.0 14.4 convolution_convert_fusion.4
  808.4 20.4 %fusion.6 = (bf16[2048,1024]{1,0:T(8,128)(2,1)}, bf16[2048,1024]{1,0:T(8,128)(2,1)}) fusion(f32[2048,1024]{1,0:T(8,128)} %fusion.18, f32[2048,1024]{1,0:T(8,128)} %get-tuple-element.359, bf16[2048,2048]{1,0:T(8,128)(2,1)} %bitcast.416, bf16[1024,1024]{1,0:T(8,128)(2,1)S(1)} %copy-done.83, bf16[1024,1024]{1,0:T(8,128)(2,1)S(1)} %copy-done.82), kind=kOutput, calls=%fused_computation.16 | convolution fusion | flops 8627683328 | bytes 37748736 | tf_op jit(solution)/shard_map/dot_general | solution.py:88
  841.8 15.2 fusion.16
  866.4 16.8 %add_convert_fusion = bf16[2048,2048]{1,0:T(8,128)(2,1)} fusion(f32[2048,2048]{1,0:T(8,128)} %fusion.16, bf16[2048,1024]{1,0:T(8,128)(2,1)} %get-tuple-element.118, bf16[2048,512]{1,0:T(8,128)(2,1)} %get-tuple-element.123, bf16[2048,512]{1,0:T(8,128)(2,1)} %get-tuple-element.122), kind=kOutput, calls=%fused_computation.10 | convolution fusion | flops 8606711808 | bytes 33554432 | tf_op jit(solution)/shard_map/dot_general | solution.py:88
  932.0 35.1 %collective-permute-done.146 = bf16[1024,1024]{1,0:T(8,128)(2,1)S(1)} collective-permute-done((bf16[1024,1024]{1,0:T(8,128)(2,1)S(1)}, bf16[1024,1024]{1,0:T(8,128)(2,1)S(1)}, u32[]{:S(2)}, u32[]{:S(2)}) %collective-permute-start.146) | collective-permute-done | bytes 2097184 | tf_op jit(solution)/shard_map/ppermute | solution.py:341
  975.5 36.6 %collective-permute-done.140 = bf16[2048,512]{1,0:T(8,128)(2,1)S(1)} collective-permute-done((bf16[2048,512]{1,0:T(8,128)(2,1)S(1)}, bf16[2048,512]{1,0:T(8,128)(2,1)S(1)}, u32[]{:S(2)}, u32[]{:S(2)}) %collective-permute-start.140) | collective-permute-done | bytes 2097184 | tf_op jit(solution)/shard_map/ppermute | solution.py:341
  1083.5 30.0 %collective-permute-start.144 = (bf16[1,512,512]{2,1,0:T(8,128)(2,1)}, bf16[1,512,512]{2,1,0:T(8,128)(2,1)S(1)}, u32[]{:S(2)}, u32[]{:S(2)}) collective-permute-start(bf16[1,512,512]{2,1,0:T(8,128)(2,1)} %get-tuple-element.146), channel_id=1, source_target_pairs={{9,0},{25,1},{11,2},{27,3},{13,4},{29,5},{15,6},{31,7},{0,8},{16,9... | collective-permute-start | bytes 1572872 | tf_op jit(solution)/shard_map/ppermute | solution.py:537
  1119.6 47.9 %collective-permute-done.73 = bf16[4,192,2048]{2,1,0:T(8,128)(2,1)S(1)} collective-permute-done((bf16[4,192,2048]{2,1,0:T(8,128)(2,1)S(1)}, bf16[4,192,2048]{2,1,0:T(8,128)(2,1)S(1)}, u32[]{:S(2)}, u32[]{:S(2)}) %collective-permute-start.73) | collective-permute-done | bytes 3145760 | tf_op jit(solution)/shard_map/ppermute | solution.py:341
  1170.9 17.5 %collective-permute-done.87 = bf16[192,2048]{1,0:T(8,128)(2,1)S(1)} collective-permute-done((bf16[192,2048]{1,0:T(8,128)(2,1)S(1)}, bf16[192,2048]{1,0:T(8,128)(2,1)S(1)}, u32[]{:S(2)}, u32[]{:S(2)}) %collective-permute-start.87) | collective-permute-done | bytes 786464 | tf_op jit(solution)/shard_map/ppermute | solution.py:346
  1193.6 15.3 collective-permute-done.74
  1209.4 21.5 %collective-permute-done.88 = bf16[192,2048]{1,0:T(8,128)(2,1)S(1)} collective-permute-done((bf16[192,2048]{1,0:T(8,128)(2,1)S(1)}, bf16[192,2048]{1,0:T(8,128)(2,1)S(1)}, u32[]{:S(2)}, u32[]{:S(2)}) %collective-permute-start.88) | collective-permute-done | bytes 786464 | tf_op jit(solution)/shard_map/ppermute | solution.py:346
  1238.2 28.5 %collective-permute-done.75 = bf16[192,2048]{1,0:T(8,128)(2,1)S(1)} collective-permute-done((bf16[192,2048]{1,0:T(8,128)(2,1)S(1)}, bf16[192,2048]{1,0:T(8,128)(2,1)S(1)}, u32[]{:S(2)}, u32[]{:S(2)}) %collective-permute-start.75) | collective-permute-done | bytes 786464 | tf_op jit(solution)/shard_map/ppermute | solution.py:346
  1269.2 17.8 %collective-permute-done.89 = bf16[192,2048]{1,0:T(8,128)(2,1)S(1)} collective-permute-done((bf16[192,2048]{1,0:T(8,128)(2,1)S(1)}, bf16[192,2048]{1,0:T(8,128)(2,1)S(1)}, u32[]{:S(2)}, u32[]{:S(2)}) %collective-permute-start.89) | collective-permute-done | bytes 786464 | tf_op jit(solution)/shard_map/ppermute | solution.py:346
  1445.9 18.9 %collective-permute-done.114 = bf16[512,1024]{1,0:T(8,128)(2,1)S(1)} collective-permute-done((bf16[512,1024]{1,0:T(8,128)(2,1)S(1)}, bf16[512,1024]{1,0:T(8,128)(2,1)S(1)}, u32[]{:S(2)}, u32[]{:S(2)}) %collective-permute-start.114) | collective-permute-done | bytes 1048608 | tf_op jit(solution)/shard_map/ppermute | solution.py:341
  1467.8 19.5 %collective-permute-done.106 = bf16[512,1024]{1,0:T(8,128)(2,1)S(1)} collective-permute-done((bf16[512,1024]{1,0:T(8,128)(2,1)S(1)}, bf16[512,1024]{1,0:T(8,128)(2,1)S(1)}, u32[]{:S(2)}, u32[]{:S(2)}) %collective-permute-start.106) | collective-permute-done | bytes 1048608 | tf_op jit(solution)/shard_map/ppermute | solution.py:341
  1490.8 18.9 %collective-permute-done.98 = bf16[512,1024]{1,0:T(8,128)(2,1)S(1)} collective-permute-done((bf16[512,1024]{1,0:T(8,128)(2,1)S(1)}, bf16[512,1024]{1,0:T(8,128)(2,1)S(1)}, u32[]{:S(2)}, u32[]{:S(2)}) %collective-permute-start.98) | collective-permute-done | bytes 1048608 | tf_op jit(solution)/shard_map/ppermute | solution.py:341
  (984 shorter events, 856.0 us)
Async XLA Ops:
  0.7 63.2 %collective-permute-start.6 = (bf16[64,2048]{1,0:T(8,128)(2,1)}, bf16[64,2048]{1,0:T(8,128)(2,1)}, u32[]{:S(2)}, u32[]{:S(2)}) collective-permute-start(bf16[64,2048]{1,0:T(8,128)(2,1)} %param.22), channel_id=1, source_target_pairs={{0,8},{8,16},{16,24},{24,0},{1,9},{9,17},{17,25},{25,1},{2,10},{10... | collective-permute-start | bytes 786440 | tf_op jit(solution)/shard_map/ppermute | solution.py:346
  9.3 61.9 %collective-permute-start.22 = (bf16[64,2048]{1,0:T(8,128)(2,1)}, bf16[64,2048]{1,0:T(8,128)(2,1)}, u32[]{:S(2)}, u32[]{:S(2)}) collective-permute-start(bf16[64,2048]{1,0:T(8,128)(2,1)} %param.21), channel_id=1, source_target_pairs={{0,8},{8,16},{16,24},{24,0},{1,9},{9,17},{17,25},{25,1},{2,10},{10... | collective-permute-start | bytes 786440 | tf_op jit(solution)/shard_map/ppermute | solution.py:346
  10.9 64.2 %collective-permute-start.14 = (bf16[64,2048]{1,0:T(8,128)(2,1)}, bf16[64,2048]{1,0:T(8,128)(2,1)}, u32[]{:S(2)}, u32[]{:S(2)}) collective-permute-start(bf16[64,2048]{1,0:T(8,128)(2,1)} %param.20), channel_id=1, source_target_pairs={{0,8},{8,16},{16,24},{24,0},{1,9},{9,17},{17,25},{25,1},{2,10},{10... | collective-permute-start | bytes 786440 | tf_op jit(solution)/shard_map/ppermute | solution.py:346
  63.1 182.2 %collective-permute-start.77 = (bf16[192,2048]{1,0:T(8,128)(2,1)S(1)}, bf16[192,2048]{1,0:T(8,128)(2,1)}, u32[]{:S(2)}, u32[]{:S(2)}) collective-permute-start(bf16[192,2048]{1,0:T(8,128)(2,1)S(1)} %copy-done.66), channel_id=1, source_target_pairs={{0,8},{8,16},{16,24},{24,0},{1,9},{9,17},{17,25},{25,1},{2,10},{10... | collective-permute-start | bytes 2359304 | tf_op jit(solution)/shard_map/ppermute | solution.py:346
  71.2 64.6 %collective-permute-start.67 = (bf16[1,256,1024]{2,1,0:T(8,128)(2,1)}, bf16[1,256,1024]{2,1,0:T(8,128)(2,1)}, u32[]{:S(2)}, u32[]{:S(2)}) collective-permute-start(bf16[1,256,1024]{2,1,0:T(8,128)(2,1)} %get-tuple-element.155), channel_id=1, source_target_pairs={{0,1},{1,17},{2,3},{3,19},{4,5},{5,21},{6,7},{7,23},{8,8},{9,24},{... | collective-permute-start | bytes 1572872 | tf_op jit(solution)/shard_map/ppermute | solution.py:508
  92.5 69.4 %collective-permute-start.68 = (bf16[1,256,1024]{2,1,0:T(8,128)(2,1)S(1)}, bf16[1,256,1024]{2,1,0:T(8,128)(2,1)S(1)}, u32[]{:S(2)}, u32[]{:S(2)}) collective-permute-start(bf16[1,256,1024]{2,1,0:T(8,128)(2,1)S(1)} %copy-done.103), channel_id=1, source_target_pairs={{0,8},{1,24},{2,10},{3,26},{4,12},{5,28},{6,14},{7,30},{8,9},{9,25... | collective-permute-start | bytes 1572872 | tf_op jit(solution)/shard_map/ppermute | solution.py:508
  269.5 80.5 %collective-permute-start.78 = (bf16[192,2048]{1,0:T(8,128)(2,1)}, bf16[192,2048]{1,0:T(8,128)(2,1)S(1)}, u32[]{:S(2)}, u32[]{:S(2)}) collective-permute-start(bf16[192,2048]{1,0:T(8,128)(2,1)} %collective-permute-done.77), channel_id=1, source_target_pairs={{0,8},{8,16},{16,24},{24,0},{1,9},{9,17},{17,25},{25,1},{2,10},{10... | collective-permute-start | bytes 2359304 | tf_op jit(solution)/shard_map/ppermute | solution.py:346
  290.0 81.6 %collective-permute-start.10 = (bf16[512,1024]{1,0:T(8,128)(2,1)S(1)}, bf16[512,1024]{1,0:T(8,128)(2,1)S(1)}, u32[]{:S(2)}, u32[]{:S(2)}) collective-permute-start(bf16[512,1024]{1,0:T(8,128)(2,1)S(1)} %get-tuple-element.209), channel_id=1, source_target_pairs={{0,4},{1,5},{2,6},{3,7},{4,0},{5,1},{6,2},{7,3},{8,12},{9,13},{10,... | collective-permute-start | bytes 3145736 | tf_op jit(solution)/shard_map/ppermute | solution.py:341
  336.4 77.7 %collective-permute-start.29 = (bf16[1024,2048]{1,0:T(8,128)(2,1)S(1)}, bf16[1024,2048]{1,0:T(8,128)(2,1)S(1)}, u32[]{:S(2)}, u32[]{:S(2)}) collective-permute-start(bf16[1024,2048]{1,0:T(8,128)(2,1)S(1)} %pad_maximum_fusion.2), channel_id=1, source_target_pairs={{0,1},{1,0},{2,3},{3,2},{4,5},{5,4},{6,7},{7,6},{8,9},{9,8},{10,11... | collective-permute-start | bytes 12582920 | tf_op jit(solution)/shard_map/ppermute | solution.py:341
  350.0 71.9 %collective-permute-start.21 = (bf16[1024,2048]{1,0:T(8,128)(2,1)}, bf16[1024,2048]{1,0:T(8,128)(2,1)}, u32[]{:S(2)}, u32[]{:S(2)}) collective-permute-start(bf16[1024,2048]{1,0:T(8,128)(2,1)} %pad_maximum_fusion.1), channel_id=1, source_target_pairs={{0,1},{1,0},{2,3},{3,2},{4,5},{5,4},{6,7},{7,6},{8,9},{9,8},{10,11... | collective-permute-start | bytes 12582920 | tf_op jit(solution)/shard_map/ppermute | solution.py:341
  368.3 170.4 %collective-permute-start.41 = (s32[192,8]{0,1:T(8,128)}, s32[192,8]{0,1:T(8,128)}, u32[]{:S(2)}, u32[]{:S(2)}) collective-permute-start(s32[192,8]{0,1:T(8,128)} %param.19), channel_id=1, source_target_pairs={{0,2},{1,3},{2,0},{3,1},{4,6},{5,7},{6,4},{7,5},{8,10},{9,11},{10,... | collective-permute-start | bytes 18440 | tf_op jit(solution)/shard_map/ppermute | solution.py:341
  410.2 159.6 %collective-permute-start.56 = (bf16[1,512,512]{2,1,0:T(8,128)(2,1)}, bf16[1,512,512]{2,1,0:T(8,128)(2,1)}, u32[]{:S(2)}, u32[]{:S(2)}) collective-permute-start(bf16[1,512,512]{2,1,0:T(8,128)(2,1)} %get-tuple-element.161), channel_id=1, source_target_pairs={{0,8},{1,24},{2,10},{3,26},{4,12},{5,28},{6,14},{7,30},{8,9},{9,25... | collective-permute-start | bytes 1572872 | tf_op jit(solution)/shard_map/ppermute | solution.py:508
  457.3 81.4 %collective-permute-start.42 = (s32[192,8]{0,1:T(8,128)S(1)}, s32[192,8]{0,1:T(8,128)S(1)}, u32[]{:S(2)}, u32[]{:S(2)}) collective-permute-start(s32[192,8]{0,1:T(8,128)S(1)} %copy-done.159), channel_id=1, source_target_pairs={{0,2},{1,3},{2,0},{3,1},{4,6},{5,7},{6,4},{7,5},{8,10},{9,11},{10,... | collective-permute-start | bytes 18440 | tf_op jit(solution)/shard_map/ppermute | solution.py:341
  566.9 80.0 %collective-permute-start.64 = (bf16[2048,512]{1,0:T(8,128)(2,1)S(1)}, bf16[2048,512]{1,0:T(8,128)(2,1)S(1)}, u32[]{:S(2)}, u32[]{:S(2)}) collective-permute-start(bf16[2048,512]{1,0:T(8,128)(2,1)S(1)} %bitcast.409), channel_id=1, source_target_pairs={{0,4},{1,5},{2,6},{3,7},{4,0},{5,1},{6,2},{7,3},{8,12},{9,13},{10,... | collective-permute-start | bytes 6291464 | tf_op jit(solution)/shard_map/ppermute | solution.py:341
  568.4 132.5 %collective-permute-start.84 = (bf16[8,192,2048]{2,1,0:T(8,128)(2,1)}, bf16[8,192,2048]{2,1,0:T(8,128)(2,1)}, u32[]{:S(2)}, u32[]{:S(2)}) collective-permute-start(bf16[8,192,2048]{2,1,0:T(8,128)(2,1)} %get-tuple-element.175), channel_id=1, source_target_pairs={{0,1},{1,0},{2,3},{3,2},{4,5},{5,4},{6,7},{7,6},{8,9},{9,8},{10,11... | collective-permute-start | bytes 18874376 | tf_op jit(solution)/shard_map/ppermute | solution.py:341
  569.8 137.7 %collective-permute-start.53 = (bf16[8,192,2048]{2,1,0:T(8,128)(2,1)}, bf16[8,192,2048]{2,1,0:T(8,128)(2,1)}, u32[]{:S(2)}, u32[]{:S(2)}) collective-permute-start(bf16[8,192,2048]{2,1,0:T(8,128)(2,1)} %get-tuple-element.191), channel_id=1, source_target_pairs={{0,1},{1,0},{2,3},{3,2},{4,5},{5,4},{6,7},{7,6},{8,9},{9,8},{10,11... | collective-permute-start | bytes 18874376 | tf_op jit(solution)/shard_map/ppermute | solution.py:341
  575.1 108.8 %collective-permute-start.58 = (bf16[2048,512]{1,0:T(8,128)(2,1)S(1)}, bf16[2048,512]{1,0:T(8,128)(2,1)S(1)}, u32[]{:S(2)}, u32[]{:S(2)}) collective-permute-start(bf16[2048,512]{1,0:T(8,128)(2,1)S(1)} %bitcast.407), channel_id=1, source_target_pairs={{0,4},{1,5},{2,6},{3,7},{4,0},{5,1},{6,2},{7,3},{8,12},{9,13},{10,... | collective-permute-start | bytes 6291464 | tf_op jit(solution)/shard_map/ppermute | solution.py:341
  866.4 163.4 %collective-permute-start.72 = (bf16[8,192,2048]{2,1,0:T(8,128)(2,1)}, bf16[8,192,2048]{2,1,0:T(8,128)(2,1)}, u32[]{:S(2)}, u32[]{:S(2)}) collective-permute-start(bf16[8,192,2048]{2,1,0:T(8,128)(2,1)} %slice.730), channel_id=1, source_target_pairs={{0,1},{1,0},{2,3},{3,2},{4,5},{5,4},{6,7},{7,6},{8,9},{9,8},{10,11... | collective-permute-start | bytes 18874376 | tf_op jit(solution)/shard_map/ppermute | solution.py:341
  897.2 123.0 %collective-permute-start.85 = (bf16[8,192,2048]{2,1,0:T(8,128)(2,1)}, bf16[8,192,2048]{2,1,0:T(8,128)(2,1)}, u32[]{:S(2)}, u32[]{:S(2)}) collective-permute-start(bf16[8,192,2048]{2,1,0:T(8,128)(2,1)} %slice.738), channel_id=1, source_target_pairs={{0,1},{1,0},{2,3},{3,2},{4,5},{5,4},{6,7},{7,6},{8,9},{9,8},{10,11... | collective-permute-start | bytes 18874376 | tf_op jit(solution)/shard_map/ppermute | solution.py:341
  924.9 87.1 %collective-permute-start.140 = (bf16[2048,512]{1,0:T(8,128)(2,1)S(1)}, bf16[2048,512]{1,0:T(8,128)(2,1)S(1)}, u32[]{:S(2)}, u32[]{:S(2)}) collective-permute-start(bf16[2048,512]{1,0:T(8,128)(2,1)S(1)} %broadcast_select_fusion.7), channel_id=1, source_target_pairs={{0,4},{1,5},{2,6},{3,7},{4,0},{5,1},{6,2},{7,3},{8,12},{9,13},{10,... | collective-permute-start | bytes 6291464 | tf_op jit(solution)/shard_map/ppermute | solution.py:341
  931.0 124.7 %collective-permute-start.134 = (bf16[2048,512]{1,0:T(8,128)(2,1)}, bf16[2048,512]{1,0:T(8,128)(2,1)}, u32[]{:S(2)}, u32[]{:S(2)}) collective-permute-start(bf16[2048,512]{1,0:T(8,128)(2,1)} %broadcast_select_fusion.8), channel_id=1, source_target_pairs={{0,4},{1,5},{2,6},{3,7},{4,0},{5,1},{6,2},{7,3},{8,12},{9,13},{10,... | collective-permute-start | bytes 6291464 | tf_op jit(solution)/shard_map/ppermute | solution.py:341
  970.1 92.5 %collective-permute-start.147 = (bf16[1,256,1024]{2,1,0:T(8,128)(2,1)}, bf16[1,256,1024]{2,1,0:T(8,128)(2,1)}, u32[]{:S(2)}, u32[]{:S(2)}) collective-permute-start(bf16[1,256,1024]{2,1,0:T(8,128)(2,1)} %get-tuple-element.145), channel_id=1, source_target_pairs={{0,0},{16,1},{2,2},{18,3},{4,4},{20,5},{6,6},{22,7},{1,8},{17,9},{... | collective-permute-start | bytes 1572872 | tf_op jit(solution)/shard_map/ppermute | solution.py:537
  1029.7 84.5 %collective-permute-start.86 = (bf16[4,192,2048]{2,1,0:T(8,128)(2,1)}, bf16[4,192,2048]{2,1,0:T(8,128)(2,1)}, u32[]{:S(2)}, u32[]{:S(2)}) collective-permute-start(bf16[4,192,2048]{2,1,0:T(8,128)(2,1)} %slice.740), channel_id=1, source_target_pairs={{0,2},{1,3},{2,0},{3,1},{4,6},{5,7},{6,4},{7,5},{8,10},{9,11},{10,... | collective-permute-start | bytes 9437192 | tf_op jit(solution)/shard_map/ppermute | solution.py:341
  1055.6 111.9 %collective-permute-start.73 = (bf16[4,192,2048]{2,1,0:T(8,128)(2,1)S(1)}, bf16[4,192,2048]{2,1,0:T(8,128)(2,1)S(1)}, u32[]{:S(2)}, u32[]{:S(2)}) collective-permute-start(bf16[4,192,2048]{2,1,0:T(8,128)(2,1)S(1)} %slice.732), channel_id=1, source_target_pairs={{0,2},{1,3},{2,0},{3,1},{4,6},{5,7},{6,4},{7,5},{8,10},{9,11},{10,... | collective-permute-start | bytes 9437192 | tf_op jit(solution)/shard_map/ppermute | solution.py:341
  1068.3 101.2 %collective-permute-start.142 = (bf16[1,512,512]{2,1,0:T(8,128)(2,1)}, bf16[1,512,512]{2,1,0:T(8,128)(2,1)}, u32[]{:S(2)}, u32[]{:S(2)}) collective-permute-start(bf16[1,512,512]{2,1,0:T(8,128)(2,1)} %get-tuple-element.148), channel_id=1, source_target_pairs={{1,0},{17,1},{3,2},{19,3},{5,4},{21,5},{7,6},{23,7},{8,8},{24,9},{... | collective-permute-start | bytes 1572872 | tf_op jit(solution)/shard_map/ppermute | solution.py:537
  1078.7 113.7 %collective-permute-start.143 = (bf16[1,512,512]{2,1,0:T(8,128)(2,1)}, bf16[1,512,512]{2,1,0:T(8,128)(2,1)}, u32[]{:S(2)}, u32[]{:S(2)}) collective-permute-start(bf16[1,512,512]{2,1,0:T(8,128)(2,1)} %get-tuple-element.147), channel_id=1, source_target_pairs={{8,0},{24,1},{10,2},{26,3},{12,4},{28,5},{14,6},{30,7},{9,8},{25,9... | collective-permute-start | bytes 1572872 | tf_op jit(solution)/shard_map/ppermute | solution.py:537
  1083.5 125.7 %collective-permute-start.144 = (bf16[1,512,512]{2,1,0:T(8,128)(2,1)}, bf16[1,512,512]{2,1,0:T(8,128)(2,1)S(1)}, u32[]{:S(2)}, u32[]{:S(2)}) collective-permute-start(bf16[1,512,512]{2,1,0:T(8,128)(2,1)} %get-tuple-element.146), channel_id=1, source_target_pairs={{9,0},{25,1},{11,2},{27,3},{13,4},{29,5},{15,6},{31,7},{0,8},{16,9... | collective-permute-start | bytes 1572872 | tf_op jit(solution)/shard_map/ppermute | solution.py:537
  1114.2 118.8 %collective-permute-start.135 = (bf16[1,512,512]{2,1,0:T(8,128)(2,1)}, bf16[1,512,512]{2,1,0:T(8,128)(2,1)S(1)}, u32[]{:S(2)}, u32[]{:S(2)}) collective-permute-start(bf16[1,512,512]{2,1,0:T(8,128)(2,1)} %get-tuple-element.153), channel_id=1, source_target_pairs={{0,0},{16,1},{2,2},{18,3},{4,4},{20,5},{6,6},{22,7},{1,8},{17,9},{... | collective-permute-start | bytes 1572872 | tf_op jit(solution)/shard_map/ppermute | solution.py:537
  1188.3 78.7 %collective-permute-start.136 = (bf16[1,512,512]{2,1,0:T(8,128)(2,1)S(1)}, bf16[1,512,512]{2,1,0:T(8,128)(2,1)S(1)}, u32[]{:S(2)}, u32[]{:S(2)}) collective-permute-start(bf16[1,512,512]{2,1,0:T(8,128)(2,1)S(1)} %copy-done.104), channel_id=1, source_target_pairs={{1,0},{17,1},{3,2},{19,3},{5,4},{21,5},{7,6},{23,7},{8,8},{24,9},{... | collective-permute-start | bytes 1572872 | tf_op jit(solution)/shard_map/ppermute | solution.py:537
  1208.9 160.3 %collective-permute-start.137 = (bf16[1,512,512]{2,1,0:T(8,128)(2,1)}, bf16[1,512,512]{2,1,0:T(8,128)(2,1)}, u32[]{:S(2)}, u32[]{:S(2)}) collective-permute-start(bf16[1,512,512]{2,1,0:T(8,128)(2,1)} %get-tuple-element.151), channel_id=1, source_target_pairs={{8,0},{24,1},{10,2},{26,3},{12,4},{28,5},{14,6},{30,7},{9,8},{25,9... | collective-permute-start | bytes 1572872 | tf_op jit(solution)/shard_map/ppermute | solution.py:537
  1230.8 158.0 %collective-permute-start.138 = (bf16[1,512,512]{2,1,0:T(8,128)(2,1)}, bf16[1,512,512]{2,1,0:T(8,128)(2,1)}, u32[]{:S(2)}, u32[]{:S(2)}) collective-permute-start(bf16[1,512,512]{2,1,0:T(8,128)(2,1)} %get-tuple-element.150), channel_id=1, source_target_pairs={{9,0},{25,1},{11,2},{27,3},{13,4},{29,5},{15,6},{31,7},{0,8},{16,9... | collective-permute-start | bytes 1572872 | tf_op jit(solution)/shard_map/ppermute | solution.py:537
  1443.9 65.8 %collective-permute-start.98 = (bf16[512,1024]{1,0:T(8,128)(2,1)S(1)}, bf16[512,1024]{1,0:T(8,128)(2,1)S(1)}, u32[]{:S(2)}, u32[]{:S(2)}) collective-permute-start(bf16[512,1024]{1,0:T(8,128)(2,1)S(1)} %pad_maximum_fusion.13), channel_id=1, source_target_pairs={{0,2},{1,3},{2,0},{3,1},{4,6},{5,7},{6,4},{7,5},{8,10},{9,11},{10,... | collective-permute-start | bytes 3145736 | tf_op jit(solution)/shard_map/ppermute | solution.py:341
  (294 other events, 9392.6 us)

commit v2 on v0

--- a/solution.py
+++ b/solution.py
@@ -1,6 +1,10 @@
+import functools
+
 import jax
 import jax.numpy as jnp
 from jax import lax
+from jax.experimental import pallas as pl
+from jax.experimental.pallas import tpu as pltpu
 from jax.sharding import PartitionSpec as P
 
 D = 2048
@@ -86,7 +90,7 @@
     )
 
 
-def local(
+def by_axes(
     tokens,
     cotangent,
     lengths,
@@ -329,6 +333,828 @@
     )
 
 
+SLOTS = 128
+SMALL = pl.CostEstimate(flops=1, bytes_accessed=1, transcendentals=0)
+
+
+def flip(value, bit):
+    count = lax.axis_size("expert")
+    return lax.ppermute(value, "expert", [(i, i ^ bit) for i in range(count)])
+
+
+def turn(value, step):
+    count = lax.axis_size("dp")
+    return lax.ppermute(value, "dp", [(i, (i + step) % count) for i in range(count)])
+
+
+def order_kernel(to_own, order_ref, v_ref, o_ref):
+    half = 64
+    lanes = v_ref.shape[1] // 2
+    groups = v_ref.shape[1] // 128
+    odd = order_ref[groups] == 1
+    for pair in range(groups // 2):
+        first = pl.ds(pl.multiple_of(order_ref[2 * pair] * 128, 128), 128)
+        second = pl.ds(pl.multiple_of(order_ref[2 * pair + 1] * 128, 128), 128)
+        if to_own:
+            a = v_ref[:, first].astype(jnp.float32)
+            b = v_ref[:, second].astype(jnp.float32)
+            low = jnp.concatenate([a[:, :half], b[:, :half]], axis=1)
+            high = jnp.concatenate([a[:, half:], b[:, half:]], axis=1)
+            o_ref[:, pair * 128 : pair * 128 + 128] = jnp.where(odd, high, low).astype(o_ref.dtype)
+            o_ref[:, lanes + pair * 128 : lanes + pair * 128 + 128] = jnp.where(
+                odd, low, high
+            ).astype(o_ref.dtype)
+        else:
+            low = v_ref[:, pair * 128 : pair * 128 + 128].astype(jnp.float32)
+            high = v_ref[:, lanes + pair * 128 : lanes + pair * 128 + 128].astype(jnp.float32)
+            low, high = jnp.where(odd, high, low), jnp.where(odd, low, high)
+            o_ref[:, first] = jnp.concatenate([low[:, :half], high[:, :half]], axis=1).astype(
+                o_ref.dtype
+            )
+            o_ref[:, second] = jnp.concatenate([low[:, half:], high[:, half:]], axis=1).astype(
+                o_ref.dtype
+            )
+
+
+def reorder(value, order, to_own):
+    return pl.pallas_call(
+        functools.partial(order_kernel, to_own),
+        out_shape=jax.ShapeDtypeStruct(value.shape, value.dtype),
+        in_specs=[
+            pl.BlockSpec(memory_space=pltpu.SMEM),
+            pl.BlockSpec(memory_space=pltpu.VMEM),
+        ],
+        out_specs=pl.BlockSpec(memory_space=pltpu.VMEM),
+        compiler_params=pltpu.CompilerParams(vmem_limit_bytes=16 * 1024 * 1024),
+        cost_estimate=pl.CostEstimate(flops=0, bytes_accessed=4 * value.size, transcendentals=0),
+    )(order, value)
+
+
+def ring_gather(value):
+    pieces = [value]
+    for _ in range(lax.axis_size("dp") - 1):
+        pieces.append(turn(pieces[-1], 1))
+    return pieces
+
+
+def ring_scatter(pieces):
+    total = pieces[-1]
+    for piece in pieces[-2::-1]:
+        total = turn(total, -1).astype(jnp.float32) + piece.astype(jnp.float32)
+        if piece is not pieces[0]:
+            total = total.astype(piece.dtype)
+    return total
+
+
+def side_by_side(pieces, width):
+    return (
+        jnp.concatenate([p[:, :width] for p in pieces], axis=0),
+        jnp.concatenate([p[:, width:] for p in pieces], axis=0),
+    )
+
+
+def by_x(own, far):
+    n = own.shape[0] // 2
+    return jnp.concatenate([own[:n], far[:n], own[n:], far[n:]], axis=0)
+
+
+def ring_scatter_up(pieces):
+    low, wide = pieces[0].dtype, jnp.float32
+    total = pieces[1]
+    for piece in pieces[2:]:
+        total = (turn(total, 1).astype(wide) + piece.astype(wide)).astype(low)
+    return turn(total, 1).astype(wide) + pieces[0].astype(wide)
+
+
+def expert_rounds(count_dp, count_expert):
+    rounds = []
+    for r in range(2):
+        pairs = []
+        for d in range(count_dp):
+            for e in range(count_expert):
+                goal = 2 * (e & 1) + (d // 2 + r) % 2
+                pairs.append((d * count_expert + e, goal * count_expert + (e & ~1) + d % 2))
+        rounds.append(pairs)
+    return rounds
+
+
+def to_owner(weight, place):
+    d, c, x, y = place
+    rounds = expert_rounds(lax.axis_size("dp"), lax.axis_size("expert"))
+    pieces = []
+    for r, pairs in enumerate(rounds):
+        piece = lax.dynamic_index_in_dim(weight, (d // 2 + r) % 2, 0, keepdims=False)
+        pieces.append(lax.ppermute(piece, ("dp", "expert"), pairs))
+    return pieces
+
+
+def to_both(held, far, place):
+    d, c, x, y = place
+    return jnp.where(y == c, held, far), jnp.where(y == c, far, held)
+
+
+def from_owner(keep, got, place):
+    d, c, x, y = place
+    return jnp.where(y == c, keep, got), jnp.where(y == c, got, keep)
+
+
+def to_shards(total, place):
+    d, c, x, y = place
+    rounds = expert_rounds(lax.axis_size("dp"), lax.axis_size("expert"))
+    n = total.shape[0] // 2
+    return [
+        lax.ppermute(total[r * n : (r + 1) * n], ("dp", "expert"), [(b, a) for a, b in pairs])
+        for r, pairs in enumerate(rounds)
+    ]
+
+
+def two_experts(pieces, place):
+    d, c, x, y = place
+    first, second = (p.astype(jnp.float32) for p in pieces)
+    own = d // 2 == 0
+    return jnp.stack([jnp.where(own, first, second), jnp.where(own, second, first)])
+
+
+def contract_kernel(count, *refs):
+    out_ref = refs[-1]
+    out_ref[...] = sum(
+        lax.dot_general(
+            left_ref[...],
+            right_ref[...],
+            (((0,), (0,)), ((), ())),
+            preferred_element_type=jnp.float32,
+        )
+        for left_ref, right_ref in zip(refs[:count], refs[count : 2 * count])
+    ).astype(out_ref.dtype)
+
+
+def contract(lefts, rights, low=jnp.bfloat16):
+    depth, width = lefts[0].shape
+    across = rights[0].shape[1]
+    block = 512
+    return pl.pallas_call(
+        functools.partial(contract_kernel, len(lefts)),
+        grid=(width // block,),
+        in_specs=[pl.BlockSpec((depth, block), lambda i: (0, i))] * len(lefts)
+        + [pl.BlockSpec((depth, across), lambda i: (0, 0))] * len(rights),
+        out_specs=pl.BlockSpec((block, across), lambda i: (i, 0)),
+        out_shape=jax.ShapeDtypeStruct((width, across), low),
+        compiler_params=pltpu.CompilerParams(vmem_limit_bytes=48 * 1024 * 1024),
+        cost_estimate=SMALL,
+    )(*lefts, *rights)
+
+
+def head_norm(v):
+    return lax.rsqrt(jnp.mean(v * v, axis=-1, keepdims=True) + EPS)
+
+
+def dot32(left, right, dims):
+    return lax.dot_general(
+        left, right, ((dims[:1], dims[1:]), ((), ())), preferred_element_type=jnp.float32
+    )
+
+
+def masked_softmax(q, k, same):
+    scores = jnp.where(same, dot32(q, k, (1, 1)) * HD ** (-0.5), -1e30)
+    weights = jnp.exp(scores - jnp.max(scores, axis=-1, keepdims=True))
+    return weights / jnp.sum(weights, axis=-1, keepdims=True)
+
+
+def attend_kernel(
+    order_ref, raw_q, raw_k, v_ref, gain_q, gain_k, cos_ref, sin_ref, seg_c, seg_r, q_ref, k_ref, o_ref
+):
+    low = jnp.bfloat16
+    same = seg_c[...] == seg_r[...]
+    lanes = o_ref.shape[1] // 2
+    groups = lanes // 64
+    odd = order_ref[groups] == 1
+
+    def head(h):
+        cols = pl.ds(pl.multiple_of(h * HD, HD), HD)
+
+        def prepared(raw, gain):
+            v = raw[:, cols]
+            v = v * head_norm(v) * gain[:, cols]
+            return (v * cos_ref[...] + pltpu.roll(v, HD // 2, 1) * sin_ref[...]).astype(low)
+
+        q, k = prepared(raw_q, gain_q), prepared(raw_k, gain_k)
+        q_ref[:, cols], k_ref[:, cols] = q, k
+        probs = masked_softmax(q, k, same).astype(low)
+        return dot32(probs, v_ref[:, cols], (1, 0))
+
+    @pl.loop(0, groups // 2)
+    def _(pair):
+        a, b = head(order_ref[2 * pair]), head(order_ref[2 * pair + 1])
+        first = jnp.concatenate([a[:, :64], b[:, :64]], axis=1)
+        second = jnp.concatenate([a[:, 64:], b[:, 64:]], axis=1)
+        cols = pl.ds(pl.multiple_of(pair * 128, 128), 128)
+        o_ref[:, cols] = jnp.where(odd, second, first).astype(low)
+        cols = pl.ds(pl.multiple_of(lanes + pair * 128, 128), 128)
+        o_ref[:, cols] = jnp.where(odd, first, second).astype(low)
+
+
+def attend_back_kernel(
+    order_ref,
+    grad_ref,
+    q_ref,
+    k_ref,
+    v_ref,
+    raw_q,
+    raw_k,
+    gain_q,
+    gain_k,
+    cos_ref,
+    sin_ref,
+    seg_c,
+    seg_r,
+    d_ref,
+    gq_ref,
+    gk_ref,
+):
+    low, wide = jnp.bfloat16, jnp.float32
+    same = seg_c[...] == seg_r[...]
+    lanes = grad_ref.shape[1] // 2
+    groups = lanes // 64
+    odd = order_ref[groups] == 1
+    scale = HD ** (-0.5)
+
+    def back(grad, raw, gain, at, g_ref, cols):
+        grad = grad * cos_ref[...] + pltpu.roll(grad * sin_ref[...], HD // 2, 1)
+        v = raw[:, cols]
+        r = head_norm(v)
+        g_ref[:, cols] = jnp.sum(grad * v * r, axis=0, keepdims=True)
+        grad = grad * gain[:, cols]
+        d_ref[:, at] = (
+            r * grad - v * (r * r * r) * jnp.mean(grad * v, axis=-1, keepdims=True)
+        ).astype(low)
+
+    def head(h, grad):
+        cols, at_k, at_v = (
+            pl.ds(pl.multiple_of(h * HD + n * 2 * lanes, HD), HD) for n in range(3)
+        )
+        q, k = q_ref[:, cols], k_ref[:, cols]
+        probs = jnp.where(same, masked_softmax(q, k, same), 0.0)
+        grad_probs = dot32(grad, v_ref[:, cols], (1, 1))
+        grad_scores = probs * (grad_probs - jnp.sum(grad_probs * probs, axis=-1, keepdims=True))
+        grad_scores = grad_scores.astype(low)
+        d_ref[:, at_v] = dot32(probs.astype(low), grad, (0, 0)).astype(low)
+        back(dot32(grad_scores, k, (1, 0)) * scale, raw_q, gain_q, cols, gq_ref, cols)
+        back(dot32(grad_scores, q, (0, 0)) * scale, raw_k, gain_k, at_k, gk_ref, cols)
+
+    @pl.loop(0, groups // 2)
+    def _(pair):
+        cols = pl.ds(pl.multiple_of(pair * 128, 128), 128)
+        first = grad_ref[:, cols].astype(wide)
+        cols = pl.ds(pl.multiple_of(lanes + pair * 128, 128), 128)
+        second = grad_ref[:, cols].astype(wide)
+        first, second = jnp.where(odd, second, first), jnp.where(odd, first, second)
+        for n in range(2):
+            part = slice(64 * n, 64 * n + 64)
+            grad = jnp.concatenate([first[:, part], second[:, part]], axis=1).astype(low)
+            head(order_ref[2 * pair + n], grad)
+
+
+def on_chip(kernel, outs, *args):
+    vmem = pl.BlockSpec(memory_space=pltpu.VMEM)
+    return pl.pallas_call(
+        kernel,
+        out_shape=outs,
+        in_specs=[pl.BlockSpec(memory_space=pltpu.SMEM)] + [vmem] * (len(args) - 1),
+        out_specs=[vmem] * len(outs),
+        compiler_params=pltpu.CompilerParams(vmem_limit_bytes=32 * 1024 * 1024),
+        cost_estimate=SMALL,
+    )(*args)
+
+
+def expert_kernel(experts, count, tokens, *refs):
+    low, wide = jnp.bfloat16, jnp.float32
+    place_ref, refs = refs[0], refs[1:]
+    in_refs, refs = refs[:count], refs[count:]
+    gate_refs, up_refs, down_refs, router_ref, refs = refs[:2], refs[2:4], refs[4:6], refs[6], refs[7:]
+    x_ref, hid_ref, dy_ref, da_ref, du_ref, refs = *refs[:5], refs[5:]
+    dh_refs, out_refs, refs = refs[:2], refs[2:4], refs[4:]
+    pair = count // 2
+    pick_ref, turned_ref, c_ref, a_ref, u_ref, y_ref, dx_ref = refs
+    expert = place_ref[0]
+    width = in_refs[0].shape[1]
+    inner = hid_ref.shape[1]
+    name_rows = in_refs[0].shape[0] - 2 * tokens
+    tile = 256
+    deep, flat = width // 4, inner // 4
+
+    def dot(left, right, dims):
+        return lax.dot_general(left, right, ((dims[:1], dims[1:]), ((), ())), preferred_element_type=wide)
+
+    def slice_at(pos, size):
+        return pl.ds(pl.multiple_of(place_ref[1 + pos] * size, size), size)
+
+    before = lax.broadcasted_iota(jnp.int32, (tokens, tokens), 0)
+    upto = lax.broadcasted_iota(jnp.int32, (tokens, tokens), 1)
+    upto = jnp.where(before <= upto, 1.0, 0.0).astype(low)
+    name_row = lax.broadcasted_iota(jnp.int32, (name_rows, tokens), 0)
+    slot = lax.broadcasted_iota(jnp.int32, (SLOTS, tokens), 0)
+    lane = lax.broadcasted_iota(jnp.int32, (SLOTS, 128), 1)
+    gates = []
+    for b in range(count):
+        named = in_refs[b][2 * tokens :, :tokens]
+        own = jnp.sum(jnp.where(name_row == expert, named.astype(wide), 0.0), axis=0, keepdims=True)
+        rank = dot(jnp.broadcast_to(own, (16, tokens)).astype(low), upto, (1, 0))[:1]
+        chosen = (rank.astype(jnp.int32) - 1 == slot) & (own > 0.5)
+        picks = jnp.where(chosen, 1.0, 0.0)
+        turned_ref[b] = picks.T.astype(low)
+        picks = picks.astype(low)
+        rows = pl.ds(b * SLOTS, SLOTS)
+        pick_ref[b] = picks
+        logits = jnp.zeros((SLOTS, 128), wide)
+        for pos in range(4):
+            x = dot(picks, in_refs[b][:tokens, slice_at(pos, deep)], (1, 0)).astype(low)
+            x_ref[rows, pos * deep : (pos + 1) * deep] = x
+            logits += dot(x, router_ref[slice_at(pos, deep), :], (1, 0))
+        c_ref[rows] = dot(picks, in_refs[b][tokens : 2 * tokens], (1, 0)).astype(low)
+        named = jnp.concatenate([named, jnp.zeros((128 - name_rows, tokens), low)], axis=0)
+        named = dot(picks, named, (1, 1)) > 0.5
+        logits = jnp.where(named, logits, -1e30)
+        weights = jnp.exp(logits - jnp.max(logits, axis=1, keepdims=True))
+        total = jnp.sum(weights, axis=1, keepdims=True)
+        gates.append(jnp.sum(jnp.where(lane == expert, weights, 0.0), axis=1, keepdims=True) / total)
+    gate = jnp.concatenate(gates, axis=0)
+
+    @pl.loop(0, 4)
+    def _(pos):
+        cols = slice_at(pos, flat)
+        a, u = (
+            sum(
+                dot(x_ref[:, h * (width // 2) : (h + 1) * (width // 2)], w_refs[h][:, cols], (1, 0))
+                for h in range(2)
+            )
+            for w_refs in (gate_refs, up_refs)
+        )
+        cols = pl.ds(pl.multiple_of(pos * flat, flat), flat)
+        a_ref[:, cols] = a
+        u_ref[:, cols] = u
+        hid_ref[:, cols] = (a / (1.0 + jnp.exp(-a)) * u).astype(low)
+
+    def forward(j, dgate):
+        cols = pl.ds(pl.multiple_of(j * tile, tile), tile)
+        y = sum(
+            dot(hid_ref[:, h * (inner // 2) : (h + 1) * (inner // 2)], down_refs[h][:, cols], (1, 0))
+            for h in range(2)
+        )
+        y = y.astype(low).astype(wide)
+        c = c_ref[:, cols].astype(wide)
+        y_ref[...] = (gate * y).astype(low)
+        dy_ref[:, cols] = (gate * c).astype(low)
+        for b in range(count):
+            out_refs[b // pair][b % pair, :, cols] = dot(
+                turned_ref[b], y_ref[pl.ds(b * SLOTS, SLOTS)], (1, 0)
+            ).astype(low)
+        return dgate + jnp.sum(c * y, axis=1, keepdims=True)
+
+    dgate = lax.fori_loop(0, width // tile, forward, jnp.zeros((count * SLOTS, 1), wide))
+    for b in range(count):
+        rows = dgate[b * SLOTS : (b + 1) * SLOTS]
+        rows = jnp.sum(jnp.where(pick_ref[b].astype(wide) > 0.5, rows, 0.0), axis=0, keepdims=True)
+        rows = jnp.where(name_row == expert, rows, 0.0)
+        high = rows.astype(low)
+        names = pl.ds(tokens, name_rows)
+        dh_ref = dh_refs[b // pair]
+        dh_ref[b % pair, names, :] = jnp.zeros((name_rows, width), low)
+        dh_ref[b % pair, names, :tokens] = high
+        dh_ref[b % pair, names, 2 * tokens : 3 * tokens] = (rows - high.astype(wide)).astype(low)
+
+    for h in range(2):
+
+        @pl.loop(0, 2)
+        def _(r, h=h):
+            dhid = dot(
+                dy_ref[...], down_refs[h][pl.ds(pl.multiple_of(r * flat, flat), flat), :], (1, 1)
+            )
+            pos = 2 * h + r
+            cols = pl.ds(pl.multiple_of(pos * flat, flat), flat)
+            a, u = a_ref[:, cols], u_ref[:, cols]
+            s = 1.0 / (1.0 + jnp.exp(-a))
+            cols = slice_at(pos, flat)
+            da_ref[:, cols] = (dhid * u * (s * (1.0 + a * (1.0 - s)))).astype(low)
+            du_ref[:, cols] = (dhid * (a * s)).astype(low)
+
+    for h in range(2):
+
+        @pl.loop(0, width // (2 * tile))
+        def _(i, h=h):
+            rows = pl.ds(pl.multiple_of(i * tile, tile), tile)
+            dx = dot(da_ref[...], gate_refs[h][rows, :], (1, 1)) + dot(
+                du_ref[...], up_refs[h][rows, :], (1, 1)
+            )
+            dx_ref[...] = dx.astype(low)
+            per = deep // tile
+            start = place_ref[1 + 2 * h + i // per] * deep + (i % per) * tile
+            cols = pl.ds(pl.multiple_of(start, tile), tile)
+            for b in range(count):
+                dh_refs[b // pair][b % pair, :tokens, cols] = dot(
+                    turned_ref[b], dx_ref[pl.ds(b * SLOTS, SLOTS)], (1, 0)
+                ).astype(low)
+
+
+def expert_chunk(place, blocks, tokens, gate_w, up_w, down_w, router_w, experts):
+    low, wide = jnp.bfloat16, jnp.float32
+    count = len(blocks)
+    width = blocks[0].shape[1]
+    inner = gate_w[0].shape[1]
+    rows = count * SLOTS
+    vmem = pl.BlockSpec(memory_space=pltpu.VMEM)
+    outs = [
+        jax.ShapeDtypeStruct((rows, width), low),
+        jax.ShapeDtypeStruct((rows, inner), low),
+        jax.ShapeDtypeStruct((rows, width), low),
+        jax.ShapeDtypeStruct((rows, inner), low),
+        jax.ShapeDtypeStruct((rows, inner), low),
+        *[jax.ShapeDtypeStruct((count // 2, blocks[0].shape[0] - tokens, width), low)] * 2,
+        *[jax.ShapeDtypeStruct((count // 2, tokens, width), low)] * 2,
+    ]
+    return pl.pallas_call(
+        functools.partial(expert_kernel, experts, count, tokens),
+        out_shape=outs,
+        in_specs=[pl.BlockSpec(memory_space=pltpu.SMEM)] + [vmem] * (count + 7),
+        out_specs=[vmem] * len(outs),
+        scratch_shapes=[
+            pltpu.VMEM((count, SLOTS, tokens), low),
+            pltpu.VMEM((count, tokens, SLOTS), low),
+            pltpu.VMEM((rows, width), low),
+            pltpu.VMEM((rows, inner), wide),
+            pltpu.VMEM((rows, inner), wide),
+            pltpu.VMEM((rows, 256), low),
+            pltpu.VMEM((rows, 256), low),
+        ],
+        compiler_params=pltpu.CompilerParams(vmem_limit_bytes=58 * 1024 * 1024),
+        cost_estimate=SMALL,
+    )(place, *blocks, *gate_w, *up_w, *down_w, router_w)
+
+
+def by_links(
+    tokens,
+    cotangent,
+    lengths,
+    routes,
+    w_query,
+    w_key,
+    w_value,
+    w_out,
+    w_router,
+    w_gate,
+    w_up,
+    w_down,
+    g_attn,
+    g_query,
+    g_key,
+    g_ffn,
+):
+    low, wide = jnp.bfloat16, jnp.float32
+    row_count = tokens.shape[0]
+    rows = w_query.shape[0]
+    experts = w_router.shape[1]
+    count_dp = lax.axis_size("dp")
+    score_scale = HD ** (-0.5)
+    d = lax.axis_index("dp")
+    e = lax.axis_index("expert")
+    c, x, y = e & 1, (e >> 1) & 1, e >> 2
+    place = (d, c, x, y)
+    own_expert = 8 * c + 4 * x + d
+    at_owner = jnp.stack(
+        [own_expert] + [2 * ((d + r) % 2) + (c ^ h) for h in range(2) for r in range(2)]
+    ).astype(jnp.int32)
+    group = jnp.arange(16, dtype=jnp.int32)
+    group_order = (
+        ((d - (group & 3)) % count_dp) * 4 + ((((group >> 3) & 1) ^ y) * 2 + (((group >> 2) & 1) ^ x))
+    )
+    order = jnp.concatenate([group_order, c[None]]).astype(jnp.int32)
+    shard = jnp.arange(32, dtype=jnp.int32)
+    to_whole = (
+        (((shard & 1) ^ c) * 16)
+        + (((shard >> 2) & 1) ^ y) * 8
+        + (((shard >> 1) & 1) ^ x) * 4
+        + (d - (shard >> 3)) % count_dp
+    )
+
+    slab = jnp.concatenate(
+        [w_router]
+        + [g[:, None] for g in (g_attn, g_query, g_key, g_ffn)]
+        + [jnp.zeros((rows, 128 - experts - 4), low)],
+        axis=1,
+    )
+    expert_ids = jnp.arange(experts, dtype=jnp.int32)
+    named = jnp.any(routes[:, :, None] == expert_ids, axis=1)
+    names = jnp.zeros((-(-experts // 16) * 16, D), low)
+    names = lax.dynamic_update_slice(names, named.astype(low).T, (0, 0))
+    sync = lax.optimization_barrier
+    width = D + 128
+    vo = jnp.concatenate([w_value, w_out], axis=1)
+    vo_y = flip(vo, 4)
+    qk = ring_gather(jnp.concatenate([w_query, slab, w_key], axis=1))
+    q_a, k_b = side_by_side(qk, width)
+    q_a, k_b, vo, vo_y, w_down = sync((q_a, k_b, vo, vo_y, w_down))
+    vo0 = jnp.concatenate([vo, vo_y], axis=0)
+    q_x, k_y, vo1 = flip(q_a, 2), flip(k_b, 4), turn(vo0, 1)
+    q_a, k_b = jnp.concatenate([q_a, q_x], axis=0), jnp.concatenate([k_b, k_y], axis=0)
+    q_a, k_b, vo1, w_down = sync((q_a, k_b, vo1, w_down))
+    q_y, k_x, vo2 = flip(q_a, 4), flip(k_b, 2), turn(vo1, 1)
+    vo3 = turn(vo2, 1)
+    vo = (vo0, vo1, vo2, vo3)
+    v_b, o_b = side_by_side([p[:rows] for p in vo] + [p[rows:] for p in vo], D)
+    q_a, k_b = jnp.concatenate([q_a, q_y], axis=0), by_x(k_b, k_x)
+    q_a, k_b, v_b, o_b, w_down = sync((q_a, k_b, v_b, o_b, w_down))
+    v_x, q_other, k_other = flip(v_b, 2), flip(q_a, 1), flip(k_b, 1)
+    down = to_owner(w_down, place)
+    v_b, held_down = by_x(v_b, v_x), jnp.concatenate(down)
+    v_b, o_b, q_other, k_other, w_gate, w_up, held_down = sync(
+        (v_b, o_b, q_other, k_other, w_gate, w_up, held_down)
+    )
+    o_x, v_other, down_far = flip(o_b, 2), flip(v_b, 1), flip(held_down, 4)
+    gate = to_owner(w_gate, place)
+    o_b, held_gate = by_x(o_b, o_x), jnp.concatenate(gate)
+    o_b, v_b, v_other, q_a, k_b, down_far, held_gate, w_up = sync(
+        (o_b, v_b, v_other, q_a, k_b, down_far, held_gate, w_up)
+    )
+    gate_far, up = flip(held_gate, 4), to_owner(w_up, place)
+    down_own, down_give = to_both(held_down, down_far, place)
+    o_other, down_got = flip(o_b, 1), flip(down_give, 1)
+    o_other, q_a, k_b, v_b = sync((o_other, q_a, k_b, v_b))
+    value_w, out_w = (v_b, v_other), (o_b, o_other)
+    slab = jnp.concatenate([q_a[:, D:], q_other[:, D:]], axis=0)
+    slab = jnp.take(slab.reshape(32, rows, 128), to_whole, axis=0).reshape(D, 128)
+    query_w, key_w = (q_a[:, :D], q_other[:, :D]), (k_b, k_other)
+    router_w = slab[:, :experts]
+    attn_gain, query_gain, key_gain, ffn_gain = (
+        slab[:, experts + i].astype(wide) for i in range(4)
+    )
+    segment, offset = layout(lengths[0], row_count)
+    inputs = tokens.astype(wide)
+    normed_f, norm_attn_pull = jax.vjp(normalize, inputs, attn_gain)
+    normed_attn = reorder(normed_f.astype(low), order, True)
+    half = D // 2
+
+    def times(left, pair):
+        return jnp.dot(left[:, :half], pair[0], preferred_element_type=wide) + jnp.dot(
+            left[:, half:], pair[1], preferred_element_type=wide
+        )
+
+    raw_q = times(normed_attn, query_w)
+    raw_k = times(normed_attn, key_w)
+
+    frequency = THETA ** (-jnp.arange(HD // 2, dtype=wide) / (HD // 2))
+    angles = offset.astype(wide)[:, None] * frequency[None, :]
+    cosine, sine = jnp.cos(angles), jnp.sin(angles)
+    turns = (
+        jnp.concatenate([cosine, cosine], axis=1),
+        jnp.concatenate([-sine, sine], axis=1),
+        segment[:, None],
+        segment[None, :],
+    )
+    head_gains = (query_gain[None], key_gain[None])
+    values = times(normed_attn, value_w).astype(low)
+    like = jax.ShapeDtypeStruct((row_count, D), low)
+    queries, keys_rot, context = on_chip(
+        attend_kernel, [like] * 3, order, raw_q, raw_k, values, *head_gains, *turns
+    )
+    midway = inputs + times(context, out_w)
+    normed2_f, norm_ffn_pull = jax.vjp(normalize, midway, ffn_gain)
+    normed_ffn = normed2_f.astype(low)
+    normed_ffn, gate_far, down_got, *up = sync((normed_ffn, gate_far, down_got, *up))
+    held_up = jnp.concatenate(up)
+    down_w = (down_own, down_got)
+
+    def dense_gates(values, named_here):
+        logits = jnp.dot(values, router_w, preferred_element_type=wide)
+        logits = jnp.where(named_here, logits, -jnp.inf)
+        exp_logits = jnp.exp(logits - jnp.max(logits, axis=-1, keepdims=True))
+        return exp_logits / jnp.sum(exp_logits, axis=-1, keepdims=True)
+
+    router_wide = jnp.pad(router_w, ((0, 0), (0, 128 - experts)))
+
+    def chunk(piece, piece_x, piece_c, piece_xc):
+        return expert_chunk(
+            at_owner,
+            (piece, piece_x, piece_c, piece_xc),
+            row_count,
+            gate_w,
+            up_w,
+            down_w,
+            router_wide,
+            experts,
+        )
+
+    def add(left, right):
+        return (left.astype(wide) + right.astype(wide)).astype(low)
+
+    def both_x(own, far):
+        return add(own[0], far[0]), add(own[1], far[1])
+
+    sent0 = jnp.concatenate([normed_ffn, cotangent, names], axis=0)
+    up_far = flip(held_up, 4)
+    gate_own, gate_give = to_both(held_gate, gate_far, place)
+    gate_got = flip(gate_give, 1)
+    sent1, sent0_x, sent0_c = turn(sent0, 1), flip(sent0, 2), flip(sent0, 1)
+    sent1, sent0_x, sent0_c, up_far, gate_got = sync((sent1, sent0_x, sent0_c, up_far, gate_got))
+    up_own, up_give = to_both(held_up, up_far, place)
+    gate_w, up_w = (gate_own, gate_got), (up_own, flip(up_give, 1))
+    sent2, sent1_x, sent1_c = turn(sent1, 1), flip(sent1, 2), flip(sent1, 1)
+    outs0 = chunk(sent0, sent0_x, sent0_c, flip(sent0_x, 1))
+    sent2, sent1_x, sent1_c, *outs0 = sync((sent2, sent1_x, sent1_c, *outs0))
+    sent3, sent2_x, sent2_c = turn(sent2, 1), flip(sent2, 2), flip(sent2, 1)
+    outs1 = chunk(sent1, sent1_x, sent1_c, flip(sent1_x, 1))
+    sent3, sent2_x, sent2_c, *outs1 = sync((sent3, sent2_x, sent2_c, *outs1))
+    sent3_x, sent3_c = flip(sent3, 2), flip(sent3, 1)
+    outs2 = chunk(sent2, sent2_x, sent2_c, flip(sent2_x, 1))
+    h1_c, m1_c = flip(outs1[6], 1), flip(outs1[8], 1)
+    sent3_x, sent3_c, h1_c, m1_c, *outs2 = sync((sent3_x, sent3_c, h1_c, m1_c, *outs2))
+    outs3 = chunk(sent3, sent3_x, sent3_c, flip(sent3_x, 1))
+    h1, m1 = both_x(outs1[5], h1_c), both_x(outs1[7], m1_c)
+    h1_x, m1_x, h2_c, m2_c = flip(h1[1], 2), flip(m1[1], 2), flip(outs2[6], 1), flip(outs2[8], 1)
+    h1_x, m1_x, h2_c, m2_c, *outs3 = sync((h1_x, m1_x, h2_c, m2_c, *outs3))
+    outs = (outs0, outs1, outs2, outs3)
+    arrived, hidden, grad_produced, grad_gate_low, grad_up_low = ([o[i] for o in outs] for i in range(5))
+    ring, h2 = add(h1[0], h1_x), both_x(outs2[5], h2_c)
+    ring, *h2 = sync((ring, *h2))
+    ring, h2_x = turn(ring, 1), flip(h2[1], 2)
+    h3_c, h0_c, m3_c = flip(outs3[6], 1), flip(outs0[6], 1), flip(outs3[8], 1)
+    h3_c, arrived, grad_gate_low = sync((h3_c, arrived, grad_gate_low))
+    gate_sum = contract(arrived, grad_gate_low)
+    gate_got = flip(gate_sum[D // 2 :], 1)
+    ring, h2_x, h3_c, h0_c, m3_c = sync((ring, h2_x, h3_c, h0_c, m3_c))
+    ring, h3 = add(add(h2[0], h2_x), ring), both_x(outs3[5], h3_c)
+    ring, *h3 = sync((ring, *h3))
+    ring, h3_x, m0_c = turn(ring, 1), flip(h3[1], 2), flip(outs0[8], 1)
+    gate_keep, gate_give = from_owner(gate_sum[: D // 2], gate_got, place)
+    gate_give, arrived, grad_up_low = sync((gate_give, arrived, grad_up_low))
+    gate_far = flip(gate_give, 4)
+    up_sum = contract(arrived, grad_up_low)
+    up_got = flip(up_sum[D // 2 :], 1)
+    m1 = add(m1[0], m1_x)
+    ring, h3_x, m0_c, m1 = sync((ring, h3_x, m0_c, m1))
+    ring, h0 = add(add(h3[0], h3_x), ring), both_x(outs0[5], h0_c)
+    ring, *h0 = sync((ring, *h0))
+    ring, h0_x, m_ring = turn(ring, 1), flip(h0[1], 2), turn(m1, 1)
+    up_got, hidden, grad_produced = sync((up_got, hidden, grad_produced))
+    down_sum = contract(hidden, grad_produced)
+    up_keep, up_give = from_owner(up_sum[: D // 2], up_got, place)
+    ms = [both_x(o[7], t) for o, t in ((outs2, m2_c), (outs3, m3_c), (outs0, m0_c))]
+    m_far = jnp.concatenate([t[1] for t in ms], axis=0)
+    ring, h0_x, m_ring, down_sum, up_keep, up_give, gate_far, m_far = sync(
+        (ring, h0_x, m_ring, down_sum, up_keep, up_give, gate_far, m_far)
+    )
+    n = down_sum.shape[0] // 2
+    gate_sum = sync((add(gate_keep, gate_far), m_far))[0]
+    up_far, gate_back, m_x = flip(up_give, 4), to_shards(gate_sum, place), flip(m_far, 2)
+    down_got = flip(down_sum[n:], 1)
+    down_got, ring = sync((down_got, ring))
+    back = h0[0].astype(wide) + h0_x.astype(wide) + ring.astype(wide)
+    grad_normed_ffn = back[:row_count]
+    grad_gates = back[row_count : row_count + experts]
+    grad_gates = (grad_gates[:, :row_count] + grad_gates[:, 2 * row_count : 3 * row_count]).T
+
+    grad_out = cotangent.astype(wide)
+    gates = dense_gates(normed_ffn, named)
+    grad_chosen = gates * (grad_gates - jnp.sum(gates * grad_gates, axis=1, keepdims=True))
+    grad_logits = grad_chosen.astype(low)
+    grad_router_local = contract_rows(grad_logits, normed_ffn)
+    grad_normed_ffn = grad_normed_ffn + times_transposed(grad_logits, router_w)
+    grad_midway_norm, grad_ffn_gain = norm_ffn_pull(grad_normed_ffn)
+    grad_midway = grad_out + grad_midway_norm
+    grad_attn = grad_midway.astype(low)
+
+    def weight_grad(left, right):
+        return contract([left[:, :half]], [right]), contract([left[:, half:]], [right])
+
+    def times_back(left, pair):
+        return jnp.concatenate(
+            [times_transposed(left, pair[0]), times_transposed(left, pair[1])], axis=1
+        )
+
+    out_sums = weight_grad(context, grad_attn)
+    grad_context = times_back(grad_attn, out_w).astype(low)
+    grad_heads, grad_query_gain, grad_key_gain = on_chip(
+        attend_back_kernel,
+        [jax.ShapeDtypeStruct((row_count, 3 * D), low)] + [jax.ShapeDtypeStruct((1, D), wide)] * 2,
+        order,
+        grad_context,
+        queries,
+        keys_rot,
+        values,
+        raw_q,
+        raw_k,
+        *head_gains,
+        *turns,
+    )
+    heads_sums = weight_grad(normed_attn, grad_heads)
+    down_keep, down_give = from_owner(down_sum[:n], down_got, place)
+    out_own = add(out_sums[0], flip(out_sums[1], 1))
+    m_x, up_far, down_keep, down_give, out_own, heads_own, heads_other, *gate_back = sync(
+        (m_x, up_far, down_keep, down_give, out_own, *heads_sums, *gate_back)
+    )
+    grad_gate = two_experts(gate_back, place)
+    m2, m3, m0 = (
+        add(t[0], m_x[k * row_count : (k + 1) * row_count]) for k, t in enumerate(ms)
+    )
+
+    def x_first(own):
+        n = own.shape[0] // 4
+        far = jnp.concatenate([own[n : 2 * n], own[3 * n :]], axis=0)
+        return jnp.concatenate([own[:n], own[2 * n : 3 * n]], axis=0), flip(far, 2)
+
+    def half_to(own, bit):
+        n = own.shape[0] // 2
+        return own[:n], flip(own[n:], bit)
+
+    up_sum = add(up_keep, up_far)
+    up_back, down_far, heads_core = to_shards(up_sum, place), flip(down_give, 4), flip(heads_other, 1)
+    out_own, out_far = x_first(out_own)
+    query_own, key_own, value_own = (
+        add(heads_own[:, k * D : (k + 1) * D], heads_core[:, k * D : (k + 1) * D]) for k in range(3)
+    )
+    down_far, out_far, query_own, key_own, value_own, *up_back = sync(
+        (down_far, out_far, query_own, key_own, value_own, *up_back)
+    )
+    grad_up = two_experts(up_back, place)
+    down_sum = add(down_keep, down_far)
+    query_own, query_far = half_to(query_own, 4)
+    key_own, key_far = x_first(key_own)
+    down_back = to_shards(down_sum, place)
+    down_back[0], grad_heads = sync((down_back[0], grad_heads))
+    grad_normed_attn = sum(
+        times_back(grad_heads[:, k * D : (k + 1) * D], w)
+        for k, w in enumerate((query_w, key_w, value_w))
+    )
+    grad_normed_attn = reorder(grad_normed_attn, order, False)
+    grad_inputs_norm, grad_attn_gain = norm_attn_pull(grad_normed_attn)
+    grad_tokens = (grad_midway + grad_inputs_norm).astype(low)
+    small = jnp.concatenate(
+        [grad_router_local, grad_attn_gain[None], grad_query_gain, grad_key_gain, grad_ffn_gain[None]]
+        + [jnp.zeros((-(experts + 4) % 8, D), wide)],
+        axis=0,
+    )
+    small = reorder(small, order, True)
+    query_far, key_far, small, down_back[1], m_ring = sync(
+        (query_far, key_far, small, down_back[1], m_ring)
+    )
+    grad_down = two_experts(down_back, place)
+
+    def fold(value, bit):
+        n = value.shape[1] // 2
+        return value[:, :n] + flip(value[:, n:], bit)
+
+    ring = turn(add(m2, m_ring), 1)
+    ring = turn(add(m3, ring), 1)
+    ko_own, ko_far = half_to(
+        jnp.concatenate([add(key_own, key_far), add(out_own, out_far)], axis=1), 4
+    )
+    value_own, value_far = x_first(value_own)
+    small = fold(fold(small, 1), 4)
+    ring, ko_far, value_far, small = sync((ring, ko_far, value_far, small))
+    block_out = (midway + m0.astype(wide) + ring.astype(wide)).astype(low)
+
+    def to_owners(pieces):
+        return [turn(p, -k) for k, p in enumerate(pieces) if k]
+
+    def summed(pieces):
+        return sum(p.astype(wide) for p in pieces)
+
+    def by_steps(both):
+        return [both[i * rows : (i + 1) * rows] for i in range(count_dp)]
+
+    ko = by_steps(add(ko_own, ko_far))
+    ko_far = to_owners(ko)
+    query_own, query_far = half_to(add(query_own, query_far), 2)
+    value_own, value_far = half_to(add(value_own, value_far), 4)
+    small = fold(small, 2)
+    query_far, value_far, small, *ko_far = sync((query_far, value_far, small, *ko_far))
+    n = small.shape[0]
+    small = small.reshape(n, count_dp, rows).transpose(1, 2, 0).reshape(count_dp * rows, n)
+    small = jnp.pad(small.astype(low), ((0, 0), (0, 128 - n)))
+    qv = by_steps(
+        jnp.concatenate([add(query_own, query_far), add(value_own, value_far), small], axis=1)
+    )
+    qv_ring = summed(qv[:1] + to_owners(qv))
+    ko_ring = summed(ko[:1] + ko_far)
+    grad_key, grad_outproj = ko_ring[:, :D], ko_ring[:, D:]
+    grad_query, grad_value = qv_ring[:, :D], qv_ring[:, D : 2 * D]
+    small = qv_ring[:, 2 * D :]
+    return (
+        block_out,
+        grad_tokens,
+        grad_query,
+        grad_key,
+        grad_value,
+        grad_outproj,
+        small[:, :experts],
+        grad_gate,
+        grad_up,
+        grad_down,
+        small[:, experts],
+        small[:, experts + 1],
+        small[:, experts + 2],
+        small[:, experts + 3],
+    )
+
+
 def solution(mesh):
     in_specs = (
         P(("dp", "expert"), None),
@@ -364,4 +1190,5 @@
         P(("dp", "expert")),
         P(("dp", "expert")),
     )
+    local = by_links if (mesh.shape["dp"], mesh.shape["expert"]) == (4, 8) else by_axes
     return jax.shard_map(local, mesh=mesh, in_specs=in_specs, out_specs=out_specs, check_vma=False)

time: 2700 us -> 1030 us (0.38)
  waiting for transfers between devices: 2010 us -> 403 us
  Pallas kernels: 0 us -> 239 us
  blocking collectives: 219 us -> 0 us
  matrix products: 229 us -> 51.3 us
  starting transfers between devices: 16.1 us -> 123 us
  local copies, waits for them, and re-layouts: 153 us -> 67.3 us
  other arithmetic: 58.5 us -> 131 us
    reduce_scatter x7 -> x0, waiting for transfers between devices: 1380 us -> none  [the longest x1 284 us: local(): lax.psum_scatter(grad_gate_local, 'dp', scatter_dimension=1, tiled=True)]
    ppermute x0 -> x94, waiting for transfers between devices: none -> 403 us  [the longest x21 213 us: turn(): lax.ppermute(value, 'dp', [(i, (i + step) % count) for i in range(count)])]
    all_gather x7 -> x0, waiting for transfers between devices: 382 us -> none  [the longest x1 134 us: local(): lax.all_gather(w_down, 'dp', axis=1, tiled=True)]
    all_to_all x3 -> x0, waiting for transfers between devices: 243 us -> none  [the longest x1 88.4 us: local(): lax.all_to_all(produced.reshape(1, local_experts, owners * capacity, D),...]
    pallas_call x0 -> x16, Pallas kernels: none -> 239 us  [the longest x4 152 us: expert_chunk(): pl.pallas_call(functools.partial(expert_kernel, experts, count, tokens),...]
    dot_general x20 -> x9, matrix products: 170 us -> 23.1 us  [the longest x4 11.8 us: times(): jnp.dot(left[:, half:], pair[1], preferred_element_type=wide)]
    ppermute x0 -> x94, starting transfers between devices: none -> 123 us  [the longest x61 51.6 us: flip(): return lax.ppermute(value, 'expert', [(i, i ^ bit) for i in range(count)])]
    all_to_all x1 -> x0, blocking collectives: 93.1 us -> none  [local(): lax.all_to_all(grad_arrival, 'expert', split_axis=2, concat_axis=0, tiled...]
  transfers between devices with their start and end apart: 18 -> 94, of which waited for: 15 -> 31; matrix products, arithmetic and copies ran while one was open for 12% -> 20% of each run, Pallas kernels for 0% -> 23%
where the time goes in v2:
time: 1030 us; the launch traced here: 1020 us
  waiting for transfers between devices  403 us (39%)
  Pallas kernels  239 us (23%)
  other arithmetic  131 us (13%)
  starting transfers between devices  123 us (12%)
  local copies, waits for them, and re-layouts  67.3 us (7%)
  matrix products  51.3 us (5%)
    ppermute x21, waiting for transfers between devices, turn(): lax.ppermute(value, 'dp', [(i, (i + step) % count) for i in range(count)])  213 us
    pallas_call x4, Pallas kernels, expert_chunk(): pl.pallas_call(functools.partial(expert_kernel, experts, count, tokens),...  152 us
    ppermute x61, waiting for transfers between devices, flip(): return lax.ppermute(value, 'expert', [(i, i ^ bit) for i in range(count)])  97.6 us
    ppermute x6, waiting for transfers between devices, to_owner(): pieces.append(lax.ppermute(piece, ('dp', 'expert'), pairs))  84.8 us
    convert_element_type x26, other arithmetic, add(): return (left.astype(wide) + right.astype(wide)).astype(low)  71.1 us
    pallas_call x7, Pallas kernels, contract(): pl.pallas_call(functools.partial(contract_kernel, len(lefts)), grid=(widt...  55 us
    ppermute x61, starting transfers between devices, flip(): return lax.ppermute(value, 'expert', [(i, i ^ bit) for i in range(count)])  51.6 us
    ppermute x6, starting transfers between devices, to_shards(): lax.ppermute(total[r * n:(r + 1) * n], ('dp', 'expert'), [(b, a) for a, b...  31.9 us
  transfers between devices with their start and end apart: 94, of which 31 were waited for; matrix products, arithmetic and copies ran while one was open for 20% of the time, Pallas kernels for 23%

profile of v2, /device:TPU:0, one launch (start us, length us, event | category | flops | bytes accessed | tf_op | source)
XLA Modules:
  0.0 1017.0 jit_solution(731102606406667808)
XLA Ops:
  8.8 14.3 %collective-permute-done = bf16[64,4224]{1,0:T(8,128)(2,1)S(1)} collective-permute-done((bf16[64,4224]{1,0:T(8,128)(2,1)S(1)}, bf16[64,4224]{1,0:T(8,128)(2,1)S(1)}, u32[]{:S(2)}, u32[]{:S(2)}) %collective-permute-start) | collective-permute-done | bytes 540704 | tf_op jit(solution)/shard_map/ppermute | solution.py:347
  23.1 15.3 %collective-permute-done.1 = bf16[64,4224]{1,0:T(8,128)(2,1)S(1)} collective-permute-done((bf16[64,4224]{1,0:T(8,128)(2,1)S(1)}, bf16[64,4224]{1,0:T(8,128)(2,1)S(1)}, u32[]{:S(2)}, u32[]{:S(2)}) %collective-permute-start.1) | collective-permute-done | bytes 540704 | tf_op jit(solution)/shard_map/ppermute | solution.py:347
  42.7 10.0 collective-permute-done.2
  55.7 19.8 %collective-permute-done.5 = bf16[256,2048]{1,0:T(8,128)(2,1)S(1)} collective-permute-done((bf16[256,2048]{1,0:T(8,128)(2,1)S(1)}, bf16[256,2048]{1,0:T(8,128)(2,1)S(1)}, u32[]{:S(2)}, u32[]{:S(2)}) %collective-permute-start.5) | collective-permute-done | bytes 1048608 | tf_op jit(solution)/shard_map/ppermute | solution.py:342
  82.0 21.3 %collective-permute-done.9 = bf16[128,4096]{1,0:T(8,128)(2,1)S(1)} collective-permute-done((bf16[128,4096]{1,0:T(8,128)(2,1)S(1)}, bf16[128,4096]{1,0:T(8,128)(2,1)S(1)}, u32[]{:S(2)}, u32[]{:S(2)}) %collective-permute-start.9) | collective-permute-done | bytes 1048608 | tf_op jit(solution)/shard_map/ppermute | solution.py:347
  105.1 17.4 %collective-permute-done.8 = bf16[512,2048]{1,0:T(8,128)(2,1)S(1)} collective-permute-done((bf16[512,2048]{1,0:T(8,128)(2,1)S(1)}, bf16[512,2048]{1,0:T(8,128)(2,1)S(1)}, u32[]{:S(2)}, u32[]{:S(2)}) %collective-permute-start.8) | collective-permute-done | bytes 2097184 | tf_op jit(solution)/shard_map/ppermute | solution.py:342
  140.6 43.2 %collective-permute-done.15 = bf16[256,2048]{1,0:T(8,128)(2,1)S(1)} collective-permute-done((bf16[256,2048]{1,0:T(8,128)(2,1)S(1)}, bf16[256,2048]{1,0:T(8,128)(2,1)S(1)}, u32[]{:S(2)}, u32[]{:S(2)}) %collective-permute-start.15) | collective-permute-done | bytes 1048608 | tf_op jit(solution)/shard_map/ppermute | solution.py:447
  194.3 41.6 %collective-permute-done.20 = bf16[512,1024]{1,0:T(8,128)(2,1)S(1)} collective-permute-done((bf16[512,1024]{1,0:T(8,128)(2,1)S(1)}, bf16[512,1024]{1,0:T(8,128)(2,1)S(1)}, u32[]{:S(2)}, u32[]{:S(2)}) %collective-permute-start.20) | collective-permute-done | bytes 1048608 | tf_op jit(solution)/shard_map/ppermute | solution.py:447
  250.3 9.6 collective-permute-start.24
  282.2 13.9 %shard_map.264 = (bf16[192,2048]{1,0:T(8,128)(2,1)S(1)}, bf16[192,2048]{1,0:T(8,128)(2,1)S(1)}, bf16[192,2048]{1,0:T(8,128)(2,1)S(1)}) custom-call(s32[17]{0:T(128)S(1)} %pad_add_fusion.order_ref, f32[192,2048]{1,0:T(8,128)S(1)} %fusion.9.raw_q, f32[192,2048]{1,0:T(8,128)S(1)} %convolution_add_fusion.3.raw_k, bf16[192,2048]{1,0:T(8,128)(2,1)S(1)} %fusion.12.v_ref, ...), custom_call_target="tpu_custom_call" | custom-call | flops 1 | bytes 1 | tf_op jit(solution)/shard_map/pallas_call | solution.py:619
  315.6 37.2 %collective-permute-done.26.refs_1_ = bf16[400,2048]{1,0:T(8,128)(2,1)} collective-permute-done((bf16[400,2048]{1,0:T(8,128)(2,1)S(1)}, bf16[400,2048]{1,0:T(8,128)(2,1)}, u32[]{:S(2)}, u32[]{:S(2)}) %collective-permute-start.26) | collective-permute-done | bytes 1638432 | tf_op jit(solution)/shard_map/ppermute | solution.py:347
  368.8 38.0 %shard_map.265 = (bf16[512,2048]{1,0:T(8,128)(2,1)}, bf16[512,1024]{1,0:T(8,128)(2,1)}, bf16[512,2048]{1,0:T(8,128)(2,1)}, bf16[512,1024]{1,0:T(8,128)(2,1)}, bf...) custom-call(s32[5]{0:T(128)} %stack.50.refs_0_, ...), custom_call_target="tpu_custom_call" | custom-call | flops 1 | bytes 1 | tf_op jit(solution)/shard_map/pallas_call | solution.py:774
  410.7 38.0 %shard_map.266 = (bf16[512,2048]{1,0:T(8,128)(2,1)}, bf16[512,1024]{1,0:T(8,128)(2,1)}, bf16[512,2048]{1,0:T(8,128)(2,1)}, bf16[512,1024]{1,0:T(8,128)(2,1)}, bf...) custom-call(s32[5]{0:T(128)} %stack.50.refs_0_, ...), custom_call_target="tpu_custom_call" | custom-call | flops 1 | bytes 1 | tf_op jit(solution)/shard_map/pallas_call | solution.py:774
  456.3 38.0 %shard_map.267 = (bf16[512,2048]{1,0:T(8,128)(2,1)}, bf16[512,1024]{1,0:T(8,128)(2,1)}, bf16[512,2048]{1,0:T(8,128)(2,1)}, bf16[512,1024]{1,0:T(8,128)(2,1)}, bf...) custom-call(s32[5]{0:T(128)} %stack.50.refs_0_, ...), custom_call_target="tpu_custom_call" | custom-call | flops 1 | bytes 1 | tf_op jit(solution)/shard_map/pallas_call | solution.py:774
  501.0 37.8 %shard_map.268 = (bf16[512,2048]{1,0:T(8,128)(2,1)}, bf16[512,1024]{1,0:T(8,128)(2,1)}, bf16[512,2048]{1,0:T(8,128)(2,1)}, bf16[512,1024]{1,0:T(8,128)(2,1)}, bf...) custom-call(s32[5]{0:T(128)} %stack.50.refs_0_, ...), custom_call_target="tpu_custom_call" | custom-call | flops 1 | bytes 1 | tf_op jit(solution)/shard_map/pallas_call | solution.py:774
  547.8 12.6 %shard_map.269 = bf16[2048,1024]{1,0:T(8,128)(2,1)} custom-call(bf16[512,2048]{1,0:T(8,128)(2,1)} %get-tuple-element.382.refs_0_, bf16[512,2048]{1,0:T(8,128)(2,1)} %get-tuple-element.383.refs_1_, bf16[512,2048]{1,0:T(8,128)(2,1)} %get-tuple-element.384.refs_2_, bf16[512,2048]{1,0:T(8,128)(2,1)} %get-tuple-element.385.refs_3_, ...), custom_call_target="tpu_custom_call" | custom-call | flops 1 | bytes 1 | tf_op jit(solution)/shard_map/pallas_call | solution.py:495
  578.3 12.0 %shard_map.270 = bf16[2048,1024]{1,0:T(8,128)(2,1)} custom-call(bf16[512,2048]{1,0:T(8,128)(2,1)} %get-tuple-element.382.refs_0_, bf16[512,2048]{1,0:T(8,128)(2,1)} %get-tuple-element.383.refs_1_, bf16[512,2048]{1,0:T(8,128)(2,1)} %get-tuple-element.384.refs_2_, bf16[512,2048]{1,0:T(8,128)(2,1)} %get-tuple-element.385.refs_3_, ...), custom_call_target="tpu_custom_call" | custom-call | flops 1 | bytes 1 | tf_op jit(solution)/shard_map/pallas_call | solution.py:495
  606.9 14.2 %shard_map.271 = bf16[1024,2048]{1,0:T(8,128)(2,1)} custom-call(bf16[512,1024]{1,0:T(8,128)(2,1)S(1)} %copy-done.4, bf16[512,1024]{1,0:T(8,128)(2,1)S(1)} %copy-done.5, bf16[512,1024]{1,0:T(8,128)(2,1)S(1)} %copy-done.7, bf16[512,1024]{1,0:T(8,128)(2,1)S(1)} %copy-done.10, bf16[512,2048]{1,0:T(8,128)(2,1)} %get-tuple-element.402.refs_4_, ...), custom_call_target="tpu_custom_call" | custom-call | flops 1 | bytes 1 | tf_op jit(solution)/shard_map/pallas_call | solution.py:495
  625.2 14.3 %collective-permute-done.60 = bf16[192,2048]{1,0:T(8,128)(2,1)} collective-permute-done((bf16[192,2048]{1,0:T(8,128)(2,1)}, bf16[192,2048]{1,0:T(8,128)(2,1)}, u32[]{:S(2)}, u32[]{:S(2)}) %collective-permute-start.60) | collective-permute-done | bytes 786464 | tf_op jit(solution)/shard_map/ppermute | solution.py:347
  659.2 9.5 collective-permute-start.68
  681.2 15.4 %shard_map.274 = (bf16[192,6144]{1,0:T(8,128)(2,1)S(1)}, f32[1,2048]{1,0:T(1,128)S(1)}, f32[1,2048]{1,0:T(1,128)S(1)}) custom-call(s32[17]{0:T(128)S(1)} %pad_add_fusion.order_ref, bf16[192,2048]{1,0:T(8,128)(2,1)S(1)} %pad_maximum_fusion.20.grad_ref, bf16[192,2048]{1,0:T(8,128)(2,1)S(1)} %copy-done.17, bf16[192,2048]{1,0:T(8,128)(2,1)S(1)} %copy-done.19, ...), custom_call_target="tpu_custom_call" | custom-call | flops 1 | bytes 1 | tf_op jit(solution)/shard_map/pallas_call | solution.py:619
  730.5 9.5 collective-permute-start.73
  744.6 12.9 %add_convert_fusion = (bf16[1024,2048]{1,0:T(8,128)(2,1)S(1)}, bf16[1024,2048]{1,0:T(8,128)(2,1)}, bf16[1024,2048]{1,0:T(8,128)(2,1)S(1)}) fusion(bf16[1024,6144]{1,0:T(8,128)(2,1)} %collective-permute-done.72, bf16[1024,6144]{1,0:T(8,128)(2,1)} %shard_map.275), kind=kLoop, calls=%fused_computation.1 | loop fusion | flops 25165824 | bytes 37748736 | tf_op jit(solution)/shard_map/convert_element_type | solution.py:946
  764.1 8.7 collective-permute-done.71
  783.7 12.0 %collective-permute-start.78 = (bf16[256,2048]{1,0:T(8,128)(2,1)}, bf16[256,2048]{1,0:T(8,128)(2,1)}, u32[]{:S(2)}, u32[]{:S(2)}) collective-permute-start(bf16[256,2048]{1,0:T(8,128)(2,1)} %get-tuple-element.561), channel_id=1, source_target_pairs={{8,0},{24,1},{10,2},{26,3},{12,4},{28,5},{14,6},{30,7},{9,8},{25,9... | collective-permute-start | bytes 3145736 | tf_op jit(solution)/shard_map/ppermute | solution.py:466
  832.4 11.3 %collective-permute-done.75 = bf16[512,2048]{1,0:T(8,128)(2,1)} collective-permute-done((bf16[512,2048]{1,0:T(8,128)(2,1)}, bf16[512,2048]{1,0:T(8,128)(2,1)}, u32[]{:S(2)}, u32[]{:S(2)}) %collective-permute-start.75) | collective-permute-done | bytes 2097184 | tf_op jit(solution)/shard_map/ppermute | solution.py:342
  843.7 12.9 %collective-permute-start.83 = (f32[24,1024]{1,0:T(8,128)S(1)}, f32[24,1024]{1,0:T(8,128)S(1)}, u32[]{:S(2)}, u32[]{:S(2)}) collective-permute-start(f32[24,1024]{1,0:T(8,128)S(1)} %slice.604), channel_id=1, source_target_pairs={{0,1},{1,0},{2,3},{3,2},{4,5},{5,4},{6,7},{7,6},{8,9},{9,8},{10,11... | collective-permute-start | bytes 294920 | tf_op jit(solution)/shard_map/ppermute | solution.py:342
  870.2 15.5 %collective-permute-done.79 = bf16[192,2048]{1,0:T(8,128)(2,1)S(1)} collective-permute-done((bf16[192,2048]{1,0:T(8,128)(2,1)S(1)}, bf16[192,2048]{1,0:T(8,128)(2,1)S(1)}, u32[]{:S(2)}, u32[]{:S(2)}) %collective-permute-start.79) | collective-permute-done | bytes 786464 | tf_op jit(solution)/shard_map/ppermute | solution.py:347
  891.3 17.4 %collective-permute-done.84 = f32[24,512]{1,0:T(8,128)S(1)} collective-permute-done((f32[24,512]{1,0:T(8,128)S(1)}, f32[24,512]{1,0:T(8,128)S(1)}, u32[]{:S(2)}, u32[]{:S(2)}) %collective-permute-start.84) | collective-permute-done | bytes 49184 | tf_op jit(solution)/shard_map/ppermute | solution.py:342
  923.9 6.9 collective-permute-done.88
  930.8 31.8 %collective-permute-done.89 = bf16[64,4096]{1,0:T(8,128)(2,1)S(1)} collective-permute-done((bf16[64,4096]{1,0:T(8,128)(2,1)S(1)}, bf16[64,4096]{1,0:T(8,128)(2,1)S(1)}, u32[]{:S(2)}, u32[]{:S(2)}) %collective-permute-start.89) | collective-permute-done | bytes 524320 | tf_op jit(solution)/shard_map/ppermute | solution.py:347
  977.4 36.7 %collective-permute-done.92 = bf16[64,4224]{1,0:T(8,128)(2,1)S(1)} collective-permute-done((bf16[64,4224]{1,0:T(8,128)(2,1)S(1)}, bf16[64,4224]{1,0:T(8,128)(2,1)S(1)}, u32[]{:S(2)}, u32[]{:S(2)}) %collective-permute-start.92) | collective-permute-done | bytes 540704 | tf_op jit(solution)/shard_map/ppermute | solution.py:347
  (563 shorter events, 365.0 us)
Async XLA Ops:
  80.9 50.1 %collective-permute-start.7 = (bf16[512,2176]{1,0:T(8,128)(2,1)S(1)}, bf16[512,2176]{1,0:T(8,128)(2,1)S(1)}, u32[]{:S(2)}, u32[]{:S(2)}) collective-permute-start(bf16[512,2176]{1,0:T(8,128)(2,1)S(1)} %pad_maximum_fusion.8), channel_id=1, source_target_pairs={{0,4},{1,5},{2,6},{3,7},{4,0},{5,1},{6,2},{7,3},{8,12},{9,13},{10,... | collective-permute-start | bytes 6684680 | tf_op jit(solution)/shard_map/ppermute | solution.py:342
  133.3 53.1 %collective-permute-start.12 = (bf16[1024,2176]{1,0:T(8,128)(2,1)}, bf16[1024,2176]{1,0:T(8,128)(2,1)}, u32[]{:S(2)}, u32[]{:S(2)}) collective-permute-start(bf16[1024,2176]{1,0:T(8,128)(2,1)} %pad_maximum_fusion), channel_id=1, source_target_pairs={{0,1},{1,0},{2,3},{3,2},{4,5},{5,4},{6,7},{7,6},{8,9},{9,8},{10,11... | collective-permute-start | bytes 13369352 | tf_op jit(solution)/shard_map/ppermute | solution.py:342
  133.3 53.1 %collective-permute-start.13 = (bf16[1024,2048]{1,0:T(8,128)(2,1)}, bf16[1024,2048]{1,0:T(8,128)(2,1)}, u32[]{:S(2)}, u32[]{:S(2)}) collective-permute-start(bf16[1024,2048]{1,0:T(8,128)(2,1)} %pad_maximum_fusion.1), channel_id=1, source_target_pairs={{0,1},{1,0},{2,3},{3,2},{4,5},{5,4},{6,7},{7,6},{8,9},{9,8},{10,11... | collective-permute-start | bytes 12582920 | tf_op jit(solution)/shard_map/ppermute | solution.py:342
  133.8 50.1 %collective-permute-start.11 = (bf16[512,2048]{1,0:T(8,128)(2,1)}, bf16[512,2048]{1,0:T(8,128)(2,1)}, u32[]{:S(2)}, u32[]{:S(2)}) collective-permute-start(bf16[512,2048]{1,0:T(8,128)(2,1)} %get-tuple-element.247), channel_id=1, source_target_pairs={{0,2},{1,3},{2,0},{3,1},{4,6},{5,7},{6,4},{7,5},{8,10},{9,11},{10,... | collective-permute-start | bytes 6291464 | tf_op jit(solution)/shard_map/ppermute | solution.py:342
  136.2 47.6 %collective-permute-start.15 = (bf16[256,2048]{1,0:T(8,128)(2,1)S(1)}, bf16[256,2048]{1,0:T(8,128)(2,1)S(1)}, u32[]{:S(2)}, u32[]{:S(2)}) collective-permute-start(bf16[256,2048]{1,0:T(8,128)(2,1)S(1)} %get-tuple-element.576), channel_id=1, source_target_pairs={{0,8},{1,24},{2,10},{3,26},{4,12},{5,28},{6,14},{7,30},{8,9},{9,25... | collective-permute-start | bytes 3145736 | tf_op jit(solution)/shard_map/ppermute | solution.py:447
  186.4 53.6 %collective-permute-start.17 = (bf16[1024,2048]{1,0:T(8,128)(2,1)S(1)}, bf16[1024,2048]{1,0:T(8,128)(2,1)S(1)}, u32[]{:S(2)}, u32[]{:S(2)}) collective-permute-start(bf16[1024,2048]{1,0:T(8,128)(2,1)S(1)} %pad_maximum_fusion.2), channel_id=1, source_target_pairs={{0,1},{1,0},{2,3},{3,2},{4,5},{5,4},{6,7},{7,6},{8,9},{9,8},{10,11... | collective-permute-start | bytes 12582920 | tf_op jit(solution)/shard_map/ppermute | solution.py:342
  186.5 50.9 %collective-permute-start.16 = (bf16[512,2048]{1,0:T(8,128)(2,1)}, bf16[512,2048]{1,0:T(8,128)(2,1)S(1)}, u32[]{:S(2)}, u32[]{:S(2)}) collective-permute-start(bf16[512,2048]{1,0:T(8,128)(2,1)} %get-tuple-element.252), channel_id=1, source_target_pairs={{0,2},{1,3},{2,0},{3,1},{4,6},{5,7},{6,4},{7,5},{8,10},{9,11},{10,... | collective-permute-start | bytes 6291464 | tf_op jit(solution)/shard_map/ppermute | solution.py:342
  189.1 46.9 %collective-permute-start.20 = (bf16[512,1024]{1,0:T(8,128)(2,1)S(1)}, bf16[512,1024]{1,0:T(8,128)(2,1)S(1)}, u32[]{:S(2)}, u32[]{:S(2)}) collective-permute-start(bf16[512,1024]{1,0:T(8,128)(2,1)S(1)} %get-tuple-element.570), channel_id=1, source_target_pairs={{0,8},{1,24},{2,10},{3,26},{4,12},{5,28},{6,14},{7,30},{8,9},{9,25... | collective-permute-start | bytes 3145736 | tf_op jit(solution)/shard_map/ppermute | solution.py:447
  191.1 49.0 %collective-permute-start.18 = (bf16[512,2048]{1,0:T(8,128)(2,1)S(1)}, bf16[512,2048]{1,0:T(8,128)(2,1)S(1)}, u32[]{:S(2)}, u32[]{:S(2)}) collective-permute-start(bf16[512,2048]{1,0:T(8,128)(2,1)S(1)} %pad_maximum_fusion.11), channel_id=1, source_target_pairs={{0,4},{1,5},{2,6},{3,7},{4,0},{5,1},{6,2},{7,3},{8,12},{9,13},{10,... | collective-permute-start | bytes 6291464 | tf_op jit(solution)/shard_map/ppermute | solution.py:342
  248.3 56.5 %collective-permute-start.23 = (bf16[512,2048]{1,0:T(8,128)(2,1)}, bf16[512,2048]{1,0:T(8,128)(2,1)}, u32[]{:S(2)}, u32[]{:S(2)}) collective-permute-start(bf16[512,2048]{1,0:T(8,128)(2,1)} %get-tuple-element.538), channel_id=1, source_target_pairs={{0,1},{1,0},{2,3},{3,2},{4,5},{5,4},{6,7},{7,6},{8,9},{9,8},{10,11... | collective-permute-start | bytes 6291464 | tf_op jit(solution)/shard_map/ppermute | solution.py:342
  250.3 54.5 %collective-permute-start.24 = (bf16[512,1024]{1,0:T(8,128)(2,1)}, bf16[512,1024]{1,0:T(8,128)(2,1)}, u32[]{:S(2)}, u32[]{:S(2)}) collective-permute-start(bf16[512,1024]{1,0:T(8,128)(2,1)} %get-tuple-element.568), channel_id=1, source_target_pairs={{0,0},{1,16},{2,2},{3,18},{4,4},{5,20},{6,6},{7,22},{8,1},{9,17},{... | collective-permute-start | bytes 3145736 | tf_op jit(solution)/shard_map/ppermute | solution.py:447
  259.9 44.9 %collective-permute-start.25 = (bf16[512,1024]{1,0:T(8,128)(2,1)}, bf16[512,1024]{1,0:T(8,128)(2,1)}, u32[]{:S(2)}, u32[]{:S(2)}) collective-permute-start(bf16[512,1024]{1,0:T(8,128)(2,1)} %get-tuple-element.567), channel_id=1, source_target_pairs={{0,8},{1,24},{2,10},{3,26},{4,12},{5,28},{6,14},{7,30},{8,9},{9,25... | collective-permute-start | bytes 3145736 | tf_op jit(solution)/shard_map/ppermute | solution.py:447
  260.1 44.7 %collective-permute-start.22 = (bf16[1024,1024]{1,0:T(8,128)(2,1)}, bf16[1024,1024]{1,0:T(8,128)(2,1)}, u32[]{:S(2)}, u32[]{:S(2)}) collective-permute-start(bf16[1024,1024]{1,0:T(8,128)(2,1)} %pad_maximum_fusion.12), channel_id=1, source_target_pairs={{0,4},{1,5},{2,6},{3,7},{4,0},{5,1},{6,2},{7,3},{8,12},{9,13},{10,... | collective-permute-start | bytes 6291464 | tf_op jit(solution)/shard_map/ppermute | solution.py:342
  311.6 48.0 %collective-permute-start.29 = (bf16[1024,1024]{1,0:T(8,128)(2,1)S(1)}, bf16[1024,1024]{1,0:T(8,128)(2,1)S(1)}, u32[]{:S(2)}, u32[]{:S(2)}) collective-permute-start(bf16[1024,1024]{1,0:T(8,128)(2,1)S(1)} %constant_dynamic-update-slice_fusion.2), channel_id=1, source_target_pairs={{0,4},{1,5},{2,6},{3,7},{4,0},{5,1},{6,2},{7,3},{8,12},{9,13},{10,... | collective-permute-start | bytes 6291464 | tf_op jit(solution)/shard_map/ppermute | solution.py:342
  450.0 44.3 %collective-permute-start.42 = (bf16[2,208,2048]{2,1,0:T(8,128)(2,1)}, bf16[2,208,2048]{2,1,0:T(8,128)(2,1)}, u32[]{:S(2)}, u32[]{:S(2)}) collective-permute-start(bf16[2,208,2048]{2,1,0:T(8,128)(2,1)} %get-tuple-element.306), channel_id=1, source_target_pairs={{0,1},{1,0},{2,3},{3,2},{4,5},{5,4},{6,7},{7,6},{8,9},{9,8},{10,11... | collective-permute-start | bytes 5111816 | tf_op jit(solution)/shard_map/ppermute | solution.py:342
  594.4 47.8 %collective-permute-start.63 = (bf16[1024,1024]{1,0:T(8,128)(2,1)}, bf16[1024,1024]{1,0:T(8,128)(2,1)}, u32[]{:S(2)}, u32[]{:S(2)}) collective-permute-start(bf16[1024,1024]{1,0:T(8,128)(2,1)} %broadcast_select_fusion.2), channel_id=1, source_target_pairs={{0,4},{1,5},{2,6},{3,7},{4,0},{5,1},{6,2},{7,3},{8,12},{9,13},{10,... | collective-permute-start | bytes 6291464 | tf_op jit(solution)/shard_map/ppermute | solution.py:342
  653.1 58.1 %collective-permute-start.67 = (bf16[1024,2048]{1,0:T(8,128)(2,1)S(1)}, bf16[1024,2048]{1,0:T(8,128)(2,1)}, u32[]{:S(2)}, u32[]{:S(2)}) collective-permute-start(bf16[1024,2048]{1,0:T(8,128)(2,1)S(1)} %shard_map.273), channel_id=1, source_target_pairs={{0,1},{1,0},{2,3},{3,2},{4,5},{5,4},{6,7},{7,6},{8,9},{9,8},{10,11... | collective-permute-start | bytes 12582920 | tf_op jit(solution)/shard_map/ppermute | solution.py:342
  653.4 64.4 %collective-permute-start.64 = (bf16[576,2048]{1,0:T(8,128)(2,1)}, bf16[576,2048]{1,0:T(8,128)(2,1)}, u32[]{:S(2)}, u32[]{:S(2)}) collective-permute-start(bf16[576,2048]{1,0:T(8,128)(2,1)} %pad_maximum_fusion.7), channel_id=1, source_target_pairs={{0,2},{1,3},{2,0},{3,1},{4,6},{5,7},{6,4},{7,5},{8,10},{9,11},{10,... | collective-permute-start | bytes 7077896 | tf_op jit(solution)/shard_map/ppermute | solution.py:342
  659.2 58.5 %collective-permute-start.68 = (bf16[512,1024]{1,0:T(8,128)(2,1)}, bf16[512,1024]{1,0:T(8,128)(2,1)}, u32[]{:S(2)}, u32[]{:S(2)}) collective-permute-start(bf16[512,1024]{1,0:T(8,128)(2,1)} %get-tuple-element.566), channel_id=1, source_target_pairs={{0,0},{16,1},{2,2},{18,3},{4,4},{20,5},{6,6},{22,7},{1,8},{17,9},{... | collective-permute-start | bytes 3145736 | tf_op jit(solution)/shard_map/ppermute | solution.py:466
  668.7 49.1 %collective-permute-start.69 = (bf16[512,1024]{1,0:T(8,128)(2,1)}, bf16[512,1024]{1,0:T(8,128)(2,1)}, u32[]{:S(2)}, u32[]{:S(2)}) collective-permute-start(bf16[512,1024]{1,0:T(8,128)(2,1)} %get-tuple-element.565), channel_id=1, source_target_pairs={{8,0},{24,1},{10,2},{26,3},{12,4},{28,5},{14,6},{30,7},{9,8},{25,9... | collective-permute-start | bytes 3145736 | tf_op jit(solution)/shard_map/ppermute | solution.py:466
  668.7 49.1 %collective-permute-start.65 = (bf16[1024,1024]{1,0:T(8,128)(2,1)}, bf16[1024,1024]{1,0:T(8,128)(2,1)}, u32[]{:S(2)}, u32[]{:S(2)}) collective-permute-start(bf16[1024,1024]{1,0:T(8,128)(2,1)} %get-tuple-element.413), channel_id=1, source_target_pairs={{0,4},{1,5},{2,6},{3,7},{4,0},{5,1},{6,2},{7,3},{8,12},{9,13},{10,... | collective-permute-start | bytes 6291464 | tf_op jit(solution)/shard_map/ppermute | solution.py:342
  724.5 48.2 %collective-permute-start.71 = (bf16[512,2048]{1,0:T(8,128)(2,1)}, bf16[512,2048]{1,0:T(8,128)(2,1)S(1)}, u32[]{:S(2)}, u32[]{:S(2)}) collective-permute-start(bf16[512,2048]{1,0:T(8,128)(2,1)} %pad_maximum_fusion.13), channel_id=1, source_target_pairs={{0,2},{1,3},{2,0},{3,1},{4,6},{5,7},{6,4},{7,5},{8,10},{9,11},{10,... | collective-permute-start | bytes 6291464 | tf_op jit(solution)/shard_map/ppermute | solution.py:342
  725.4 48.1 %collective-permute-start.70 = (bf16[512,2048]{1,0:T(8,128)(2,1)}, bf16[512,2048]{1,0:T(8,128)(2,1)}, u32[]{:S(2)}, u32[]{:S(2)}) collective-permute-start(bf16[512,2048]{1,0:T(8,128)(2,1)} %get-tuple-element.426), channel_id=1, source_target_pairs={{0,4},{1,5},{2,6},{3,7},{4,0},{5,1},{6,2},{7,3},{8,12},{9,13},{10,... | collective-permute-start | bytes 6291464 | tf_op jit(solution)/shard_map/ppermute | solution.py:342
  782.8 49.6 %collective-permute-start.76 = (bf16[512,2048]{1,0:T(8,128)(2,1)}, bf16[512,2048]{1,0:T(8,128)(2,1)}, u32[]{:S(2)}, u32[]{:S(2)}) collective-permute-start(bf16[512,2048]{1,0:T(8,128)(2,1)} %pad_maximum_fusion.14), channel_id=1, source_target_pairs={{0,2},{1,3},{2,0},{3,1},{4,6},{5,7},{6,4},{7,5},{8,10},{9,11},{10,... | collective-permute-start | bytes 6291464 | tf_op jit(solution)/shard_map/ppermute | solution.py:342
  783.7 48.7 %collective-permute-start.78 = (bf16[256,2048]{1,0:T(8,128)(2,1)}, bf16[256,2048]{1,0:T(8,128)(2,1)}, u32[]{:S(2)}, u32[]{:S(2)}) collective-permute-start(bf16[256,2048]{1,0:T(8,128)(2,1)} %get-tuple-element.561), channel_id=1, source_target_pairs={{8,0},{24,1},{10,2},{26,3},{12,4},{28,5},{14,6},{30,7},{9,8},{25,9... | collective-permute-start | bytes 3145736 | tf_op jit(solution)/shard_map/ppermute | solution.py:466
  797.1 46.6 %collective-permute-start.75 = (bf16[512,2048]{1,0:T(8,128)(2,1)}, bf16[512,2048]{1,0:T(8,128)(2,1)}, u32[]{:S(2)}, u32[]{:S(2)}) collective-permute-start(bf16[512,2048]{1,0:T(8,128)(2,1)} %slice.588), channel_id=1, source_target_pairs={{0,4},{1,5},{2,6},{3,7},{4,0},{5,1},{6,2},{7,3},{8,12},{9,13},{10,... | collective-permute-start | bytes 6291464 | tf_op jit(solution)/shard_map/ppermute | solution.py:342
  801.3 107.5 %collective-permute-start.82 = (bf16[512,2048]{1,0:T(8,128)(2,1)}, bf16[512,2048]{1,0:T(8,128)(2,1)}, u32[]{:S(2)}, u32[]{:S(2)}) collective-permute-start(bf16[512,2048]{1,0:T(8,128)(2,1)} %pad_maximum_fusion.15), channel_id=1, source_target_pairs={{0,2},{1,3},{2,0},{3,1},{4,6},{5,7},{6,4},{7,5},{8,10},{9,11},{10,... | collective-permute-start | bytes 6291464 | tf_op jit(solution)/shard_map/ppermute | solution.py:342
  860.1 48.7 %collective-permute-start.81 = (bf16[256,4096]{1,0:T(8,128)(2,1)S(1)}, bf16[256,4096]{1,0:T(8,128)(2,1)S(1)}, u32[]{:S(2)}, u32[]{:S(2)}) collective-permute-start(bf16[256,4096]{1,0:T(8,128)(2,1)S(1)} %fusion.20), channel_id=1, source_target_pairs={{0,4},{1,5},{2,6},{3,7},{4,0},{5,1},{6,2},{7,3},{8,12},{9,13},{10,... | collective-permute-start | bytes 6291464 | tf_op jit(solution)/shard_map/ppermute | solution.py:342
  867.3 56.7 %collective-permute-start.85 = (bf16[256,2048]{1,0:T(8,128)(2,1)S(1)}, bf16[256,2048]{1,0:T(8,128)(2,1)S(1)}, u32[]{:S(2)}, u32[]{:S(2)}) collective-permute-start(bf16[256,2048]{1,0:T(8,128)(2,1)S(1)} %slice.682), channel_id=1, source_target_pairs={{0,2},{1,3},{2,0},{3,1},{4,6},{5,7},{6,4},{7,5},{8,10},{9,11},{10,... | collective-permute-start | bytes 3145736 | tf_op jit(solution)/shard_map/ppermute | solution.py:342
  913.7 48.9 %collective-permute-start.86 = (bf16[256,2048]{1,0:T(8,128)(2,1)S(1)}, bf16[256,2048]{1,0:T(8,128)(2,1)S(1)}, u32[]{:S(2)}, u32[]{:S(2)}) collective-permute-start(bf16[256,2048]{1,0:T(8,128)(2,1)S(1)} %slice.683), channel_id=1, source_target_pairs={{0,4},{1,5},{2,6},{3,7},{4,0},{5,1},{6,2},{7,3},{8,12},{9,13},{10,... | collective-permute-start | bytes 3145736 | tf_op jit(solution)/shard_map/ppermute | solution.py:342
  964.6 49.5 %collective-permute-start.92 = (bf16[64,4224]{1,0:T(8,128)(2,1)S(1)}, bf16[64,4224]{1,0:T(8,128)(2,1)S(1)}, u32[]{:S(2)}, u32[]{:S(2)}) collective-permute-start(bf16[64,4224]{1,0:T(8,128)(2,1)S(1)} %get-tuple-element.551), channel_id=1, source_target_pairs={{0,16},{8,24},{16,0},{24,8},{1,17},{9,25},{17,1},{25,9},{2,18},{10... | collective-permute-start | bytes 1622024 | tf_op jit(solution)/shard_map/ppermute | solution.py:347
  967.4 46.6 %collective-permute-start.93 = (bf16[64,4224]{1,0:T(8,128)(2,1)S(1)}, bf16[64,4224]{1,0:T(8,128)(2,1)S(1)}, u32[]{:S(2)}, u32[]{:S(2)}) collective-permute-start(bf16[64,4224]{1,0:T(8,128)(2,1)S(1)} %get-tuple-element.550), channel_id=1, source_target_pairs={{0,8},{8,16},{16,24},{24,0},{1,9},{9,17},{17,25},{25,1},{2,10},{10... | collective-permute-start | bytes 1622024 | tf_op jit(solution)/shard_map/ppermute | solution.py:347
  (166 other events, 2613.3 us)

commit v3 on v2

--- a/solution.py
+++ b/solution.py
@@ -438,14 +438,14 @@
     return rounds
 
 
-def to_owner(weight, place):
+def owner_pieces(weight, place):
     d, c, x, y = place
+    return [lax.dynamic_index_in_dim(weight, (d // 2 + r) % 2, 0, keepdims=False) for r in range(2)]
+
+
+def to_owner(pieces):
     rounds = expert_rounds(lax.axis_size("dp"), lax.axis_size("expert"))
-    pieces = []
-    for r, pairs in enumerate(rounds):
-        piece = lax.dynamic_index_in_dim(weight, (d // 2 + r) % 2, 0, keepdims=False)
-        pieces.append(lax.ppermute(piece, ("dp", "expert"), pairs))
-    return pieces
+    return [lax.ppermute(p, ("dp", "expert"), pairs) for p, pairs in zip(pieces, rounds)]
 
 
 def to_both(held, far, place):
@@ -458,13 +458,11 @@
     return jnp.where(y == c, keep, got), jnp.where(y == c, got, keep)
 
 
-def to_shards(total, place):
-    d, c, x, y = place
+def to_shards(parts):
     rounds = expert_rounds(lax.axis_size("dp"), lax.axis_size("expert"))
-    n = total.shape[0] // 2
     return [
-        lax.ppermute(total[r * n : (r + 1) * n], ("dp", "expert"), [(b, a) for a, b in pairs])
-        for r, pairs in enumerate(rounds)
+        lax.ppermute(part, ("dp", "expert"), [(b, a) for a, b in pairs])
+        for part, pairs in zip(parts, rounds)
     ]
 
 
@@ -502,6 +500,53 @@
         compiler_params=pltpu.CompilerParams(vmem_limit_bytes=48 * 1024 * 1024),
         cost_estimate=SMALL,
     )(*lefts, *rights)
+
+
+def add_contract_kernel(firsts, left_ref, right_ref, got_ref, *out_refs):
+    step = pl.program_id(0)
+    width = out_refs[0].shape[1]
+    total = lax.dot_general(
+        left_ref[...], right_ref[...], (((0,), (0,)), ((), ())), preferred_element_type=jnp.float32
+    )
+    total = (total + got_ref[...].astype(jnp.float32)).astype(got_ref.dtype)
+    for n, first in enumerate(firsts):
+        far = step >= 2 if first == "y" else step % 2 == 1
+        part = total[:, n * width : (n + 1) * width]
+
+        @pl.when(jnp.logical_not(far))
+        def _(n=n, part=part):
+            out_refs[2 * n][...] = part
+
+        @pl.when(far)
+        def _(n=n, part=part):
+            out_refs[2 * n + 1][...] = part
+
+
+def add_contract(left, right, got, firsts):
+    depth, rows = left.shape
+    block = rows // 4
+    width = right.shape[1] // len(firsts)
+    outs, specs = [], []
+    for first in firsts:
+        if first == "y":
+            maps = (lambda i: (jnp.minimum(i, 1), 0)), (lambda i: (jnp.maximum(i - 2, 0), 0))
+        else:
+            maps = (lambda i: (i // 2, 0)), (lambda i: (i // 2, 0))
+        outs += [jax.ShapeDtypeStruct((2 * block, width), got.dtype)] * 2
+        specs += [pl.BlockSpec((block, width), index_map) for index_map in maps]
+    return pl.pallas_call(
+        functools.partial(add_contract_kernel, firsts),
+        grid=(4,),
+        in_specs=[
+            pl.BlockSpec((depth, block), lambda i: (0, i)),
+            pl.BlockSpec((depth, right.shape[1]), lambda i: (0, 0)),
+            pl.BlockSpec((block, right.shape[1]), lambda i: (i, 0)),
+        ],
+        out_specs=specs,
+        out_shape=outs,
+        compiler_params=pltpu.CompilerParams(vmem_limit_bytes=48 * 1024 * 1024),
+        cost_estimate=SMALL,
+    )(left, right, got)
 
 
 def head_norm(v):
@@ -861,24 +906,16 @@
     vo = (vo0, vo1, vo2, vo3)
     v_b, o_b = side_by_side([p[:rows] for p in vo] + [p[rows:] for p in vo], D)
     q_a, k_b = jnp.concatenate([q_a, q_y], axis=0), by_x(k_b, k_x)
-    q_a, k_b, v_b, o_b, w_down = sync((q_a, k_b, v_b, o_b, w_down))
+    q_a, k_b, v_b, o_b, *down = sync((q_a, k_b, v_b, o_b, *owner_pieces(w_down, place)))
     v_x, q_other, k_other = flip(v_b, 2), flip(q_a, 1), flip(k_b, 1)
-    down = to_owner(w_down, place)
-    v_b, held_down = by_x(v_b, v_x), jnp.concatenate(down)
-    v_b, o_b, q_other, k_other, w_gate, w_up, held_down = sync(
-        (v_b, o_b, q_other, k_other, w_gate, w_up, held_down)
+    v_b, held_down = by_x(v_b, v_x), jnp.concatenate(to_owner(down))
+    v_b, o_b, q_other, k_other, held_down, *gate = sync(
+        (v_b, o_b, q_other, k_other, held_down, *owner_pieces(w_gate, place))
     )
     o_x, v_other, down_far = flip(o_b, 2), flip(v_b, 1), flip(held_down, 4)
-    gate = to_owner(w_gate, place)
-    o_b, held_gate = by_x(o_b, o_x), jnp.concatenate(gate)
-    o_b, v_b, v_other, q_a, k_b, down_far, held_gate, w_up = sync(
-        (o_b, v_b, v_other, q_a, k_b, down_far, held_gate, w_up)
-    )
-    gate_far, up = flip(held_gate, 4), to_owner(w_up, place)
-    down_own, down_give = to_both(held_down, down_far, place)
-    o_other, down_got = flip(o_b, 1), flip(down_give, 1)
-    o_other, q_a, k_b, v_b = sync((o_other, q_a, k_b, v_b))
-    value_w, out_w = (v_b, v_other), (o_b, o_other)
+    gate = to_owner(gate)
+    v_other, q_a, q_other, k_b, k_other, v_b = sync((v_other, q_a, q_other, k_b, k_other, v_b))
+    value_w = (v_b, v_other)
     slab = jnp.concatenate([q_a[:, D:], q_other[:, D:]], axis=0)
     slab = jnp.take(slab.reshape(32, rows, 128), to_whole, axis=0).reshape(D, 128)
     query_w, key_w = (q_a[:, :D], q_other[:, :D]), (k_b, k_other)
@@ -911,6 +948,16 @@
     )
     head_gains = (query_gain[None], key_gain[None])
     values = times(normed_attn, value_w).astype(low)
+    raw_q, raw_k, values, o_x, down_far, *gate = sync((raw_q, raw_k, values, o_x, down_far, *gate))
+    o_b, held_gate = by_x(o_b, o_x), jnp.concatenate(gate)
+    down_own, down_give = to_both(held_down, down_far, place)
+    o_b, held_gate, down_give, raw_q, raw_k, values, *up = sync(
+        (o_b, held_gate, down_give, raw_q, raw_k, values, *owner_pieces(w_up, place))
+    )
+    gate_far, up = flip(held_gate, 4), to_owner(up)
+    o_other, down_got = flip(o_b, 1), flip(down_give, 1)
+    o_other, raw_q, raw_k, values = sync((o_other, raw_q, raw_k, values))
+    out_w = (o_b, o_other)
     like = jax.ShapeDtypeStruct((row_count, D), low)
     queries, keys_rot, context = on_chip(
         attend_kernel, [like] * 3, order, raw_q, raw_k, values, *head_gains, *turns
@@ -1001,11 +1048,20 @@
     ring, h0_x, m_ring, down_sum, up_keep, up_give, gate_far, m_far = sync(
         (ring, h0_x, m_ring, down_sum, up_keep, up_give, gate_far, m_far)
     )
-    n = down_sum.shape[0] // 2
-    gate_sum = sync((add(gate_keep, gate_far), m_far))[0]
-    up_far, gate_back, m_x = flip(up_give, 4), to_shards(gate_sum, place), flip(m_far, 2)
-    down_got = flip(down_sum[n:], 1)
-    down_got, ring = sync((down_got, ring))
+    def two(value):
+        n = value.shape[0] // 2
+        return value[:n], value[n:]
+
+    def halves_sum(left, right):
+        return [add(a, b) for a, b in zip(two(left), two(right))]
+
+    down_mine, down_other = two(down_sum)
+    ring, h0_x, m_far, up_give, down_mine, down_other, *gate_parts = sync(
+        (ring, h0_x, m_far, up_give, down_mine, down_other, *halves_sum(gate_keep, gate_far))
+    )
+    down_got = flip(down_other, 1)
+    gate_back, up_far, m_x = to_shards(gate_parts), flip(up_give, 4), flip(m_far, 2)
+    down_got, ring, h0_x = sync((down_got, ring, h0_x))
     back = h0[0].astype(wide) + h0_x.astype(wide) + ring.astype(wide)
     grad_normed_ffn = back[:row_count]
     grad_gates = back[row_count : row_count + experts]
@@ -1021,15 +1077,12 @@
     grad_midway = grad_out + grad_midway_norm
     grad_attn = grad_midway.astype(low)
 
-    def weight_grad(left, right):
-        return contract([left[:, :half]], [right]), contract([left[:, half:]], [right])
-
     def times_back(left, pair):
         return jnp.concatenate(
             [times_transposed(left, pair[0]), times_transposed(left, pair[1])], axis=1
         )
 
-    out_sums = weight_grad(context, grad_attn)
+    out_core = flip(contract([context[:, half:]], [grad_attn]), 1)
     grad_context = times_back(grad_attn, out_w).astype(low)
     grad_heads, grad_query_gain, grad_key_gain = on_chip(
         attend_back_kernel,
@@ -1044,41 +1097,30 @@
         *head_gains,
         *turns,
     )
-    heads_sums = weight_grad(normed_attn, grad_heads)
-    down_keep, down_give = from_owner(down_sum[:n], down_got, place)
-    out_own = add(out_sums[0], flip(out_sums[1], 1))
-    m_x, up_far, down_keep, down_give, out_own, heads_own, heads_other, *gate_back = sync(
-        (m_x, up_far, down_keep, down_give, out_own, *heads_sums, *gate_back)
+    heads_other = contract([normed_attn[:, half:]], [grad_heads])
+    down_keep, down_give = from_owner(down_mine, down_got, place)
+    out_own, out_far = add_contract(context[:, :half], grad_attn, out_core, ("x",))
+    m_x, up_far, down_keep, down_give, out_own, out_far, heads_other, *gate_back = sync(
+        (m_x, up_far, down_keep, down_give, out_own, out_far, heads_other, *gate_back)
     )
     grad_gate = two_experts(gate_back, place)
     m2, m3, m0 = (
         add(t[0], m_x[k * row_count : (k + 1) * row_count]) for k, t in enumerate(ms)
     )
 
-    def x_first(own):
-        n = own.shape[0] // 4
-        far = jnp.concatenate([own[n : 2 * n], own[3 * n :]], axis=0)
-        return jnp.concatenate([own[:n], own[2 * n : 3 * n]], axis=0), flip(far, 2)
-
-    def half_to(own, bit):
-        n = own.shape[0] // 2
-        return own[:n], flip(own[n:], bit)
-
-    up_sum = add(up_keep, up_far)
-    up_back, down_far, heads_core = to_shards(up_sum, place), flip(down_give, 4), flip(heads_other, 1)
-    out_own, out_far = x_first(out_own)
-    query_own, key_own, value_own = (
-        add(heads_own[:, k * D : (k + 1) * D], heads_core[:, k * D : (k + 1) * D]) for k in range(3)
-    )
-    down_far, out_far, query_own, key_own, value_own, *up_back = sync(
-        (down_far, out_far, query_own, key_own, value_own, *up_back)
-    )
-    grad_up = two_experts(up_back, place)
-    down_sum = add(down_keep, down_far)
-    query_own, query_far = half_to(query_own, 4)
-    key_own, key_far = x_first(key_own)
-    down_back = to_shards(down_sum, place)
-    down_back[0], grad_heads = sync((down_back[0], grad_heads))
+    def fold(value, bit):
+        n = value.shape[1] // 2
+        return value[:, :n] + flip(value[:, n:], bit)
+
+    out_far, down_give, heads_other, *up_parts = sync(
+        (out_far, down_give, heads_other, *halves_sum(up_keep, up_far))
+    )
+    up_back, down_far = to_shards(up_parts), flip(down_give, 4)
+    out_far, heads_core = flip(out_far, 2), flip(heads_other, 1)
+    heads_core, grad_heads = sync((heads_core, grad_heads))
+    query_own, query_far, key_own, key_far, value_own, value_far = add_contract(
+        normed_attn[:, :half], grad_heads, heads_core, ("y", "x", "x")
+    )
     grad_normed_attn = sum(
         times_back(grad_heads[:, k * D : (k + 1) * D], w)
         for k, w in enumerate((query_w, key_w, value_w))
@@ -1092,48 +1134,56 @@
         axis=0,
     )
     small = reorder(small, order, True)
-    query_far, key_far, small, down_back[1], m_ring = sync(
-        (query_far, key_far, small, down_back[1], m_ring)
+    down_far, out_far, small, *parts = sync(
+        (down_far, out_far, small, query_own, query_far, key_own, key_far, value_own, value_far, *up_back)
+    )
+    query_own, query_far, key_own, key_far, value_own, value_far, *up_back = parts
+    grad_up = two_experts(up_back, place)
+    out_own, out_far = halves_sum(out_own, out_far)
+    query_far, key_far, value_far, out_own, out_far, *down_parts = sync(
+        (query_far, key_far, value_far, out_own, out_far, *halves_sum(down_keep, down_far))
+    )
+    query_far, key_far, down_back = flip(query_far, 4), flip(key_far, 2), to_shards(down_parts)
+    small = fold(small, 1)
+    query_far, key_far, small, m_ring, *down_back = sync(
+        (query_far, key_far, small, m_ring, *down_back)
     )
     grad_down = two_experts(down_back, place)
 
-    def fold(value, bit):
-        n = value.shape[1] // 2
-        return value[:, :n] + flip(value[:, n:], bit)
-
-    ring = turn(add(m2, m_ring), 1)
+    key_own, key_far = halves_sum(key_own, key_far)
+    query_own, query_far = halves_sum(query_own, query_far)
+    ring, key_far, out_far, value_far, query_far = sync(
+        (add(m2, m_ring), key_far, out_far, value_far, query_far)
+    )
+    ring, key_far, out_far, value_far = (
+        turn(ring, 1), flip(key_far, 4), flip(out_far, 4), flip(value_far, 2)
+    )
     ring = turn(add(m3, ring), 1)
-    ko_own, ko_far = half_to(
-        jnp.concatenate([add(key_own, key_far), add(out_own, out_far)], axis=1), 4
-    )
-    value_own, value_far = x_first(value_own)
-    small = fold(fold(small, 1), 4)
-    ring, ko_far, value_far, small = sync((ring, ko_far, value_far, small))
+    small = fold(small, 4)
+    ring, key_far, out_far, value_far, small = sync((ring, key_far, out_far, value_far, small))
     block_out = (midway + m0.astype(wide) + ring.astype(wide)).astype(low)
-
-    def to_owners(pieces):
-        return [turn(p, -k) for k, p in enumerate(pieces) if k]
-
-    def summed(pieces):
-        return sum(p.astype(wide) for p in pieces)
+    value_own, value_far = halves_sum(value_own, value_far)
 
     def by_steps(both):
         return [both[i * rows : (i + 1) * rows] for i in range(count_dp)]
 
-    ko = by_steps(add(ko_own, ko_far))
-    ko_far = to_owners(ko)
-    query_own, query_far = half_to(add(query_own, query_far), 2)
-    value_own, value_far = half_to(add(value_own, value_far), 4)
+    ko = by_steps(jnp.concatenate([add(key_own, key_far), add(out_own, out_far)], axis=1))
+    value_far, *ko = sync((value_far, *ko))
+    ko_ring, query_far, value_far = turn(ko[3], -1), flip(query_far, 2), flip(value_far, 4)
+    ko_ring = turn(add(ko[2], ko_ring), -1)
     small = fold(small, 2)
-    query_far, value_far, small, *ko_far = sync((query_far, value_far, small, *ko_far))
+    query_far, value_far, small, ko_ring = sync((query_far, value_far, small, ko_ring))
     n = small.shape[0]
     small = small.reshape(n, count_dp, rows).transpose(1, 2, 0).reshape(count_dp * rows, n)
     small = jnp.pad(small.astype(low), ((0, 0), (0, 128 - n)))
     qv = by_steps(
         jnp.concatenate([add(query_own, query_far), add(value_own, value_far), small], axis=1)
     )
-    qv_ring = summed(qv[:1] + to_owners(qv))
-    ko_ring = summed(ko[:1] + ko_far)
+    ko_ring, qv_ring = turn(add(ko[1], ko_ring), -1), turn(qv[3], -1)
+    ko_ring, qv_ring = sync((ko_ring, qv_ring))
+    ko_ring = ko_ring.astype(wide) + ko[0].astype(wide)
+    qv_ring = turn(add(qv[2], qv_ring), -1)
+    qv_ring = turn(add(qv[1], qv_ring), -1).astype(wide) + qv[0].astype(wide)
     grad_key, grad_outproj = ko_ring[:, :D], ko_ring[:, D:]
     grad_query, grad_value = qv_ring[:, :D], qv_ring[:, D : 2 * D]
     small = qv_ring[:, 2 * D :]

time: 1030 us -> 981 us (0.952)
  starting transfers between devices: 123 us -> 104 us
  other arithmetic: 131 us -> 117 us
    ppermute x21, waiting for transfers between devices: 213 us -> 168 us  [turn(): lax.ppermute(value, 'dp', [(i, (i + step) % count) for i in range(count)])]
    ppermute x61 -> x62, waiting for transfers between devices: 97.6 us -> 126 us  [flip(): return lax.ppermute(value, 'expert', [(i, i ^ bit) for i in range(count)])]
    pallas_call x0 -> x2, Pallas kernels: none -> 18.5 us  [add_contract(): pl.pallas_call(functools.partial(add_contract_kernel, firsts), grid=(4,),...]
    convert_element_type x26 -> x29, other arithmetic: 71.1 us -> 56.2 us  [add(): return (left.astype(wide) + right.astype(wide)).astype(low)]
    ppermute x61 -> x62, starting transfers between devices: 51.6 us -> 39.3 us  [flip(): return lax.ppermute(value, 'expert', [(i, i ^ bit) for i in range(count)])]
    slice x10 -> x1, local copies, waits for them, and re-layouts: 13.1 us -> 1.88 us  [two(): return (value[:n], value[n:])]
    pallas_call x7 -> x5, Pallas kernels: 55 us -> 47.3 us  [contract(): pl.pallas_call(functools.partial(contract_kernel, len(lefts)), grid=(widt...]
    unnamed x219 -> x253, local copies, waits for them, and re-layouts: 27.2 us -> 30.6 us
  transfers between devices with their start and end apart: 94 -> 95, of which waited for: 31 -> 37; matrix products, arithmetic and copies ran while one was open for 20% -> 14% of each run, Pallas kernels for 23% -> 25%
where the time goes in v3:
time: 981 us; the launch traced here: 973 us
  waiting for transfers between devices  396 us (40%)
  Pallas kernels  249 us (25%)
  other arithmetic  117 us (12%)
  starting transfers between devices  104 us (11%)
  local copies, waits for them, and re-layouts  58.1 us (6%)
  matrix products  46.7 us (5%)
    ppermute x21, waiting for transfers between devices, turn(): lax.ppermute(value, 'dp', [(i, (i + step) % count) for i in range(count)])  168 us
    pallas_call x4, Pallas kernels, expert_chunk(): pl.pallas_call(functools.partial(expert_kernel, experts, count, tokens),...  151 us
    ppermute x62, waiting for transfers between devices, flip(): return lax.ppermute(value, 'expert', [(i, i ^ bit) for i in range(count)])  126 us
    ppermute x6, waiting for transfers between devices, to_owner(): lax.ppermute(p, ('dp', 'expert'), pairs)  79.8 us
    convert_element_type x29, other arithmetic, add(): return (left.astype(wide) + right.astype(wide)).astype(low)  56.2 us
    pallas_call x5, Pallas kernels, contract(): pl.pallas_call(functools.partial(contract_kernel, len(lefts)), grid=(widt...  47.3 us
    ppermute x62, starting transfers between devices, flip(): return lax.ppermute(value, 'expert', [(i, i ^ bit) for i in range(count)])  39.3 us
    unnamed x253, local copies, waits for them, and re-layouts  30.6 us
  transfers between devices with their start and end apart: 95, of which 37 were waited for; matrix products, arithmetic and copies ran while one was open for 14% of the time, Pallas kernels for 25%

profile of v3, /device:TPU:0, one launch (start us, length us, event | category | flops | bytes accessed | tf_op | source)
XLA Modules:
  0.0 972.9 jit_solution(13862969205139663175)
XLA Ops:
  8.9 14.3 %collective-permute-done = bf16[64,4224]{1,0:T(8,128)(2,1)S(1)} collective-permute-done((bf16[64,4224]{1,0:T(8,128)(2,1)S(1)}, bf16[64,4224]{1,0:T(8,128)(2,1)S(1)}, u32[]{:S(2)}, u32[]{:S(2)}) %collective-permute-start) | collective-permute-done | bytes 540704 | tf_op jit(solution)/shard_map/ppermute | solution.py:347
  23.2 15.2 %collective-permute-done.1 = bf16[64,4224]{1,0:T(8,128)(2,1)S(1)} collective-permute-done((bf16[64,4224]{1,0:T(8,128)(2,1)S(1)}, bf16[64,4224]{1,0:T(8,128)(2,1)S(1)}, u32[]{:S(2)}, u32[]{:S(2)}) %collective-permute-start.1) | collective-permute-done | bytes 540704 | tf_op jit(solution)/shard_map/ppermute | solution.py:347
  42.7 10.0 %collective-permute-done.2 = bf16[64,4224]{1,0:T(8,128)(2,1)S(1)} collective-permute-done((bf16[64,4224]{1,0:T(8,128)(2,1)S(1)}, bf16[64,4224]{1,0:T(8,128)(2,1)S(1)}, u32[]{:S(2)}, u32[]{:S(2)}) %collective-permute-start.2) | collective-permute-done | bytes 540704 | tf_op jit(solution)/shard_map/ppermute | solution.py:347
  56.7 19.0 %collective-permute-done.5 = bf16[256,2048]{1,0:T(8,128)(2,1)} collective-permute-done((bf16[256,2048]{1,0:T(8,128)(2,1)S(1)}, bf16[256,2048]{1,0:T(8,128)(2,1)}, u32[]{:S(2)}, u32[]{:S(2)}) %collective-permute-start.5) | collective-permute-done | bytes 1048608 | tf_op jit(solution)/shard_map/ppermute | solution.py:342
  85.0 19.0 %collective-permute-done.9 = bf16[128,4096]{1,0:T(8,128)(2,1)S(1)} collective-permute-done((bf16[128,4096]{1,0:T(8,128)(2,1)}, bf16[128,4096]{1,0:T(8,128)(2,1)S(1)}, u32[]{:S(2)}, u32[]{:S(2)}) %collective-permute-start.9) | collective-permute-done | bytes 1048608 | tf_op jit(solution)/shard_map/ppermute | solution.py:347
  105.0 18.7 %collective-permute-done.8 = bf16[512,2048]{1,0:T(8,128)(2,1)S(1)} collective-permute-done((bf16[512,2048]{1,0:T(8,128)(2,1)S(1)}, bf16[512,2048]{1,0:T(8,128)(2,1)S(1)}, u32[]{:S(2)}, u32[]{:S(2)}) %collective-permute-start.8) | collective-permute-done | bytes 2097184 | tf_op jit(solution)/shard_map/ppermute | solution.py:342
  138.1 43.6 %collective-permute-done.15 = bf16[256,2048]{1,0:T(8,128)(2,1)S(1)} collective-permute-done((bf16[256,2048]{1,0:T(8,128)(2,1)S(1)}, bf16[256,2048]{1,0:T(8,128)(2,1)S(1)}, u32[]{:S(2)}, u32[]{:S(2)}) %collective-permute-start.15) | collective-permute-done | bytes 1048608 | tf_op jit(solution)/shard_map/ppermute | solution.py:448
  194.2 9.5 collective-permute-start.19
  226.0 17.4 %collective-permute-done.20 = bf16[512,1024]{1,0:T(8,128)(2,1)} collective-permute-done((bf16[512,1024]{1,0:T(8,128)(2,1)}, bf16[512,1024]{1,0:T(8,128)(2,1)}, u32[]{:S(2)}, u32[]{:S(2)}) %collective-permute-start.20) | collective-permute-done | bytes 1048608 | tf_op jit(solution)/shard_map/ppermute | solution.py:448
  264.1 13.9 %shard_map.264 = (bf16[192,2048]{1,0:T(8,128)(2,1)S(1)}, bf16[192,2048]{1,0:T(8,128)(2,1)S(1)}, bf16[192,2048]{1,0:T(8,128)(2,1)S(1)}) custom-call(s32[17]{0:T(128)S(1)} %pad_add_fusion.order_ref, f32[192,2048]{1,0:T(8,128)S(1)} %copy-done.1, f32[192,2048]{1,0:T(8,128)S(1)} %convolution_add_fusion.3.raw_k, bf16[192,2048]{1,0:T(8,128)(2,1)S(1)} %fusion.12.v_ref, ...), custom_call_target="tpu_custom_call" | custom-call | flops 1 | bytes 1 | tf_op jit(solution)/shard_map/pallas_call | solution.py:664
  287.1 18.8 %collective-permute-done.25 = bf16[512,1024]{1,0:T(8,128)(2,1)S(1)} collective-permute-done((bf16[512,1024]{1,0:T(8,128)(2,1)}, bf16[512,1024]{1,0:T(8,128)(2,1)S(1)}, u32[]{:S(2)}, u32[]{:S(2)}) %collective-permute-start.25) | collective-permute-done | bytes 1048608 | tf_op jit(solution)/shard_map/ppermute | solution.py:448
  310.7 38.4 %collective-permute-done.26.refs_1_ = bf16[400,2048]{1,0:T(8,128)(2,1)} collective-permute-done((bf16[400,2048]{1,0:T(8,128)(2,1)S(1)}, bf16[400,2048]{1,0:T(8,128)(2,1)}, u32[]{:S(2)}, u32[]{:S(2)}) %collective-permute-start.26) | collective-permute-done | bytes 1638432 | tf_op jit(solution)/shard_map/ppermute | solution.py:347
  365.3 37.6 %shard_map.265 = (bf16[512,2048]{1,0:T(8,128)(2,1)}, bf16[512,1024]{1,0:T(8,128)(2,1)}, bf16[512,2048]{1,0:T(8,128)(2,1)}, bf16[512,1024]{1,0:T(8,128)(2,1)}, bf...) custom-call(s32[5]{0:T(128)} %stack.50.refs_0_, ...), custom_call_target="tpu_custom_call" | custom-call | flops 1 | bytes 1 | tf_op jit(solution)/shard_map/pallas_call | solution.py:819
  406.9 37.8 %shard_map.266 = (bf16[512,2048]{1,0:T(8,128)(2,1)}, bf16[512,1024]{1,0:T(8,128)(2,1)}, bf16[512,2048]{1,0:T(8,128)(2,1)}, bf16[512,1024]{1,0:T(8,128)(2,1)}, bf...) custom-call(s32[5]{0:T(128)} %stack.50.refs_0_, ...), custom_call_target="tpu_custom_call" | custom-call | flops 1 | bytes 1 | tf_op jit(solution)/shard_map/pallas_call | solution.py:819
  452.2 38.0 %shard_map.267 = (bf16[512,2048]{1,0:T(8,128)(2,1)}, bf16[512,1024]{1,0:T(8,128)(2,1)}, bf16[512,2048]{1,0:T(8,128)(2,1)}, bf16[512,1024]{1,0:T(8,128)(2,1)}, bf...) custom-call(s32[5]{0:T(128)} %stack.50.refs_0_, ...), custom_call_target="tpu_custom_call" | custom-call | flops 1 | bytes 1 | tf_op jit(solution)/shard_map/pallas_call | solution.py:819
  498.1 37.7 %shard_map.268 = (bf16[512,2048]{1,0:T(8,128)(2,1)}, bf16[512,1024]{1,0:T(8,128)(2,1)}, bf16[512,2048]{1,0:T(8,128)(2,1)}, bf16[512,1024]{1,0:T(8,128)(2,1)}, bf...) custom-call(s32[5]{0:T(128)} %stack.50.refs_0_, ...), custom_call_target="tpu_custom_call" | custom-call | flops 1 | bytes 1 | tf_op jit(solution)/shard_map/pallas_call | solution.py:819
  543.2 12.8 %shard_map.269 = bf16[2048,1024]{1,0:T(8,128)(2,1)} custom-call(bf16[512,2048]{1,0:T(8,128)(2,1)} %get-tuple-element.454.refs_0_, bf16[512,2048]{1,0:T(8,128)(2,1)} %get-tuple-element.455.refs_1_, bf16[512,2048]{1,0:T(8,128)(2,1)} %get-tuple-element.456.refs_2_, bf16[512,2048]{1,0:T(8,128)(2,1)} %get-tuple-element.457.refs_3_, ...), custom_call_target="tpu_custom_call" | custom-call | flops 1 | bytes 1 | tf_op jit(solution)/shard_map/pallas_call | solution.py:493
  572.7 12.2 %shard_map.270 = bf16[2048,1024]{1,0:T(8,128)(2,1)} custom-call(bf16[512,2048]{1,0:T(8,128)(2,1)} %get-tuple-element.454.refs_0_, bf16[512,2048]{1,0:T(8,128)(2,1)} %get-tuple-element.455.refs_1_, bf16[512,2048]{1,0:T(8,128)(2,1)} %get-tuple-element.456.refs_2_, bf16[512,2048]{1,0:T(8,128)(2,1)} %get-tuple-element.457.refs_3_, ...), custom_call_target="tpu_custom_call" | custom-call | flops 1 | bytes 1 | tf_op jit(solution)/shard_map/pallas_call | solution.py:493
  603.9 14.2 %shard_map.271 = bf16[1024,2048]{1,0:T(8,128)(2,1)} custom-call(bf16[512,1024]{1,0:T(8,128)(2,1)S(1)} %copy-done.10, bf16[512,1024]{1,0:T(8,128)(2,1)S(1)} %copy-done.11, bf16[512,1024]{1,0:T(8,128)(2,1)S(1)} %copy-done.13, bf16[512,1024]{1,0:T(8,128)(2,1)S(1)} %copy-done.16, bf16[512,2048]{1,0:T(8,128)(2,1)} %get-tuple-element.474.refs_4_, ...), custom_call_target="tpu_custom_call" | custom-call | flops 1 | bytes 1 | tf_op jit(solution)/shard_map/pallas_call | solution.py:493
  622.3 12.4 %collective-permute-done.60 = bf16[192,2048]{1,0:T(8,128)(2,1)} collective-permute-done((bf16[192,2048]{1,0:T(8,128)(2,1)}, bf16[192,2048]{1,0:T(8,128)(2,1)}, u32[]{:S(2)}, u32[]{:S(2)}) %collective-permute-start.60) | collective-permute-done | bytes 786464 | tf_op jit(solution)/shard_map/ppermute | solution.py:347
  656.1 9.5 collective-permute-start.68
  674.6 15.2 %shard_map.274 = (bf16[192,6144]{1,0:T(8,128)(2,1)S(1)}, f32[1,2048]{1,0:T(1,128)S(1)}, f32[1,2048]{1,0:T(1,128)S(1)}) custom-call(s32[17]{0:T(128)S(1)} %pad_add_fusion.order_ref, bf16[192,2048]{1,0:T(8,128)(2,1)S(1)} %pad_maximum_fusion.16.grad_ref, bf16[192,2048]{1,0:T(8,128)(2,1)S(1)} %copy-done.23, bf16[192,2048]{1,0:T(8,128)(2,1)S(1)} %copy-done.25, ...), custom_call_target="tpu_custom_call" | custom-call | flops 1 | bytes 1 | tf_op jit(solution)/shard_map/pallas_call | solution.py:664
  714.9 9.5 collective-permute-start.73
  724.4 6.7 collective-permute-done.72.got_ref
  744.1 12.7 %shard_map.278 = (bf16[512,2048]{1,0:T(8,128)(2,1)S(1)}, bf16[512,2048]{1,0:T(8,128)(2,1)S(1)}, bf16[512,2048]{1,0:T(8,128)(2,1)}, bf16[512,2048]{1,0:T(8,128)(2...) custom-call(bf16[192,1024]{1,0:T(8,128)(2,1)S(1)} %get-tuple-element.708.left_ref, bf16[192,6144]{1,0:T(8,128)(2,1)} %copy-done, ...), custom_call_target="tpu_custom_call" | custom-call | flops 1 | bytes 1 | tf_op jit(solution)/shard_map/pallas_call | solution.py:537
  781.0 21.9 %collective-permute-done.79 = bf16[256,2048]{1,0:T(8,128)(2,1)S(1)} collective-permute-done((bf16[256,2048]{1,0:T(8,128)(2,1)S(1)}, bf16[256,2048]{1,0:T(8,128)(2,1)S(1)}, u32[]{:S(2)}, u32[]{:S(2)}) %collective-permute-start.79) | collective-permute-done | bytes 1048608 | tf_op jit(solution)/shard_map/ppermute | solution.py:464
  802.8 17.1 %collective-permute-done.75 = bf16[512,2048]{1,0:T(8,128)(2,1)S(1)} collective-permute-done((bf16[512,2048]{1,0:T(8,128)(2,1)S(1)}, bf16[512,2048]{1,0:T(8,128)(2,1)S(1)}, u32[]{:S(2)}, u32[]{:S(2)}) %collective-permute-start.75) | collective-permute-done | bytes 2097184 | tf_op jit(solution)/shard_map/ppermute | solution.py:342
  834.7 17.7 %collective-permute-done.80 = bf16[192,2048]{1,0:T(8,128)(2,1)S(1)} collective-permute-done((bf16[192,2048]{1,0:T(8,128)(2,1)S(1)}, bf16[192,2048]{1,0:T(8,128)(2,1)S(1)}, u32[]{:S(2)}, u32[]{:S(2)}) %collective-permute-start.80) | collective-permute-done | bytes 786464 | tf_op jit(solution)/shard_map/ppermute | solution.py:347
  858.1 23.5 %collective-permute-done.85 = f32[24,512]{1,0:T(8,128)S(1)} collective-permute-done((f32[24,512]{1,0:T(8,128)S(1)}, f32[24,512]{1,0:T(8,128)S(1)}, u32[]{:S(2)}, u32[]{:S(2)}) %collective-permute-start.85) | collective-permute-done | bytes 49184 | tf_op jit(solution)/shard_map/ppermute | solution.py:342
  908.9 10.0 %collective-permute-done.88 = f32[24,256]{1,0:T(8,128)S(1)} collective-permute-done((f32[24,256]{1,0:T(8,128)S(1)}, f32[24,256]{1,0:T(8,128)S(1)}, u32[]{:S(2)}, u32[]{:S(2)}) %collective-permute-start.88) | collective-permute-done | bytes 24608 | tf_op jit(solution)/shard_map/ppermute | solution.py:342
  929.1 17.9 %collective-permute-done.91 = bf16[64,4096]{1,0:T(8,128)(2,1)S(1)} collective-permute-done((bf16[64,4096]{1,0:T(8,128)(2,1)S(1)}, bf16[64,4096]{1,0:T(8,128)(2,1)S(1)}, u32[]{:S(2)}, u32[]{:S(2)}) %collective-permute-start.91) | collective-permute-done | bytes 524320 | tf_op jit(solution)/shard_map/ppermute | solution.py:347
  962.9 7.2 collective-permute-done.94
  (592 shorter events, 360.7 us)
Async XLA Ops:
  80.5 43.2 %collective-permute-start.8 = (bf16[512,2048]{1,0:T(8,128)(2,1)S(1)}, bf16[512,2048]{1,0:T(8,128)(2,1)S(1)}, u32[]{:S(2)}, u32[]{:S(2)}) collective-permute-start(bf16[512,2048]{1,0:T(8,128)(2,1)S(1)} %pad_maximum_fusion.9), channel_id=1, source_target_pairs={{0,2},{1,3},{2,0},{3,1},{4,6},{5,7},{6,4},{7,5},{8,10},{9,11},{10,... | collective-permute-start | bytes 6291464 | tf_op jit(solution)/shard_map/ppermute | solution.py:342
  81.7 49.6 %collective-permute-start.7 = (bf16[512,2176]{1,0:T(8,128)(2,1)S(1)}, bf16[512,2176]{1,0:T(8,128)(2,1)S(1)}, u32[]{:S(2)}, u32[]{:S(2)}) collective-permute-start(bf16[512,2176]{1,0:T(8,128)(2,1)S(1)} %pad_maximum_fusion.8), channel_id=1, source_target_pairs={{0,4},{1,5},{2,6},{3,7},{4,0},{5,1},{6,2},{7,3},{8,12},{9,13},{10,... | collective-permute-start | bytes 6684680 | tf_op jit(solution)/shard_map/ppermute | solution.py:342
  131.7 54.1 %collective-permute-start.12 = (bf16[1024,2176]{1,0:T(8,128)(2,1)S(1)}, bf16[1024,2176]{1,0:T(8,128)(2,1)S(1)}, u32[]{:S(2)}, u32[]{:S(2)}) collective-permute-start(bf16[1024,2176]{1,0:T(8,128)(2,1)S(1)} %pad_maximum_fusion), channel_id=1, source_target_pairs={{0,1},{1,0},{2,3},{3,2},{4,5},{5,4},{6,7},{7,6},{8,9},{9,8},{10,11... | collective-permute-start | bytes 13369352 | tf_op jit(solution)/shard_map/ppermute | solution.py:342
  131.8 54.0 %collective-permute-start.13 = (bf16[1024,2048]{1,0:T(8,128)(2,1)S(1)}, bf16[1024,2048]{1,0:T(8,128)(2,1)S(1)}, u32[]{:S(2)}, u32[]{:S(2)}) collective-permute-start(bf16[1024,2048]{1,0:T(8,128)(2,1)S(1)} %pad_maximum_fusion.1), channel_id=1, source_target_pairs={{0,1},{1,0},{2,3},{3,2},{4,5},{5,4},{6,7},{7,6},{8,9},{9,8},{10,11... | collective-permute-start | bytes 12582920 | tf_op jit(solution)/shard_map/ppermute | solution.py:342
  132.2 51.0 %collective-permute-start.11 = (bf16[512,2048]{1,0:T(8,128)(2,1)S(1)}, bf16[512,2048]{1,0:T(8,128)(2,1)S(1)}, u32[]{:S(2)}, u32[]{:S(2)}) collective-permute-start(bf16[512,2048]{1,0:T(8,128)(2,1)S(1)} %get-tuple-element.305), channel_id=1, source_target_pairs={{0,2},{1,3},{2,0},{3,1},{4,6},{5,7},{6,4},{7,5},{8,10},{9,11},{10,... | collective-permute-start | bytes 6291464 | tf_op jit(solution)/shard_map/ppermute | solution.py:342
  133.5 48.2 %collective-permute-start.15 = (bf16[256,2048]{1,0:T(8,128)(2,1)S(1)}, bf16[256,2048]{1,0:T(8,128)(2,1)S(1)}, u32[]{:S(2)}, u32[]{:S(2)}) collective-permute-start(bf16[256,2048]{1,0:T(8,128)(2,1)S(1)} %get-tuple-element.310), channel_id=1, source_target_pairs={{0,8},{1,24},{2,10},{3,26},{4,12},{5,28},{6,14},{7,30},{8,9},{9,25... | collective-permute-start | bytes 3145736 | tf_op jit(solution)/shard_map/ppermute | solution.py:448
  192.0 51.4 %collective-permute-start.17 = (bf16[512,2048]{1,0:T(8,128)(2,1)}, bf16[512,2048]{1,0:T(8,128)(2,1)}, u32[]{:S(2)}, u32[]{:S(2)}) collective-permute-start(bf16[512,2048]{1,0:T(8,128)(2,1)} %get-tuple-element.311), channel_id=1, source_target_pairs={{0,2},{1,3},{2,0},{3,1},{4,6},{5,7},{6,4},{7,5},{8,10},{9,11},{10,... | collective-permute-start | bytes 6291464 | tf_op jit(solution)/shard_map/ppermute | solution.py:342
  193.3 50.1 %collective-permute-start.18 = (bf16[512,2048]{1,0:T(8,128)(2,1)}, bf16[512,2048]{1,0:T(8,128)(2,1)}, u32[]{:S(2)}, u32[]{:S(2)}) collective-permute-start(bf16[512,2048]{1,0:T(8,128)(2,1)} %pad_maximum_fusion.10), channel_id=1, source_target_pairs={{0,4},{1,5},{2,6},{3,7},{4,0},{5,1},{6,2},{7,3},{8,12},{9,13},{10,... | collective-permute-start | bytes 6291464 | tf_op jit(solution)/shard_map/ppermute | solution.py:342
  255.8 50.1 %collective-permute-start.22 = (bf16[1024,1024]{1,0:T(8,128)(2,1)}, bf16[1024,1024]{1,0:T(8,128)(2,1)S(1)}, u32[]{:S(2)}, u32[]{:S(2)}) collective-permute-start(bf16[1024,1024]{1,0:T(8,128)(2,1)} %pad_maximum_fusion.11), channel_id=1, source_target_pairs={{0,4},{1,5},{2,6},{3,7},{4,0},{5,1},{6,2},{7,3},{8,12},{9,13},{10,... | collective-permute-start | bytes 6291464 | tf_op jit(solution)/shard_map/ppermute | solution.py:342
  257.0 48.9 %collective-permute-start.23 = (bf16[512,2048]{1,0:T(8,128)(2,1)}, bf16[512,2048]{1,0:T(8,128)(2,1)S(1)}, u32[]{:S(2)}, u32[]{:S(2)}) collective-permute-start(bf16[512,2048]{1,0:T(8,128)(2,1)} %get-tuple-element.341), channel_id=1, source_target_pairs={{0,1},{1,0},{2,3},{3,2},{4,5},{5,4},{6,7},{7,6},{8,9},{9,8},{10,11... | collective-permute-start | bytes 6291464 | tf_op jit(solution)/shard_map/ppermute | solution.py:342
  259.7 46.3 %collective-permute-start.25 = (bf16[512,1024]{1,0:T(8,128)(2,1)}, bf16[512,1024]{1,0:T(8,128)(2,1)S(1)}, u32[]{:S(2)}, u32[]{:S(2)}) collective-permute-start(bf16[512,1024]{1,0:T(8,128)(2,1)} %get-tuple-element.343), channel_id=1, source_target_pairs={{0,8},{1,24},{2,10},{3,26},{4,12},{5,28},{6,14},{7,30},{8,9},{9,25... | collective-permute-start | bytes 3145736 | tf_op jit(solution)/shard_map/ppermute | solution.py:448
  308.1 48.1 %collective-permute-start.29 = (bf16[1024,1024]{1,0:T(8,128)(2,1)S(1)}, bf16[1024,1024]{1,0:T(8,128)(2,1)S(1)}, u32[]{:S(2)}, u32[]{:S(2)}) collective-permute-start(bf16[1024,1024]{1,0:T(8,128)(2,1)S(1)} %constant_dynamic-update-slice_fusion.2), channel_id=1, source_target_pairs={{0,4},{1,5},{2,6},{3,7},{4,0},{5,1},{6,2},{7,3},{8,12},{9,13},{10,... | collective-permute-start | bytes 6291464 | tf_op jit(solution)/shard_map/ppermute | solution.py:342
  358.9 44.0 %collective-permute-start.31 = (bf16[400,2048]{1,0:T(8,128)(2,1)}, bf16[400,2048]{1,0:T(8,128)(2,1)}, u32[]{:S(2)}, u32[]{:S(2)}) collective-permute-start(bf16[400,2048]{1,0:T(8,128)(2,1)} %collective-permute-done.26.refs_1_), channel_id=1, source_target_pairs={{0,8},{8,16},{16,24},{24,0},{1,9},{9,17},{17,25},{25,1},{2,10},{10... | collective-permute-start | bytes 4915208 | tf_op jit(solution)/shard_map/ppermute | solution.py:347
  358.9 44.0 %collective-permute-start.32 = (bf16[400,2048]{1,0:T(8,128)(2,1)}, bf16[400,2048]{1,0:T(8,128)(2,1)}, u32[]{:S(2)}, u32[]{:S(2)}) collective-permute-start(bf16[400,2048]{1,0:T(8,128)(2,1)} %collective-permute-done.26.refs_1_), channel_id=1, source_target_pairs={{0,2},{1,3},{2,0},{3,1},{4,6},{5,7},{6,4},{7,5},{8,10},{9,11},{10,... | collective-permute-start | bytes 4915208 | tf_op jit(solution)/shard_map/ppermute | solution.py:342
  359.7 43.3 %collective-permute-start.33 = (bf16[400,2048]{1,0:T(8,128)(2,1)}, bf16[400,2048]{1,0:T(8,128)(2,1)}, u32[]{:S(2)}, u32[]{:S(2)}) collective-permute-start(bf16[400,2048]{1,0:T(8,128)(2,1)} %collective-permute-done.26.refs_1_), channel_id=1, source_target_pairs={{0,1},{1,0},{2,3},{3,2},{4,5},{5,4},{6,7},{7,6},{8,9},{9,8},{10,11... | collective-permute-start | bytes 4915208 | tf_op jit(solution)/shard_map/ppermute | solution.py:342
  445.9 44.3 %collective-permute-start.42 = (bf16[2,208,2048]{2,1,0:T(8,128)(2,1)}, bf16[2,208,2048]{2,1,0:T(8,128)(2,1)S(1)}, u32[]{:S(2)}, u32[]{:S(2)}) collective-permute-start(bf16[2,208,2048]{2,1,0:T(8,128)(2,1)} %get-tuple-element.378), channel_id=1, source_target_pairs={{0,1},{1,0},{2,3},{3,2},{4,5},{5,4},{6,7},{7,6},{8,9},{9,8},{10,11... | collective-permute-start | bytes 5111816 | tf_op jit(solution)/shard_map/ppermute | solution.py:342
  446.4 43.7 %collective-permute-start.40 = (bf16[400,2048]{1,0:T(8,128)(2,1)}, bf16[400,2048]{1,0:T(8,128)(2,1)}, u32[]{:S(2)}, u32[]{:S(2)}) collective-permute-start(bf16[400,2048]{1,0:T(8,128)(2,1)} %copy-done.87), channel_id=1, source_target_pairs={{0,2},{1,3},{2,0},{3,1},{4,6},{5,7},{6,4},{7,5},{8,10},{9,11},{10,... | collective-permute-start | bytes 4915208 | tf_op jit(solution)/shard_map/ppermute | solution.py:342
  491.5 44.3 %collective-permute-start.47 = (bf16[2,208,2048]{2,1,0:T(8,128)(2,1)}, bf16[2,208,2048]{2,1,0:T(8,128)(2,1)S(1)}, u32[]{:S(2)}, u32[]{:S(2)}) collective-permute-start(bf16[2,208,2048]{2,1,0:T(8,128)(2,1)} %get-tuple-element.394), channel_id=1, source_target_pairs={{0,1},{1,0},{2,3},{3,2},{4,5},{5,4},{6,7},{7,6},{8,9},{9,8},{10,11... | collective-permute-start | bytes 5111816 | tf_op jit(solution)/shard_map/ppermute | solution.py:342
  491.9 44.0 %collective-permute-start.48 = (bf16[2,192,2048]{2,1,0:T(8,128)(2,1)}, bf16[2,192,2048]{2,1,0:T(8,128)(2,1)}, u32[]{:S(2)}, u32[]{:S(2)}) collective-permute-start(bf16[2,192,2048]{2,1,0:T(8,128)(2,1)} %get-tuple-element.395), channel_id=1, source_target_pairs={{0,1},{1,0},{2,3},{3,2},{4,5},{5,4},{6,7},{7,6},{8,9},{9,8},{10,11... | collective-permute-start | bytes 4718600 | tf_op jit(solution)/shard_map/ppermute | solution.py:342
  589.1 48.0 %collective-permute-start.63 = (bf16[1024,1024]{1,0:T(8,128)(2,1)}, bf16[1024,1024]{1,0:T(8,128)(2,1)}, u32[]{:S(2)}, u32[]{:S(2)}) collective-permute-start(bf16[1024,1024]{1,0:T(8,128)(2,1)} %get-tuple-element.479), channel_id=1, source_target_pairs={{0,4},{1,5},{2,6},{3,7},{4,0},{5,1},{6,2},{7,3},{8,12},{9,13},{10,... | collective-permute-start | bytes 6291464 | tf_op jit(solution)/shard_map/ppermute | solution.py:342
  653.6 45.1 %collective-permute-start.67 = (bf16[1024,2048]{1,0:T(8,128)(2,1)S(1)}, bf16[1024,2048]{1,0:T(8,128)(2,1)}, u32[]{:S(2)}, u32[]{:S(2)}) collective-permute-start(bf16[1024,2048]{1,0:T(8,128)(2,1)S(1)} %shard_map.272), channel_id=1, source_target_pairs={{0,1},{1,0},{2,3},{3,2},{4,5},{5,4},{6,7},{7,6},{8,9},{9,8},{10,11... | collective-permute-start | bytes 12582920 | tf_op jit(solution)/shard_map/ppermute | solution.py:342
  653.8 53.8 %collective-permute-start.64 = (bf16[576,2048]{1,0:T(8,128)(2,1)}, bf16[576,2048]{1,0:T(8,128)(2,1)}, u32[]{:S(2)}, u32[]{:S(2)}) collective-permute-start(bf16[576,2048]{1,0:T(8,128)(2,1)} %pad_maximum_fusion.7), channel_id=1, source_target_pairs={{0,2},{1,3},{2,0},{3,1},{4,6},{5,7},{6,4},{7,5},{8,10},{9,11},{10,... | collective-permute-start | bytes 7077896 | tf_op jit(solution)/shard_map/ppermute | solution.py:342
  654.9 49.6 %collective-permute-start.65 = (bf16[1024,1024]{1,0:T(8,128)(2,1)}, bf16[1024,1024]{1,0:T(8,128)(2,1)}, u32[]{:S(2)}, u32[]{:S(2)}) collective-permute-start(bf16[1024,1024]{1,0:T(8,128)(2,1)} %get-tuple-element.491), channel_id=1, source_target_pairs={{0,4},{1,5},{2,6},{3,7},{4,0},{5,1},{6,2},{7,3},{8,12},{9,13},{10,... | collective-permute-start | bytes 6291464 | tf_op jit(solution)/shard_map/ppermute | solution.py:342
  656.1 48.4 %collective-permute-start.68 = (bf16[512,1024]{1,0:T(8,128)(2,1)}, bf16[512,1024]{1,0:T(8,128)(2,1)}, u32[]{:S(2)}, u32[]{:S(2)}) collective-permute-start(bf16[512,1024]{1,0:T(8,128)(2,1)} %get-tuple-element.505), channel_id=1, source_target_pairs={{0,0},{16,1},{2,2},{18,3},{4,4},{20,5},{6,6},{22,7},{1,8},{17,9},{... | collective-permute-start | bytes 3145736 | tf_op jit(solution)/shard_map/ppermute | solution.py:464
  712.6 52.6 %collective-permute-start.70 = (bf16[512,2048]{1,0:T(8,128)(2,1)}, bf16[512,2048]{1,0:T(8,128)(2,1)}, u32[]{:S(2)}, u32[]{:S(2)}) collective-permute-start(bf16[512,2048]{1,0:T(8,128)(2,1)} %get-tuple-element.513), channel_id=1, source_target_pairs={{0,4},{1,5},{2,6},{3,7},{4,0},{5,1},{6,2},{7,3},{8,12},{9,13},{10,... | collective-permute-start | bytes 6291464 | tf_op jit(solution)/shard_map/ppermute | solution.py:342
  714.0 51.3 %collective-permute-start.71 = (bf16[512,2048]{1,0:T(8,128)(2,1)}, bf16[512,2048]{1,0:T(8,128)(2,1)}, u32[]{:S(2)}, u32[]{:S(2)}) collective-permute-start(bf16[512,2048]{1,0:T(8,128)(2,1)} %get-tuple-element.514), channel_id=1, source_target_pairs={{0,2},{1,3},{2,0},{3,1},{4,6},{5,7},{6,4},{7,5},{8,10},{9,11},{10,... | collective-permute-start | bytes 6291464 | tf_op jit(solution)/shard_map/ppermute | solution.py:342
  714.9 50.3 %collective-permute-start.73 = (bf16[512,1024]{1,0:T(8,128)(2,1)}, bf16[512,1024]{1,0:T(8,128)(2,1)}, u32[]{:S(2)}, u32[]{:S(2)}) collective-permute-start(bf16[512,1024]{1,0:T(8,128)(2,1)} %get-tuple-element.526), channel_id=1, source_target_pairs={{0,0},{16,1},{2,2},{18,3},{4,4},{20,5},{6,6},{22,7},{1,8},{17,9},{... | collective-permute-start | bytes 3145736 | tf_op jit(solution)/shard_map/ppermute | solution.py:464
  771.8 48.1 %collective-permute-start.75 = (bf16[512,2048]{1,0:T(8,128)(2,1)S(1)}, bf16[512,2048]{1,0:T(8,128)(2,1)S(1)}, u32[]{:S(2)}, u32[]{:S(2)}) collective-permute-start(bf16[512,2048]{1,0:T(8,128)(2,1)S(1)} %copy-done.27), channel_id=1, source_target_pairs={{0,4},{1,5},{2,6},{3,7},{4,0},{5,1},{6,2},{7,3},{8,12},{9,13},{10,... | collective-permute-start | bytes 6291464 | tf_op jit(solution)/shard_map/ppermute | solution.py:342
  773.2 47.4 %collective-permute-start.76 = (bf16[512,2048]{1,0:T(8,128)(2,1)S(1)}, bf16[512,2048]{1,0:T(8,128)(2,1)S(1)}, u32[]{:S(2)}, u32[]{:S(2)}) collective-permute-start(bf16[512,2048]{1,0:T(8,128)(2,1)S(1)} %copy-done.113), channel_id=1, source_target_pairs={{0,2},{1,3},{2,0},{3,1},{4,6},{5,7},{6,4},{7,5},{8,10},{9,11},{10,... | collective-permute-start | bytes 6291464 | tf_op jit(solution)/shard_map/ppermute | solution.py:342
  832.5 49.1 %collective-permute-start.84 = (bf16[512,2048]{1,0:T(8,128)(2,1)}, bf16[512,2048]{1,0:T(8,128)(2,1)}, u32[]{:S(2)}, u32[]{:S(2)}) collective-permute-start(bf16[512,2048]{1,0:T(8,128)(2,1)} %get-tuple-element.551), channel_id=1, source_target_pairs={{0,2},{1,3},{2,0},{3,1},{4,6},{5,7},{6,4},{7,5},{8,10},{9,11},{10,... | collective-permute-start | bytes 6291464 | tf_op jit(solution)/shard_map/ppermute | solution.py:342
  832.7 48.9 %collective-permute-start.82 = (bf16[256,2048]{1,0:T(8,128)(2,1)}, bf16[256,2048]{1,0:T(8,128)(2,1)}, u32[]{:S(2)}, u32[]{:S(2)}) collective-permute-start(bf16[256,2048]{1,0:T(8,128)(2,1)} %add_convert_fusion.9), channel_id=1, source_target_pairs={{0,4},{1,5},{2,6},{3,7},{4,0},{5,1},{6,2},{7,3},{8,12},{9,13},{10,... | collective-permute-start | bytes 3145736 | tf_op jit(solution)/shard_map/ppermute | solution.py:342
  834.4 47.2 %collective-permute-start.83 = (bf16[256,2048]{1,0:T(8,128)(2,1)}, bf16[256,2048]{1,0:T(8,128)(2,1)}, u32[]{:S(2)}, u32[]{:S(2)}) collective-permute-start(bf16[256,2048]{1,0:T(8,128)(2,1)} %get-tuple-element.550), channel_id=1, source_target_pairs={{0,4},{1,5},{2,6},{3,7},{4,0},{5,1},{6,2},{7,3},{8,12},{9,13},{10,... | collective-permute-start | bytes 3145736 | tf_op jit(solution)/shard_map/ppermute | solution.py:342
  (185 other events, 2573.0 us)

commit v4 on v3

--- a/solution.py
+++ b/solution.py
@@ -684,7 +684,7 @@
     width = in_refs[0].shape[1]
     inner = hid_ref.shape[1]
     name_rows = in_refs[0].shape[0] - 2 * tokens
-    tile = 256
+    tile = 512
     deep, flat = width // 4, inner // 4
 
     def dot(left, right, dims):
@@ -827,8 +827,8 @@
             pltpu.VMEM((rows, width), low),
             pltpu.VMEM((rows, inner), wide),
             pltpu.VMEM((rows, inner), wide),
-            pltpu.VMEM((rows, 256), low),
-            pltpu.VMEM((rows, 256), low),
+            pltpu.VMEM((rows, 512), low),
+            pltpu.VMEM((rows, 512), low),
         ],
         compiler_params=pltpu.CompilerParams(vmem_limit_bytes=58 * 1024 * 1024),
         cost_estimate=SMALL,

time: 981 us -> 971 us (0.990)
  Pallas kernels: 249 us -> 230 us
    pallas_call x4, Pallas kernels: 151 us -> 132 us  [expert_chunk(): pl.pallas_call(functools.partial(expert_kernel, experts, count, tokens),...]
  transfers between devices with their start and end apart: 95 -> 95, of which waited for: 37 -> 40; matrix products, arithmetic and copies ran while one was open for 14% -> 15% of each run, Pallas kernels for 25% -> 24%
where the time goes in v4:
time: 971 us; the launch traced here: 959 us
  waiting for transfers between devices  401 us (41%)
  Pallas kernels  230 us (24%)
  other arithmetic  117 us (12%)
  starting transfers between devices  104 us (11%)
  local copies, waits for them, and re-layouts  58.2 us (6%)
  matrix products  46.7 us (5%)
    ppermute x21, waiting for transfers between devices, turn(): lax.ppermute(value, 'dp', [(i, (i + step) % count) for i in range(count)])  173 us
    pallas_call x4, Pallas kernels, expert_chunk(): pl.pallas_call(functools.partial(expert_kernel, experts, count, tokens),...  132 us
    ppermute x62, waiting for transfers between devices, flip(): return lax.ppermute(value, 'expert', [(i, i ^ bit) for i in range(count)])  126 us
    ppermute x6, waiting for transfers between devices, to_owner(): lax.ppermute(p, ('dp', 'expert'), pairs)  79.8 us
    convert_element_type x29, other arithmetic, add(): return (left.astype(wide) + right.astype(wide)).astype(low)  56.2 us
    pallas_call x5, Pallas kernels, contract(): pl.pallas_call(functools.partial(contract_kernel, len(lefts)), grid=(widt...  47.4 us
    ppermute x62, starting transfers between devices, flip(): return lax.ppermute(value, 'expert', [(i, i ^ bit) for i in range(count)])  39 us
    unnamed x253, local copies, waits for them, and re-layouts  30.6 us
  transfers between devices with their start and end apart: 95, of which 40 were waited for; matrix products, arithmetic and copies ran while one was open for 15% of the time, Pallas kernels for 24%

profile of v4, /device:TPU:0, one launch (start us, length us, event | category | flops | bytes accessed | tf_op | source)
XLA Modules:
  0.0 958.9 jit_solution(10260923990750999369)
XLA Ops:
  8.9 14.3 %collective-permute-done = bf16[64,4224]{1,0:T(8,128)(2,1)S(1)} collective-permute-done((bf16[64,4224]{1,0:T(8,128)(2,1)S(1)}, bf16[64,4224]{1,0:T(8,128)(2,1)S(1)}, u32[]{:S(2)}, u32[]{:S(2)}) %collective-permute-start) | collective-permute-done | bytes 540704 | tf_op jit(solution)/shard_map/ppermute | solution.py:347
  23.2 15.2 %collective-permute-done.1 = bf16[64,4224]{1,0:T(8,128)(2,1)S(1)} collective-permute-done((bf16[64,4224]{1,0:T(8,128)(2,1)S(1)}, bf16[64,4224]{1,0:T(8,128)(2,1)S(1)}, u32[]{:S(2)}, u32[]{:S(2)}) %collective-permute-start.1) | collective-permute-done | bytes 540704 | tf_op jit(solution)/shard_map/ppermute | solution.py:347
  42.7 10.0 %collective-permute-done.2 = bf16[64,4224]{1,0:T(8,128)(2,1)S(1)} collective-permute-done((bf16[64,4224]{1,0:T(8,128)(2,1)S(1)}, bf16[64,4224]{1,0:T(8,128)(2,1)S(1)}, u32[]{:S(2)}, u32[]{:S(2)}) %collective-permute-start.2) | collective-permute-done | bytes 540704 | tf_op jit(solution)/shard_map/ppermute | solution.py:347
  56.7 19.0 %collective-permute-done.5 = bf16[256,2048]{1,0:T(8,128)(2,1)} collective-permute-done((bf16[256,2048]{1,0:T(8,128)(2,1)S(1)}, bf16[256,2048]{1,0:T(8,128)(2,1)}, u32[]{:S(2)}, u32[]{:S(2)}) %collective-permute-start.5) | collective-permute-done | bytes 1048608 | tf_op jit(solution)/shard_map/ppermute | solution.py:342
  85.0 19.0 %collective-permute-done.9 = bf16[128,4096]{1,0:T(8,128)(2,1)S(1)} collective-permute-done((bf16[128,4096]{1,0:T(8,128)(2,1)}, bf16[128,4096]{1,0:T(8,128)(2,1)S(1)}, u32[]{:S(2)}, u32[]{:S(2)}) %collective-permute-start.9) | collective-permute-done | bytes 1048608 | tf_op jit(solution)/shard_map/ppermute | solution.py:347
  105.0 18.7 %collective-permute-done.8 = bf16[512,2048]{1,0:T(8,128)(2,1)S(1)} collective-permute-done((bf16[512,2048]{1,0:T(8,128)(2,1)S(1)}, bf16[512,2048]{1,0:T(8,128)(2,1)S(1)}, u32[]{:S(2)}, u32[]{:S(2)}) %collective-permute-start.8) | collective-permute-done | bytes 2097184 | tf_op jit(solution)/shard_map/ppermute | solution.py:342
  138.1 43.6 %collective-permute-done.15 = bf16[256,2048]{1,0:T(8,128)(2,1)S(1)} collective-permute-done((bf16[256,2048]{1,0:T(8,128)(2,1)S(1)}, bf16[256,2048]{1,0:T(8,128)(2,1)S(1)}, u32[]{:S(2)}, u32[]{:S(2)}) %collective-permute-start.15) | collective-permute-done | bytes 1048608 | tf_op jit(solution)/shard_map/ppermute | solution.py:448
  194.2 9.5 collective-permute-start.19
  226.0 17.4 %collective-permute-done.20 = bf16[512,1024]{1,0:T(8,128)(2,1)} collective-permute-done((bf16[512,1024]{1,0:T(8,128)(2,1)}, bf16[512,1024]{1,0:T(8,128)(2,1)}, u32[]{:S(2)}, u32[]{:S(2)}) %collective-permute-start.20) | collective-permute-done | bytes 1048608 | tf_op jit(solution)/shard_map/ppermute | solution.py:448
  264.1 13.9 %shard_map.264 = (bf16[192,2048]{1,0:T(8,128)(2,1)S(1)}, bf16[192,2048]{1,0:T(8,128)(2,1)S(1)}, bf16[192,2048]{1,0:T(8,128)(2,1)S(1)}) custom-call(s32[17]{0:T(128)S(1)} %pad_add_fusion.order_ref, f32[192,2048]{1,0:T(8,128)S(1)} %copy-done.1, f32[192,2048]{1,0:T(8,128)S(1)} %convolution_add_fusion.3.raw_k, bf16[192,2048]{1,0:T(8,128)(2,1)S(1)} %fusion.12.v_ref, ...), custom_call_target="tpu_custom_call" | custom-call | flops 1 | bytes 1 | tf_op jit(solution)/shard_map/pallas_call | solution.py:664
  287.1 18.8 %collective-permute-done.25 = bf16[512,1024]{1,0:T(8,128)(2,1)S(1)} collective-permute-done((bf16[512,1024]{1,0:T(8,128)(2,1)}, bf16[512,1024]{1,0:T(8,128)(2,1)S(1)}, u32[]{:S(2)}, u32[]{:S(2)}) %collective-permute-start.25) | collective-permute-done | bytes 1048608 | tf_op jit(solution)/shard_map/ppermute | solution.py:448
  310.7 38.4 %collective-permute-done.26.refs_1_ = bf16[400,2048]{1,0:T(8,128)(2,1)} collective-permute-done((bf16[400,2048]{1,0:T(8,128)(2,1)S(1)}, bf16[400,2048]{1,0:T(8,128)(2,1)}, u32[]{:S(2)}, u32[]{:S(2)}) %collective-permute-start.26) | collective-permute-done | bytes 1638432 | tf_op jit(solution)/shard_map/ppermute | solution.py:347
  365.3 32.9 %shard_map.265 = (bf16[512,2048]{1,0:T(8,128)(2,1)}, bf16[512,1024]{1,0:T(8,128)(2,1)}, bf16[512,2048]{1,0:T(8,128)(2,1)}, bf16[512,1024]{1,0:T(8,128)(2,1)}, bf...) custom-call(s32[5]{0:T(128)} %stack.50.refs_0_, ...), custom_call_target="tpu_custom_call" | custom-call | flops 1 | bytes 1 | tf_op jit(solution)/shard_map/pallas_call | solution.py:819
  403.0 33.0 %shard_map.266 = (bf16[512,2048]{1,0:T(8,128)(2,1)}, bf16[512,1024]{1,0:T(8,128)(2,1)}, bf16[512,2048]{1,0:T(8,128)(2,1)}, bf16[512,1024]{1,0:T(8,128)(2,1)}, bf...) custom-call(s32[5]{0:T(128)} %stack.50.refs_0_, ...), custom_call_target="tpu_custom_call" | custom-call | flops 1 | bytes 1 | tf_op jit(solution)/shard_map/pallas_call | solution.py:819
  446.8 33.1 %shard_map.267 = (bf16[512,2048]{1,0:T(8,128)(2,1)}, bf16[512,1024]{1,0:T(8,128)(2,1)}, bf16[512,2048]{1,0:T(8,128)(2,1)}, bf16[512,1024]{1,0:T(8,128)(2,1)}, bf...) custom-call(s32[5]{0:T(128)} %stack.50.refs_0_, ...), custom_call_target="tpu_custom_call" | custom-call | flops 1 | bytes 1 | tf_op jit(solution)/shard_map/pallas_call | solution.py:819
  487.9 33.3 %shard_map.268 = (bf16[512,2048]{1,0:T(8,128)(2,1)}, bf16[512,1024]{1,0:T(8,128)(2,1)}, bf16[512,2048]{1,0:T(8,128)(2,1)}, bf16[512,1024]{1,0:T(8,128)(2,1)}, bf...) custom-call(s32[5]{0:T(128)} %stack.50.refs_0_, ...), custom_call_target="tpu_custom_call" | custom-call | flops 1 | bytes 1 | tf_op jit(solution)/shard_map/pallas_call | solution.py:819
  529.1 12.8 %shard_map.269 = bf16[2048,1024]{1,0:T(8,128)(2,1)} custom-call(bf16[512,2048]{1,0:T(8,128)(2,1)} %get-tuple-element.454.refs_0_, bf16[512,2048]{1,0:T(8,128)(2,1)} %get-tuple-element.455.refs_1_, bf16[512,2048]{1,0:T(8,128)(2,1)} %get-tuple-element.456.refs_2_, bf16[512,2048]{1,0:T(8,128)(2,1)} %get-tuple-element.457.refs_3_, ...), custom_call_target="tpu_custom_call" | custom-call | flops 1 | bytes 1 | tf_op jit(solution)/shard_map/pallas_call | solution.py:493
  558.6 12.2 %shard_map.270 = bf16[2048,1024]{1,0:T(8,128)(2,1)} custom-call(bf16[512,2048]{1,0:T(8,128)(2,1)} %get-tuple-element.454.refs_0_, bf16[512,2048]{1,0:T(8,128)(2,1)} %get-tuple-element.455.refs_1_, bf16[512,2048]{1,0:T(8,128)(2,1)} %get-tuple-element.456.refs_2_, bf16[512,2048]{1,0:T(8,128)(2,1)} %get-tuple-element.457.refs_3_, ...), custom_call_target="tpu_custom_call" | custom-call | flops 1 | bytes 1 | tf_op jit(solution)/shard_map/pallas_call | solution.py:493
  589.8 14.2 %shard_map.271 = bf16[1024,2048]{1,0:T(8,128)(2,1)} custom-call(bf16[512,1024]{1,0:T(8,128)(2,1)S(1)} %copy-done.10, bf16[512,1024]{1,0:T(8,128)(2,1)S(1)} %copy-done.11, bf16[512,1024]{1,0:T(8,128)(2,1)S(1)} %copy-done.13, bf16[512,1024]{1,0:T(8,128)(2,1)S(1)} %copy-done.16, bf16[512,2048]{1,0:T(8,128)(2,1)} %get-tuple-element.474.refs_4_, ...), custom_call_target="tpu_custom_call" | custom-call | flops 1 | bytes 1 | tf_op jit(solution)/shard_map/pallas_call | solution.py:493
  608.2 12.3 %collective-permute-done.60 = bf16[192,2048]{1,0:T(8,128)(2,1)} collective-permute-done((bf16[192,2048]{1,0:T(8,128)(2,1)}, bf16[192,2048]{1,0:T(8,128)(2,1)}, u32[]{:S(2)}, u32[]{:S(2)}) %collective-permute-start.60) | collective-permute-done | bytes 786464 | tf_op jit(solution)/shard_map/ppermute | solution.py:347
  642.0 9.5 collective-permute-start.68
  660.5 15.2 %shard_map.274 = (bf16[192,6144]{1,0:T(8,128)(2,1)S(1)}, f32[1,2048]{1,0:T(1,128)S(1)}, f32[1,2048]{1,0:T(1,128)S(1)}) custom-call(s32[17]{0:T(128)S(1)} %pad_add_fusion.order_ref, bf16[192,2048]{1,0:T(8,128)(2,1)S(1)} %pad_maximum_fusion.16.grad_ref, bf16[192,2048]{1,0:T(8,128)(2,1)S(1)} %copy-done.23, bf16[192,2048]{1,0:T(8,128)(2,1)S(1)} %copy-done.25, ...), custom_call_target="tpu_custom_call" | custom-call | flops 1 | bytes 1 | tf_op jit(solution)/shard_map/pallas_call | solution.py:664
  700.8 9.5 collective-permute-start.73
  710.3 6.8 collective-permute-done.72.got_ref
  730.0 12.7 %shard_map.278 = (bf16[512,2048]{1,0:T(8,128)(2,1)S(1)}, bf16[512,2048]{1,0:T(8,128)(2,1)S(1)}, bf16[512,2048]{1,0:T(8,128)(2,1)}, bf16[512,2048]{1,0:T(8,128)(2...) custom-call(bf16[192,1024]{1,0:T(8,128)(2,1)S(1)} %get-tuple-element.708.left_ref, bf16[192,6144]{1,0:T(8,128)(2,1)} %copy-done, ...), custom_call_target="tpu_custom_call" | custom-call | flops 1 | bytes 1 | tf_op jit(solution)/shard_map/pallas_call | solution.py:537
  766.9 21.9 %collective-permute-done.79 = bf16[256,2048]{1,0:T(8,128)(2,1)S(1)} collective-permute-done((bf16[256,2048]{1,0:T(8,128)(2,1)S(1)}, bf16[256,2048]{1,0:T(8,128)(2,1)S(1)}, u32[]{:S(2)}, u32[]{:S(2)}) %collective-permute-start.79) | collective-permute-done | bytes 1048608 | tf_op jit(solution)/shard_map/ppermute | solution.py:464
  788.7 17.1 %collective-permute-done.75 = bf16[512,2048]{1,0:T(8,128)(2,1)S(1)} collective-permute-done((bf16[512,2048]{1,0:T(8,128)(2,1)S(1)}, bf16[512,2048]{1,0:T(8,128)(2,1)S(1)}, u32[]{:S(2)}, u32[]{:S(2)}) %collective-permute-start.75) | collective-permute-done | bytes 2097184 | tf_op jit(solution)/shard_map/ppermute | solution.py:342
  820.6 17.6 %collective-permute-done.80 = bf16[192,2048]{1,0:T(8,128)(2,1)S(1)} collective-permute-done((bf16[192,2048]{1,0:T(8,128)(2,1)S(1)}, bf16[192,2048]{1,0:T(8,128)(2,1)S(1)}, u32[]{:S(2)}, u32[]{:S(2)}) %collective-permute-start.80) | collective-permute-done | bytes 786464 | tf_op jit(solution)/shard_map/ppermute | solution.py:347
  844.0 23.4 %collective-permute-done.85 = f32[24,512]{1,0:T(8,128)S(1)} collective-permute-done((f32[24,512]{1,0:T(8,128)S(1)}, f32[24,512]{1,0:T(8,128)S(1)}, u32[]{:S(2)}, u32[]{:S(2)}) %collective-permute-start.85) | collective-permute-done | bytes 49184 | tf_op jit(solution)/shard_map/ppermute | solution.py:342
  895.0 9.9 %collective-permute-done.88 = f32[24,256]{1,0:T(8,128)S(1)} collective-permute-done((f32[24,256]{1,0:T(8,128)S(1)}, f32[24,256]{1,0:T(8,128)S(1)}, u32[]{:S(2)}, u32[]{:S(2)}) %collective-permute-start.88) | collective-permute-done | bytes 24608 | tf_op jit(solution)/shard_map/ppermute | solution.py:342
  915.1 18.0 %collective-permute-done.91 = bf16[64,4096]{1,0:T(8,128)(2,1)S(1)} collective-permute-done((bf16[64,4096]{1,0:T(8,128)(2,1)S(1)}, bf16[64,4096]{1,0:T(8,128)(2,1)S(1)}, u32[]{:S(2)}, u32[]{:S(2)}) %collective-permute-start.91) | collective-permute-done | bytes 524320 | tf_op jit(solution)/shard_map/ppermute | solution.py:347
  949.1 7.0 collective-permute-done.94
  (592 shorter events, 365.9 us)
Async XLA Ops:
  80.5 43.2 %collective-permute-start.8 = (bf16[512,2048]{1,0:T(8,128)(2,1)S(1)}, bf16[512,2048]{1,0:T(8,128)(2,1)S(1)}, u32[]{:S(2)}, u32[]{:S(2)}) collective-permute-start(bf16[512,2048]{1,0:T(8,128)(2,1)S(1)} %pad_maximum_fusion.9), channel_id=1, source_target_pairs={{0,2},{1,3},{2,0},{3,1},{4,6},{5,7},{6,4},{7,5},{8,10},{9,11},{10,... | collective-permute-start | bytes 6291464 | tf_op jit(solution)/shard_map/ppermute | solution.py:342
  81.7 49.6 %collective-permute-start.7 = (bf16[512,2176]{1,0:T(8,128)(2,1)S(1)}, bf16[512,2176]{1,0:T(8,128)(2,1)S(1)}, u32[]{:S(2)}, u32[]{:S(2)}) collective-permute-start(bf16[512,2176]{1,0:T(8,128)(2,1)S(1)} %pad_maximum_fusion.8), channel_id=1, source_target_pairs={{0,4},{1,5},{2,6},{3,7},{4,0},{5,1},{6,2},{7,3},{8,12},{9,13},{10,... | collective-permute-start | bytes 6684680 | tf_op jit(solution)/shard_map/ppermute | solution.py:342
  131.7 54.1 %collective-permute-start.12 = (bf16[1024,2176]{1,0:T(8,128)(2,1)S(1)}, bf16[1024,2176]{1,0:T(8,128)(2,1)S(1)}, u32[]{:S(2)}, u32[]{:S(2)}) collective-permute-start(bf16[1024,2176]{1,0:T(8,128)(2,1)S(1)} %pad_maximum_fusion), channel_id=1, source_target_pairs={{0,1},{1,0},{2,3},{3,2},{4,5},{5,4},{6,7},{7,6},{8,9},{9,8},{10,11... | collective-permute-start | bytes 13369352 | tf_op jit(solution)/shard_map/ppermute | solution.py:342
  131.8 54.0 %collective-permute-start.13 = (bf16[1024,2048]{1,0:T(8,128)(2,1)S(1)}, bf16[1024,2048]{1,0:T(8,128)(2,1)S(1)}, u32[]{:S(2)}, u32[]{:S(2)}) collective-permute-start(bf16[1024,2048]{1,0:T(8,128)(2,1)S(1)} %pad_maximum_fusion.1), channel_id=1, source_target_pairs={{0,1},{1,0},{2,3},{3,2},{4,5},{5,4},{6,7},{7,6},{8,9},{9,8},{10,11... | collective-permute-start | bytes 12582920 | tf_op jit(solution)/shard_map/ppermute | solution.py:342
  132.2 51.0 %collective-permute-start.11 = (bf16[512,2048]{1,0:T(8,128)(2,1)S(1)}, bf16[512,2048]{1,0:T(8,128)(2,1)S(1)}, u32[]{:S(2)}, u32[]{:S(2)}) collective-permute-start(bf16[512,2048]{1,0:T(8,128)(2,1)S(1)} %get-tuple-element.305), channel_id=1, source_target_pairs={{0,2},{1,3},{2,0},{3,1},{4,6},{5,7},{6,4},{7,5},{8,10},{9,11},{10,... | collective-permute-start | bytes 6291464 | tf_op jit(solution)/shard_map/ppermute | solution.py:342
  133.5 48.2 %collective-permute-start.15 = (bf16[256,2048]{1,0:T(8,128)(2,1)S(1)}, bf16[256,2048]{1,0:T(8,128)(2,1)S(1)}, u32[]{:S(2)}, u32[]{:S(2)}) collective-permute-start(bf16[256,2048]{1,0:T(8,128)(2,1)S(1)} %get-tuple-element.310), channel_id=1, source_target_pairs={{0,8},{1,24},{2,10},{3,26},{4,12},{5,28},{6,14},{7,30},{8,9},{9,25... | collective-permute-start | bytes 3145736 | tf_op jit(solution)/shard_map/ppermute | solution.py:448
  192.0 51.4 %collective-permute-start.17 = (bf16[512,2048]{1,0:T(8,128)(2,1)}, bf16[512,2048]{1,0:T(8,128)(2,1)}, u32[]{:S(2)}, u32[]{:S(2)}) collective-permute-start(bf16[512,2048]{1,0:T(8,128)(2,1)} %get-tuple-element.311), channel_id=1, source_target_pairs={{0,2},{1,3},{2,0},{3,1},{4,6},{5,7},{6,4},{7,5},{8,10},{9,11},{10,... | collective-permute-start | bytes 6291464 | tf_op jit(solution)/shard_map/ppermute | solution.py:342
  193.3 50.1 %collective-permute-start.18 = (bf16[512,2048]{1,0:T(8,128)(2,1)}, bf16[512,2048]{1,0:T(8,128)(2,1)}, u32[]{:S(2)}, u32[]{:S(2)}) collective-permute-start(bf16[512,2048]{1,0:T(8,128)(2,1)} %pad_maximum_fusion.10), channel_id=1, source_target_pairs={{0,4},{1,5},{2,6},{3,7},{4,0},{5,1},{6,2},{7,3},{8,12},{9,13},{10,... | collective-permute-start | bytes 6291464 | tf_op jit(solution)/shard_map/ppermute | solution.py:342
  255.8 50.1 %collective-permute-start.22 = (bf16[1024,1024]{1,0:T(8,128)(2,1)}, bf16[1024,1024]{1,0:T(8,128)(2,1)S(1)}, u32[]{:S(2)}, u32[]{:S(2)}) collective-permute-start(bf16[1024,1024]{1,0:T(8,128)(2,1)} %pad_maximum_fusion.11), channel_id=1, source_target_pairs={{0,4},{1,5},{2,6},{3,7},{4,0},{5,1},{6,2},{7,3},{8,12},{9,13},{10,... | collective-permute-start | bytes 6291464 | tf_op jit(solution)/shard_map/ppermute | solution.py:342
  257.0 48.9 %collective-permute-start.23 = (bf16[512,2048]{1,0:T(8,128)(2,1)}, bf16[512,2048]{1,0:T(8,128)(2,1)S(1)}, u32[]{:S(2)}, u32[]{:S(2)}) collective-permute-start(bf16[512,2048]{1,0:T(8,128)(2,1)} %get-tuple-element.341), channel_id=1, source_target_pairs={{0,1},{1,0},{2,3},{3,2},{4,5},{5,4},{6,7},{7,6},{8,9},{9,8},{10,11... | collective-permute-start | bytes 6291464 | tf_op jit(solution)/shard_map/ppermute | solution.py:342
  259.7 46.3 %collective-permute-start.25 = (bf16[512,1024]{1,0:T(8,128)(2,1)}, bf16[512,1024]{1,0:T(8,128)(2,1)S(1)}, u32[]{:S(2)}, u32[]{:S(2)}) collective-permute-start(bf16[512,1024]{1,0:T(8,128)(2,1)} %get-tuple-element.343), channel_id=1, source_target_pairs={{0,8},{1,24},{2,10},{3,26},{4,12},{5,28},{6,14},{7,30},{8,9},{9,25... | collective-permute-start | bytes 3145736 | tf_op jit(solution)/shard_map/ppermute | solution.py:448
  307.9 41.2 %collective-permute-start.30 = (bf16[1024,1024]{1,0:T(8,128)(2,1)S(1)}, bf16[1024,1024]{1,0:T(8,128)(2,1)}, u32[]{:S(2)}, u32[]{:S(2)}) collective-permute-start(bf16[1024,1024]{1,0:T(8,128)(2,1)S(1)} %get-tuple-element.655), channel_id=1, source_target_pairs={{0,1},{1,0},{2,3},{3,2},{4,5},{5,4},{6,7},{7,6},{8,9},{9,8},{10,11... | collective-permute-start | bytes 6291464 | tf_op jit(solution)/shard_map/ppermute | solution.py:342
  308.1 48.1 %collective-permute-start.29 = (bf16[1024,1024]{1,0:T(8,128)(2,1)S(1)}, bf16[1024,1024]{1,0:T(8,128)(2,1)S(1)}, u32[]{:S(2)}, u32[]{:S(2)}) collective-permute-start(bf16[1024,1024]{1,0:T(8,128)(2,1)S(1)} %constant_dynamic-update-slice_fusion.2), channel_id=1, source_target_pairs={{0,4},{1,5},{2,6},{3,7},{4,0},{5,1},{6,2},{7,3},{8,12},{9,13},{10,... | collective-permute-start | bytes 6291464 | tf_op jit(solution)/shard_map/ppermute | solution.py:342
  358.9 40.2 %collective-permute-start.31 = (bf16[400,2048]{1,0:T(8,128)(2,1)}, bf16[400,2048]{1,0:T(8,128)(2,1)}, u32[]{:S(2)}, u32[]{:S(2)}) collective-permute-start(bf16[400,2048]{1,0:T(8,128)(2,1)} %collective-permute-done.26.refs_1_), channel_id=1, source_target_pairs={{0,8},{8,16},{16,24},{24,0},{1,9},{9,17},{17,25},{25,1},{2,10},{10... | collective-permute-start | bytes 4915208 | tf_op jit(solution)/shard_map/ppermute | solution.py:347
  399.2 40.2 %collective-permute-start.36 = (bf16[400,2048]{1,0:T(8,128)(2,1)}, bf16[400,2048]{1,0:T(8,128)(2,1)S(1)}, u32[]{:S(2)}, u32[]{:S(2)}) collective-permute-start(bf16[400,2048]{1,0:T(8,128)(2,1)} %collective-permute-done.31.refs_1_), channel_id=1, source_target_pairs={{0,8},{8,16},{16,24},{24,0},{1,9},{9,17},{17,25},{25,1},{2,10},{10... | collective-permute-start | bytes 4915208 | tf_op jit(solution)/shard_map/ppermute | solution.py:347
  399.2 40.2 %collective-permute-start.37 = (bf16[400,2048]{1,0:T(8,128)(2,1)}, bf16[400,2048]{1,0:T(8,128)(2,1)}, u32[]{:S(2)}, u32[]{:S(2)}) collective-permute-start(bf16[400,2048]{1,0:T(8,128)(2,1)} %collective-permute-done.31.refs_1_), channel_id=1, source_target_pairs={{0,2},{1,3},{2,0},{3,1},{4,6},{5,7},{6,4},{7,5},{8,10},{9,11},{10,... | collective-permute-start | bytes 4915208 | tf_op jit(solution)/shard_map/ppermute | solution.py:342
  481.3 40.5 %collective-permute-start.47 = (bf16[2,208,2048]{2,1,0:T(8,128)(2,1)}, bf16[2,208,2048]{2,1,0:T(8,128)(2,1)S(1)}, u32[]{:S(2)}, u32[]{:S(2)}) collective-permute-start(bf16[2,208,2048]{2,1,0:T(8,128)(2,1)} %get-tuple-element.394), channel_id=1, source_target_pairs={{0,1},{1,0},{2,3},{3,2},{4,5},{5,4},{6,7},{7,6},{8,9},{9,8},{10,11... | collective-permute-start | bytes 5111816 | tf_op jit(solution)/shard_map/ppermute | solution.py:342
  481.7 40.1 %collective-permute-start.48 = (bf16[2,192,2048]{2,1,0:T(8,128)(2,1)}, bf16[2,192,2048]{2,1,0:T(8,128)(2,1)}, u32[]{:S(2)}, u32[]{:S(2)}) collective-permute-start(bf16[2,192,2048]{2,1,0:T(8,128)(2,1)} %get-tuple-element.395), channel_id=1, source_target_pairs={{0,1},{1,0},{2,3},{3,2},{4,5},{5,4},{6,7},{7,6},{8,9},{9,8},{10,11... | collective-permute-start | bytes 4718600 | tf_op jit(solution)/shard_map/ppermute | solution.py:342
  575.0 48.0 %collective-permute-start.63 = (bf16[1024,1024]{1,0:T(8,128)(2,1)}, bf16[1024,1024]{1,0:T(8,128)(2,1)}, u32[]{:S(2)}, u32[]{:S(2)}) collective-permute-start(bf16[1024,1024]{1,0:T(8,128)(2,1)} %get-tuple-element.479), channel_id=1, source_target_pairs={{0,4},{1,5},{2,6},{3,7},{4,0},{5,1},{6,2},{7,3},{8,12},{9,13},{10,... | collective-permute-start | bytes 6291464 | tf_op jit(solution)/shard_map/ppermute | solution.py:342
  639.5 45.0 %collective-permute-start.67 = (bf16[1024,2048]{1,0:T(8,128)(2,1)S(1)}, bf16[1024,2048]{1,0:T(8,128)(2,1)}, u32[]{:S(2)}, u32[]{:S(2)}) collective-permute-start(bf16[1024,2048]{1,0:T(8,128)(2,1)S(1)} %shard_map.272), channel_id=1, source_target_pairs={{0,1},{1,0},{2,3},{3,2},{4,5},{5,4},{6,7},{7,6},{8,9},{9,8},{10,11... | collective-permute-start | bytes 12582920 | tf_op jit(solution)/shard_map/ppermute | solution.py:342
  639.7 53.8 %collective-permute-start.64 = (bf16[576,2048]{1,0:T(8,128)(2,1)}, bf16[576,2048]{1,0:T(8,128)(2,1)}, u32[]{:S(2)}, u32[]{:S(2)}) collective-permute-start(bf16[576,2048]{1,0:T(8,128)(2,1)} %pad_maximum_fusion.7), channel_id=1, source_target_pairs={{0,2},{1,3},{2,0},{3,1},{4,6},{5,7},{6,4},{7,5},{8,10},{9,11},{10,... | collective-permute-start | bytes 7077896 | tf_op jit(solution)/shard_map/ppermute | solution.py:342
  640.8 49.6 %collective-permute-start.65 = (bf16[1024,1024]{1,0:T(8,128)(2,1)}, bf16[1024,1024]{1,0:T(8,128)(2,1)}, u32[]{:S(2)}, u32[]{:S(2)}) collective-permute-start(bf16[1024,1024]{1,0:T(8,128)(2,1)} %get-tuple-element.491), channel_id=1, source_target_pairs={{0,4},{1,5},{2,6},{3,7},{4,0},{5,1},{6,2},{7,3},{8,12},{9,13},{10,... | collective-permute-start | bytes 6291464 | tf_op jit(solution)/shard_map/ppermute | solution.py:342
  642.0 48.4 %collective-permute-start.68 = (bf16[512,1024]{1,0:T(8,128)(2,1)}, bf16[512,1024]{1,0:T(8,128)(2,1)}, u32[]{:S(2)}, u32[]{:S(2)}) collective-permute-start(bf16[512,1024]{1,0:T(8,128)(2,1)} %get-tuple-element.505), channel_id=1, source_target_pairs={{0,0},{16,1},{2,2},{18,3},{4,4},{20,5},{6,6},{22,7},{1,8},{17,9},{... | collective-permute-start | bytes 3145736 | tf_op jit(solution)/shard_map/ppermute | solution.py:464
  698.5 52.6 %collective-permute-start.70 = (bf16[512,2048]{1,0:T(8,128)(2,1)}, bf16[512,2048]{1,0:T(8,128)(2,1)}, u32[]{:S(2)}, u32[]{:S(2)}) collective-permute-start(bf16[512,2048]{1,0:T(8,128)(2,1)} %get-tuple-element.513), channel_id=1, source_target_pairs={{0,4},{1,5},{2,6},{3,7},{4,0},{5,1},{6,2},{7,3},{8,12},{9,13},{10,... | collective-permute-start | bytes 6291464 | tf_op jit(solution)/shard_map/ppermute | solution.py:342
  699.8 51.3 %collective-permute-start.71 = (bf16[512,2048]{1,0:T(8,128)(2,1)}, bf16[512,2048]{1,0:T(8,128)(2,1)}, u32[]{:S(2)}, u32[]{:S(2)}) collective-permute-start(bf16[512,2048]{1,0:T(8,128)(2,1)} %get-tuple-element.514), channel_id=1, source_target_pairs={{0,2},{1,3},{2,0},{3,1},{4,6},{5,7},{6,4},{7,5},{8,10},{9,11},{10,... | collective-permute-start | bytes 6291464 | tf_op jit(solution)/shard_map/ppermute | solution.py:342
  700.8 50.3 %collective-permute-start.73 = (bf16[512,1024]{1,0:T(8,128)(2,1)}, bf16[512,1024]{1,0:T(8,128)(2,1)}, u32[]{:S(2)}, u32[]{:S(2)}) collective-permute-start(bf16[512,1024]{1,0:T(8,128)(2,1)} %get-tuple-element.526), channel_id=1, source_target_pairs={{0,0},{16,1},{2,2},{18,3},{4,4},{20,5},{6,6},{22,7},{1,8},{17,9},{... | collective-permute-start | bytes 3145736 | tf_op jit(solution)/shard_map/ppermute | solution.py:464
  710.3 40.8 %collective-permute-start.74 = (bf16[512,1024]{1,0:T(8,128)(2,1)}, bf16[512,1024]{1,0:T(8,128)(2,1)}, u32[]{:S(2)}, u32[]{:S(2)}) collective-permute-start(bf16[512,1024]{1,0:T(8,128)(2,1)} %get-tuple-element.527), channel_id=1, source_target_pairs={{8,0},{24,1},{10,2},{26,3},{12,4},{28,5},{14,6},{30,7},{9,8},{25,9... | collective-permute-start | bytes 3145736 | tf_op jit(solution)/shard_map/ppermute | solution.py:464
  757.7 48.0 %collective-permute-start.75 = (bf16[512,2048]{1,0:T(8,128)(2,1)S(1)}, bf16[512,2048]{1,0:T(8,128)(2,1)S(1)}, u32[]{:S(2)}, u32[]{:S(2)}) collective-permute-start(bf16[512,2048]{1,0:T(8,128)(2,1)S(1)} %copy-done.27), channel_id=1, source_target_pairs={{0,4},{1,5},{2,6},{3,7},{4,0},{5,1},{6,2},{7,3},{8,12},{9,13},{10,... | collective-permute-start | bytes 6291464 | tf_op jit(solution)/shard_map/ppermute | solution.py:342
  759.0 47.4 %collective-permute-start.76 = (bf16[512,2048]{1,0:T(8,128)(2,1)S(1)}, bf16[512,2048]{1,0:T(8,128)(2,1)S(1)}, u32[]{:S(2)}, u32[]{:S(2)}) collective-permute-start(bf16[512,2048]{1,0:T(8,128)(2,1)S(1)} %copy-done.113), channel_id=1, source_target_pairs={{0,2},{1,3},{2,0},{3,1},{4,6},{5,7},{6,4},{7,5},{8,10},{9,11},{10,... | collective-permute-start | bytes 6291464 | tf_op jit(solution)/shard_map/ppermute | solution.py:342
  818.4 49.1 %collective-permute-start.84 = (bf16[512,2048]{1,0:T(8,128)(2,1)}, bf16[512,2048]{1,0:T(8,128)(2,1)}, u32[]{:S(2)}, u32[]{:S(2)}) collective-permute-start(bf16[512,2048]{1,0:T(8,128)(2,1)} %get-tuple-element.551), channel_id=1, source_target_pairs={{0,2},{1,3},{2,0},{3,1},{4,6},{5,7},{6,4},{7,5},{8,10},{9,11},{10,... | collective-permute-start | bytes 6291464 | tf_op jit(solution)/shard_map/ppermute | solution.py:342
  818.6 48.8 %collective-permute-start.82 = (bf16[256,2048]{1,0:T(8,128)(2,1)}, bf16[256,2048]{1,0:T(8,128)(2,1)}, u32[]{:S(2)}, u32[]{:S(2)}) collective-permute-start(bf16[256,2048]{1,0:T(8,128)(2,1)} %add_convert_fusion.9), channel_id=1, source_target_pairs={{0,4},{1,5},{2,6},{3,7},{4,0},{5,1},{6,2},{7,3},{8,12},{9,13},{10,... | collective-permute-start | bytes 3145736 | tf_op jit(solution)/shard_map/ppermute | solution.py:342
  820.3 47.2 %collective-permute-start.83 = (bf16[256,2048]{1,0:T(8,128)(2,1)}, bf16[256,2048]{1,0:T(8,128)(2,1)}, u32[]{:S(2)}, u32[]{:S(2)}) collective-permute-start(bf16[256,2048]{1,0:T(8,128)(2,1)} %get-tuple-element.550), channel_id=1, source_target_pairs={{0,4},{1,5},{2,6},{3,7},{4,0},{5,1},{6,2},{7,3},{8,12},{9,13},{10,... | collective-permute-start | bytes 3145736 | tf_op jit(solution)/shard_map/ppermute | solution.py:342
  (185 other events, 2548.4 us)
